TPU v7x, 32 devices: a whole 2x2x4 slice. The times are simulated.
32 devices in a mesh: view: 2 (over core), dp: 16 (over z, y, x).
Axes of the slice: x: 2, y: 2, z: 4, core: 2. Of those that a mesh axis runs over, the one named last changes fastest.
Arguments:
- augmented: bfloat16 [2, 64, 32, 32, 3], P('view', 'dp'), may hold values from -8 to 8
- shake_ratio: int32 [2, 64], P('view', 'dp'), may hold values from 0 to 16
- labels: int32 [64], P('dp'), may hold values from 0 to 9
- labelled: int32 [64], P('dp'), may hold values from 0 to 1
- view_order: int32 [64], replicated, may hold values from 0 to 63, each once
- stem_weight: float32 [27, 96], replicated, may hold values from -1.25 to 1.25
- conv_weight: float32 [4, 864, 96], replicated, may hold values from -0.21875 to 0.21875
- head_weight: float32 [96, 10], replicated, may hold values from -2.5 to 2.5
- norm_param: float32 [2, 4, 96], replicated, may hold values from 0.25 to 1.75
- teacher_stem: float32 [27, 96], replicated, may hold values from -1.25 to 1.25
- teacher_conv: float32 [4, 864, 96], replicated, may hold values from -0.21875 to 0.21875
- teacher_head: float32 [96, 10], replicated, may hold values from -2.5 to 2.5
- teacher_norm: float32 [2, 4, 96], replicated, may hold values from 0.25 to 1.75
- first_stem: float32 [27, 96], replicated, may hold values from -0.00021362305 to 0.00021362305
- first_conv: float32 [4, 864, 96], replicated, may hold values from -0.00021362305 to 0.00021362305
- first_head: float32 [96, 10], replicated, may hold values from -0.00021362305 to 0.00021362305
- first_norm: float32 [2, 4, 96], replicated, may hold values from -0.0017089844 to 0.0017089844
- second_stem: float32 [27, 96], replicated, may hold values from 1.1901361e-09 to 4.7605444e-09
- second_conv: float32 [4, 864, 96], replicated, may hold values from 1.1901361e-09 to 4.7605444e-09
- second_head: float32 [96, 10], replicated, may hold values from 1.1901361e-09 to 4.7605444e-09
- second_norm: float32 [2, 4, 96], replicated, may hold values from 7.616871e-08 to 3.0467484e-07
Outputs:
- grad_norm: float32 [], replicated
- cross_sum: float32 [], replicated
- labelled_count: float32 [], replicated
- consistency_sum: float32 [], replicated
- new_stem: float32 [27, 96], replicated
- stem_first: float32 [27, 96], replicated
- stem_second: float32 [27, 96], replicated
- stem_teacher: float32 [27, 96], replicated
- new_conv: float32 [4, 864, 96], replicated
- conv_first: float32 [4, 864, 96], replicated
- conv_second: float32 [4, 864, 96], replicated
- conv_teacher: float32 [4, 864, 96], replicated
- new_head: float32 [96, 10], replicated
- head_first: float32 [96, 10], replicated
- head_second: float32 [96, 10], replicated
- head_teacher: float32 [96, 10], replicated
- new_norm: float32 [2, 4, 96], replicated
- norm_first: float32 [2, 4, 96], replicated
- norm_second: float32 [2, 4, 96], replicated
- norm_teacher: float32 [2, 4, 96], replicated
- stem_copy: bfloat16 [27, 96], replicated
- conv_copy: bfloat16 [4, 864, 96], replicated
- head_copy: bfloat16 [96, 10], replicated
Inputs may be any that keep to these rules, and one draw needn't show every extreme that they name: `view_order`: each image number appears once.
All inputs are finite; a program needn't handle non-finite values.
Results may differ from a plain program's by a relative error of at most 0.00125.
The roundings to bfloat16 on the way count: a program that leaves them out, or rounds other values in their place, can miss the bound.
Values may be sent and summed in bfloat16 or wider, within the bound.
No kernel may reach another device: no remote copies, remote signals or barrier semaphores. Data moves between devices by JAX's collectives and lax.ppermute only.
A program may use at most 128 MiB of HBM per device.

v0:
```python
import functools

import jax
import jax.numpy as jnp
from jax import lax
from jax.experimental import pallas as pl
from jax.experimental.pallas import tpu as pltpu
from jax.sharding import PartitionSpec as P

CLASSES = 10
STEP = 5
EPS_NORM = 1e-05
LEARN_RATE = 0.03
BETA_FIRST = 0.5
BETA_SECOND = 0.5
WEIGHT_DECAY = 0.0001
ADAM_EPS = 1e-08
CLIP_LIMIT = 0.02
TEACHER_KEEP = 0.9
CONS_WEIGHT = 10.0

F32 = jnp.float32
BF16 = jnp.bfloat16
LANE = 128
CH = 96
SIDE = 32
CELLS = SIDE * SIDE
IMAGES = 4
QUARTERS = 4
ACROSS = SIDE // QUARTERS
TILE = IMAGES * QUARTERS
LINE = ACROSS * TILE
STEPS = 4
DEEP = SIDE // STEPS
CHUNK = DEEP * LINE
ALL = SIDE * LINE
BLOCK = 64
TAPS = 9
WIDE = TAPS * CH
BLOCKS = -(-WIDE // LANE)
GRAD_ROWS = BLOCKS * CH
SHARE = GRAD_ROWS // QUARTERS
PIECE = -(-(SHARE + 1) // 16) * 16
CODE_ROWS = 2 * PIECE + SIDE
STEM_ROWS = 80
CODE_TOP = 32000.0
FRAME = (SIDE + 2, ACROSS + 2, TILE)
PARAMS = pltpu.CompilerParams(vmem_limit_bytes=24 * 1024 * 1024)


def dot(a, b):
    return jnp.dot(a, b, preferred_element_type=F32)


def dot_rows(a, b):
    return lax.dot_general(a, b, (((0,), (0,)), ((), ())), preferred_element_type=F32)


def dot_lanes(a, b):
    return lax.dot_general(a, b, (((1,), (1,)), ((), ())), preferred_element_type=F32)


def frame_line(frame, first_line, values):
    lines = values.shape[0] // LINE
    width = values.shape[1]
    tiles = values.reshape(lines, ACROSS, TILE, width)
    row = lax.broadcasted_iota(jnp.int32, (1, TILE, 1), 1)
    before = jnp.where(row >= IMAGES, pltpu.roll(tiles[:, ACROSS - 1], IMAGES, 1), 0.0)
    after = jnp.where(row < TILE - IMAGES, pltpu.roll(tiles[:, 0], TILE - IMAGES, 1), 0.0)
    place = slice(first_line + 1, first_line + 1 + lines)
    frame[place, 1 : ACROSS + 1] = tiles.astype(BF16)
    frame[place, 0] = before.astype(BF16)
    frame[place, ACROSS + 1] = after.astype(BF16)


def clear_frame(frame):
    blank = jnp.zeros(frame.shape[1:], BF16)
    frame[0] = blank
    frame[SIDE + 1] = blank


def taps(frame, step, rows):
    parts = []
    for dy in rows:
        for kx in range(3):
            place = step * DEEP + 1 + dy
            lines = frame[place : place + DEEP, kx : kx + ACROSS]
            parts.append(lines.reshape(CHUNK, lines.shape[-1]))
    return jnp.concatenate(parts, axis=1)


def fold_lines(both, carry):
    upper = jnp.concatenate([carry, both[: CHUNK - LINE, LANE:]], axis=0)
    return both[:, :LANE] + upper, both[CHUNK - LINE :, LANE:]


def blank_line():
    return jnp.zeros((LINE, LANE), F32)


def new_lines(step):
    first = 0 if step == 0 else step * DEEP + 1
    return first, min((step + 1) * DEEP + 1, SIDE)


def chunk_rows(step):
    return slice(step * CHUNK, (step + 1) * CHUNK)


def eight(values):
    parts = values.reshape(values.shape[0] // 8, 8, values.shape[1])
    while parts.shape[0] > 1:
        middle = parts.shape[0] // 2
        rest = parts[2 * middle :]
        parts = parts[:middle] + parts[middle : 2 * middle]
        if rest.shape[0]:
            parts = jnp.concatenate([parts[:-1], parts[-1:] + rest], axis=0) if middle > 1 else parts + rest
    return parts[0]


def both_halves(sums):
    return sums + pltpu.roll(sums, IMAGES, 0)


def tap_block(raw, tap):
    return raw[:, tap * CH : (tap + 1) * CH]


def image_lines(image_ref, plain, moved):
    plain[...] = jnp.zeros(plain.shape, F32)
    for channel in range(3):
        side_by_side = jnp.concatenate([image_ref[i, channel].astype(F32) for i in range(IMAGES)], axis=1)
        plain[pl.ds(8 + channel, SIDE, stride=8), :] = side_by_side
    source = lax.broadcasted_iota(jnp.int32, (LANE, LANE), 0)
    target = lax.broadcasted_iota(jnp.int32, (LANE, LANE), 1)
    same = source // SIDE == (target & (IMAGES - 1))
    across = ((target // IMAGES) & (QUARTERS - 1)) * ACROSS + target // TILE
    for kx in range(3):
        picks = jnp.where(same & ((source & (SIDE - 1)) == across + (kx - 1)), 1.0, 0.0).astype(BF16)
        moved[kx] = dot(plain[...].astype(BF16), picks)


def image_taps(moved, first_line, lines):
    columns = []
    for line in range(lines):
        place = (first_line + line) * 8
        parts = [moved[kx, place : place + 24, :] for kx in range(3)]
        columns.append(jnp.concatenate(parts + [jnp.zeros((8, LANE), F32)], axis=0))
    return jnp.concatenate(columns, axis=1).astype(BF16)


def stem_row(tap):
    return (tap % 3) * 24 + (tap // 3) * 8


def pad_lanes(row):
    return jnp.concatenate([row, jnp.zeros((row.shape[0], LANE - row.shape[1]), row.dtype)], axis=1)


def norm_terms(sums, squares, cell_count):
    average = sums / cell_count
    inverse = lax.rsqrt(squares / cell_count - average * average + EPS_NORM)
    return average, inverse


def column_sum(values):
    return jnp.sum(values, axis=0, keepdims=True)


def slope_rest(half, tanh, product):
    return (tanh + half) - product * tanh


def first_kernel(
    image_hbm, stem_s_hbm, stem_t_hbm, raw_s, raw_t,
    first_s, first_t, frame_s, moved_ref, pooled_ref, msg_ref,
    plain, wst32, wst, wf, frame_t, image_ref, stem_s, stem_t, raw, sems,
):
    coming = [
        pltpu.make_async_copy(source, target, sems.at[k])
        for k, (source, target) in enumerate((
            (image_hbm, image_ref), (stem_s_hbm, stem_s), (stem_t_hbm, stem_t),
            (raw_s.at[0], raw.at[0]), (raw_s.at[2], raw.at[1]), (raw_t.at[0], raw.at[2]), (raw_t.at[2], raw.at[3]),
        ))
    ]
    for copy in coming:
        copy.start()
    wf[...] = jnp.zeros(wf.shape, BF16)
    wst32[...] = jnp.zeros(wst32.shape, F32)
    clear_frame(frame_s)
    clear_frame(frame_t)
    for copy in coming[:3]:
        copy.wait()
    image_lines(image_ref, plain, moved_ref)
    for n, stem in enumerate((stem_s, stem_t)):
        for tap in range(TAPS):
            row = stem_row(tap)
            wst32[row : row + 3, n * LANE : n * LANE + CH] = stem[3 * tap : 3 * tap + 3, :]
    wst[...] = wst32[...].astype(BF16)
    for copy in coming[3:]:
        copy.wait()
    for n in range(2):
        for b in range(2):
            for tap in range(TAPS):
                wf[n, tap * LANE : tap * LANE + CH, b * LANE : b * LANE + CH] = jnp.transpose(
                    tap_block(raw.at[2 * n + b], tap)
                ).astype(BF16)
    pooled = [0.0, 0.0]
    sums = [0.0] * 8
    for step in range(STEPS):
        first_line, end = new_lines(step)
        stems = dot_rows(image_taps(moved_ref, first_line, end - first_line), wst[...])
        for n, (frame, out_ref) in enumerate(((frame_s, first_s), (frame_t, first_t))):
            stem = stems[:, n * LANE : (n + 1) * LANE]
            pooled[n] += eight(stem)
            frame_line(frame, first_line, stem)
            out = dot(taps(frame, step, (-1, 0, 1)), wf[n])
            out_ref[chunk_rows(step), :] = out
            for b in range(2):
                part = out[:, b * LANE : (b + 1) * LANE]
                sums[4 * n + 2 * b] += eight(part)
                sums[4 * n + 2 * b + 1] += eight(part * part)
    for n in range(2):
        pooled_ref[n] = both_halves(pooled[n])
    spread_sums(msg_ref, sums)


def total_of(refs):
    total = refs[0][...]
    for ref in refs[1:]:
        total = total + ref[...]
    return total


def spread_sums(msg_ref, sums):
    sums = [column_sum(part) for part in sums]
    if len(sums) < 8:
        sums.append(jnp.zeros((8 - len(sums), LANE), F32))
    msg_ref[...] = jnp.concatenate(sums, axis=0)


def forward_weight_kernel(raw_ref, w_ref):
    w_ref[...] = jnp.zeros(w_ref.shape, BF16)
    for ky in range(3):
        for kx in range(3):
            row = (ky // 2) * 3 * LANE + kx * LANE
            lane = LANE if ky == 0 else 0
            w_ref[row : row + CH, lane : lane + CH] = jnp.transpose(tap_block(raw_ref, ky * 3 + kx)).astype(BF16)


def backward_weight_kernel(cw0, cw1, cw2, cw3, two_ref, one_ref):
    two_ref[...] = jnp.zeros(two_ref.shape, BF16)
    one_ref[...] = jnp.zeros(one_ref.shape, BF16)
    for ky in range(3):
        for kx in range(3):
            tap = (2 - ky) * 3 + 2 - kx
            lane = LANE if ky == 0 else 0
            for b, (inner, outer) in enumerate(((cw0, cw1), (cw2, cw3))):
                row = (ky // 2) * 3 * LANE + kx * LANE
                two_ref[b, row : row + CH, lane : lane + CH] = (0.5 * tap_block(outer, tap)).astype(BF16)
                one_ref[b, row : row + CH, lane : lane + CH] = tap_block(inner, tap).astype(BF16)


def norm_rows(sums, norm, terms, first_row, norm_index, cell_count):
    for b in range(2):
        row = first_row + 2 * b
        average, inverse = norm_terms(sums[row : row + 1], sums[row + 1 : row + 2], cell_count)
        gain = pad_lanes(norm[0, 2 * b + norm_index : 2 * b + norm_index + 1, :])
        shift = pad_lanes(norm[1, 2 * b + norm_index : 2 * b + norm_index + 1, :])
        scale = inverse * gain
        terms[8 * b : 8 * b + 1, :] = 0.5 * scale
        terms[8 * b + 1 : 8 * b + 2, :] = 0.5 * (shift - average * scale)
        terms[8 * b + 2 : 8 * b + 3, :] = inverse
        terms[8 * b + 3 : 8 * b + 4, :] = -average * inverse
        terms[8 * b + 4 : 8 * b + 5, :] = scale


def term(terms, b, k):
    return terms[8 * b + k : 8 * b + k + 1, :]


def second_kernel(
    cell_count, first_s, first_t, recv_ref, norm_s, norm_t, ws_ref, wt_ref,
    second_s, second_t, frame_s, bent_ref, msg_ref,
    frame_t, terms_s, terms_t,
):
    received = total_of(recv_ref)
    norm_rows(received, norm_s, terms_s, 0, 0, cell_count)
    norm_rows(received, norm_t, terms_t, 4, 0, cell_count)
    nets = ((first_s, terms_s, frame_s, ws_ref, second_s), (first_t, terms_t, frame_t, wt_ref, second_t))
    sums = [0.0] * 8
    carry = [blank_line()] * 4
    for _, _, frames, _, _ in nets:
        for b in range(2):
            clear_frame(frames.at[b])
    for step in range(STEPS):
        first_line, end = new_lines(step)
        for n, (source, terms, frames, w, target) in enumerate(nets):
            for b in range(2):
                k = 2 * n + b
                lanes = slice(b * LANE, (b + 1) * LANE)
                half = source[first_line * LINE : end * LINE, lanes] * term(terms, b, 0) + term(terms, b, 1)
                tanh = jnp.tanh(half)
                product = half * tanh
                frame_line(frames.at[b], first_line, half + product)
                if n == 0:
                    bent_ref[first_line * LINE : end * LINE, lanes] = slope_rest(half, tanh, product)
                out, carry[k] = fold_lines(dot(taps(frames.at[b], step, (0, 1)), w[b]), carry[k])
                target[chunk_rows(step), lanes] = out
                sums[2 * k] += eight(out)
                sums[2 * k + 1] += eight(out * out)
    spread_sums(msg_ref, sums)


def head_rows(head_ref):
    padded = jnp.concatenate([head_ref[...], jnp.zeros((LANE - CLASSES, CH), F32)], axis=0)
    return pad_lanes(padded).astype(BF16)


def alpha_of(ratio_ref, image):
    return (ratio_ref[0, image].astype(F32) + 1.0) / 18.0


def alpha_rows(ratio_ref):
    row = lax.broadcasted_iota(jnp.int32, (2 * IMAGES, LANE), 0) & (IMAGES - 1)
    alpha = jnp.zeros((2 * IMAGES, LANE), F32)
    for k in range(IMAGES):
        alpha = jnp.where(row == k, alpha_of(ratio_ref, k), alpha)
    return alpha


def class_lanes(rows):
    return lax.broadcasted_iota(jnp.int32, (rows, LANE), 1) < CLASSES


def log_softmax(logits, valid):
    top = jnp.max(jnp.where(valid, logits, -3e38), axis=1, keepdims=True)
    moved = logits - top
    total = jnp.sum(jnp.where(valid, jnp.exp(moved), 0.0), axis=1, keepdims=True)
    return moved - jnp.log(total)


def pooled_low(ratio_ref, sums, stem_sums):
    alpha = alpha_rows(ratio_ref)
    total = alpha * both_halves(sums[0]) + (1.0 - alpha) * both_halves(sums[1])
    return ((total + stem_sums) / CELLS).astype(BF16)


def teacher_kernel(
    cell_count, ratio_ref, second_ref, recv_ref, norm, head_ref, stem_sum_ref,
    prob_ref,
    terms,
):
    norm_rows(total_of(recv_ref), norm, terms, 4, 1, cell_count)
    plain, curved = [0.0] * 2, [0.0] * 2
    for block in range(ALL // BLOCK):
        for b in range(2):
            values = second_ref[block * BLOCK : (block + 1) * BLOCK, b * LANE : (b + 1) * LANE]
            half = values * term(terms, b, 0) + term(terms, b, 1)
            plain[b] += eight(values)
            curved[b] += eight(half * jnp.tanh(half))
    sums = [plain[b] * term(terms, b, 0) + (CELLS // 2) * term(terms, b, 1) + curved[b] for b in range(2)]
    low = pooled_low(ratio_ref, sums, stem_sum_ref[1])
    logits = dot_lanes(low, head_rows(head_ref))
    valid = class_lanes(2 * IMAGES)
    first_rows = lax.broadcasted_iota(jnp.int32, (2 * IMAGES, LANE), 0) < IMAGES
    prob = jnp.where(valid & first_rows, jnp.exp(log_softmax(logits, valid)), 0.0)
    prob_ref[...] = pltpu.roll(prob.astype(BF16).astype(F32), 16, 1)


def student_kernel(
    cell_count, ratio_ref, labels_ref, labelled_ref, order_ref,
    second_ref, recv_ref, norm, head_ref, stem_sum_ref, prob_ref,
    msg_ref, bent_ref,
    terms,
):
    norm_rows(total_of(recv_ref), norm, terms, 0, 1, cell_count)
    plain, curved, bent, bent_values = ([0.0] * 2 for _ in range(4))
    for block in range(ALL // BLOCK):
        for b in range(2):
            values = second_ref[block * BLOCK : (block + 1) * BLOCK, b * LANE : (b + 1) * LANE]
            half = values * term(terms, b, 0) + term(terms, b, 1)
            tanh = jnp.tanh(half)
            product = half * tanh
            slope = slope_rest(half, tanh, product)
            bent_ref[block * BLOCK : (block + 1) * BLOCK, b * LANE : (b + 1) * LANE] = slope
            plain[b] += eight(values)
            curved[b] += eight(product)
            bent[b] += eight(slope)
            bent_values[b] += eight(slope * values)
    cells = CELLS // 2
    sums = [plain[b] * term(terms, b, 0) + cells * term(terms, b, 1) + curved[b] for b in range(2)]
    slopes = [0.5 * (cells + bent[b]) for b in range(2)]
    sums += slopes
    sums += [
        term(terms, b, 2) * (0.5 * (plain[b] + bent_values[b])) + term(terms, b, 3) * slopes[b] for b in range(2)
    ]
    dp_index = lax.axis_index("dp")
    low = pooled_low(ratio_ref, sums, stem_sum_ref[0])
    logits = dot_lanes(low, head_rows(head_ref))
    rows = 2 * IMAGES
    info = jnp.where(class_lanes(rows), logits, 0.0)
    lane = lax.broadcasted_iota(jnp.int32, (rows, LANE), 1)
    row = lax.broadcasted_iota(jnp.int32, (rows, LANE), 0)
    for k in range(IMAGES):
        facts = (
            alpha_of(ratio_ref, k),
            labels_ref[k].astype(F32),
            labelled_ref[k].astype(F32),
            order_ref[dp_index * IMAGES + k].astype(F32),
        )
        for place, fact in enumerate(facts):
            info = jnp.where((row == k) & (lane == 32 + place), fact, info)
    for b in range(2):
        msg_ref[:, b * LANE : (b + 1) * LANE] = jnp.where(
            row < IMAGES, both_halves(sums[2 + b]), both_halves(sums[4 + b])
        )
    msg_ref[:, 2 * LANE :] = jnp.where(row < IMAGES, info + prob_ref[...], low.astype(F32))


def loss_part(images, all_images, cell_count, recv_refs, head_ref, rows_ref, means, small_ref):
    view = lax.axis_index("view")
    received = jnp.concatenate([ref[...] for ref in recv_refs], axis=0)
    count = received.shape[0] * 2 * images
    received = received.reshape(count, 3 * LANE)
    raw = received[:, 2 * LANE :]
    row = lax.broadcasted_iota(jnp.int32, (count, 1), 0)
    part = row & (2 * images - 1)
    once = part < images
    facts = jnp.where(once, raw, pltpu.roll(raw, images, 0))
    group, inner = row // (2 * images), received.shape[0] // (2 * images * len(recv_refs))
    offset = (group % inner) * len(recv_refs) + group // inner
    image = ((offset ^ lax.axis_index("dp")) * images + (part & (images - 1))).astype(F32)
    alpha = facts[:, 32:33]
    label = facts[:, 33:34]
    labelled = facts[:, 34:35]
    order = facts[:, 35:36]
    eye = row == lax.broadcasted_iota(jnp.int32, (count, count), 1)
    image_lane = jnp.sum(jnp.where(eye, image, 0.0), axis=0, keepdims=True)
    order_lane = jnp.sum(jnp.where(eye, order, 0.0), axis=0, keepdims=True)
    first_lane = jnp.sum(jnp.where(eye & once, 1.0, 0.0), axis=0, keepdims=True)
    is_one = jnp.where(view == 0, 1.0, 0.0)
    ours = is_one * image + (1.0 - is_one) * order
    theirs = is_one * order_lane + (1.0 - is_one) * image_lane
    match = jnp.where((ours == theirs) & (first_lane > 0.5), 1.0, 0.0).astype(BF16)
    valid = class_lanes(count)
    other = pltpu.roll(facts, LANE - 16, 1)
    target = dot(match, jnp.where(valid, other, 0.0).astype(BF16))
    log_prob = jnp.where(valid, log_softmax(jnp.where(valid, facts, 0.0), valid), 0.0)
    probs = jnp.where(valid, jnp.exp(log_prob), 0.0)
    lane = lax.broadcasted_iota(jnp.int32, (count, LANE), 1)
    onehot = jnp.where(lane.astype(F32) == label, 1.0, 0.0)
    total = jnp.sum(jnp.where(once, labelled, 0.0), axis=0, keepdims=True)
    mask = labelled * is_one
    away = probs - target
    grad_prob = CONS_WEIGHT / all_images * away
    grad = mask * (probs - onehot) / total + probs * (
        grad_prob - jnp.sum(probs * grad_prob, axis=1, keepdims=True)
    )
    grad_low = grad.astype(BF16)
    dmix = dot(grad_low, head_rows(head_ref)) / CELLS
    weights = (dmix * alpha, dmix * (1.0 - alpha))
    for b in range(2):
        product = weights[b] * received[:, b * LANE : (b + 1) * LANE]
        plain = column_sum(jnp.where(once, product, 0.0))
        normal = column_sum(jnp.where(once, 0.0, product))
        means[2 * b : 2 * b + 1, :] = plain / cell_count
        means[2 * b + 1 : 2 * b + 2, :] = normal / cell_count
        rows_ref[b] = weights[b]
        small_ref[16 + 2 * b : 16 + 2 * b + 1, :] = plain
        small_ref[16 + 2 * b + 1 : 16 + 2 * b + 2, :] = normal
    rows_ref[2] = dmix
    cross = -jnp.sum(
        jnp.where(once, mask * jnp.sum(onehot * log_prob, axis=1, keepdims=True), 0.0), axis=0, keepdims=True
    )
    consistency = jnp.sum(
        jnp.where(once, jnp.sum(away * away, axis=1, keepdims=True), 0.0), axis=0, keepdims=True
    )
    lane_row = lax.broadcasted_iota(jnp.int32, (1, LANE), 1)
    small_ref[20:21, :] = jnp.where(
        lane_row == 0, cross, jnp.where(lane_row == 1, consistency, jnp.where(lane_row == 2, total, 0.0))
    )
    small_ref[21:24, :] = jnp.zeros((3, LANE), F32)
    pooled = jnp.where(once, 0.0, raw).astype(BF16)
    small_ref[0:16, :] = dot_rows(grad_low, pooled)[0:16, :]


def pack_grad(ref, blocks):
    side_by_side = jnp.concatenate(blocks + [jnp.zeros((CH, BLOCKS * LANE - WIDE), F32)], axis=1)
    for k in range(BLOCKS):
        ref[k * CH : (k + 1) * CH, :] = side_by_side[:, k * LANE : (k + 1) * LANE]


def keep_and_send(keep_ref, send_ref, blocks):
    view = lax.axis_index("view")
    for own, ref in ((0, keep_ref), (1, send_ref)):
        @pl.when(view == own)
        def _():
            pack_grad(ref, blocks[0])

        @pl.when(view != own)
        def _():
            pack_grad(ref, blocks[1])


def back_second_kernel(
    cell_count, all_images,
    second_ref, first_ref, bent_two, bent_one, recv1_ref, recv2_ref, recv3_ref, norm, head_ref, w_ref,
    du_ref, frames, msg_ref, small_ref, dmix_ref,
    terms1, terms2, rows_ref, means,
):
    rows = 2 * IMAGES
    norm_rows(total_of(recv1_ref), norm, terms1, 0, 0, cell_count)
    norm_rows(total_of(recv2_ref), norm, terms2, 0, 1, cell_count)
    loss_part(IMAGES, all_images, cell_count, recv3_ref, head_ref, rows_ref, means, small_ref)
    dmix_ref[...] = rows_ref[2, 0:rows, :]
    scales, linears, offsets = [], [], []
    for b in range(2):
        gain = term(terms2, b, 4)
        mean, slant = means[2 * b : 2 * b + 1, :], means[2 * b + 1 : 2 * b + 2, :]
        scales.append(0.5 * gain * rows_ref[b, 0:rows, :])
        linears.append(-gain * slant * term(terms2, b, 2))
        offsets.append(scales[b] - gain * (mean + slant * term(terms2, b, 3)))
    sums = [0.0] * 4
    carry = [blank_line()] * 2
    for b in range(2):
        clear_frame(frames.at[b])
    for step in range(STEPS):
        first_line, end = new_lines(step)
        for b in range(2):
            lanes = slice(b * LANE, (b + 1) * LANE)
            values = second_ref[first_line * LINE : end * LINE, lanes]
            bent = bent_two[first_line * LINE : end * LINE, lanes]
            shape = (values.shape[0] // 8, 8, LANE)
            dy = (bent.reshape(shape) * scales[b][None] + offsets[b][None]).reshape(values.shape) + values * linears[b]
            frame_line(frames.at[b], first_line, dy)
            dh, carry[b] = fold_lines(dot(taps(frames.at[b], step, (0, 1)), w_ref[b]), carry[b])
            before = first_ref[chunk_rows(step), lanes]
            du = dh + dh * bent_one[chunk_rows(step), lanes]
            du_ref[chunk_rows(step), lanes] = du
            sums[2 * b] += eight(du)
            sums[2 * b + 1] += eight(du * before)
    for b in range(2):
        plain, product = column_sum(sums[2 * b]), column_sum(sums[2 * b + 1])
        sums[2 * b] = plain
        sums[2 * b + 1] = term(terms1, b, 2) * product + term(terms1, b, 3) * plain
    spread_sums(msg_ref, sums)


def middle_lines(frame, first_line):
    return frame[first_line + 1 : first_line + 1 + DEEP, 1 : ACROSS + 1].reshape(CHUNK, frame.shape[-1])


def second_weight_kernel(frame_ref, dy_ref, keep_ref, send_ref, gacc):
    for b in range(2):
        for step in range(STEPS):
            pair = jnp.concatenate(
                [middle_lines(dy_ref.at[b], step * DEEP), middle_lines(dy_ref.at[b], step * DEEP + 1)], axis=1
            )
            product = dot_rows(pair, taps(frame_ref.at[b], step, (0, 1)))
            gacc[b] = product if step == 0 else gacc[b] + product
    blocks = []
    for b in range(2):
        blocks.append([])
        for tap in range(TAPS):
            ky, kx = tap // 3, tap % 3
            row = LANE if ky == 0 else 0
            lane = (ky // 2) * 3 * LANE + kx * LANE
            blocks[b].append(gacc[b, row : row + CH, lane : lane + CH])
    keep_and_send(keep_ref, send_ref, blocks)


def back_weight_kernel(
    cell_count,
    du_ref, first_ref, low_ref, recv1_ref, recv5_ref, norm, small_ref,
    frame_ref, keep_ref, send_ref,
    terms1, gacc,
):
    norm_rows(total_of(recv1_ref), norm, terms1, 0, 0, cell_count)
    sums = total_of(recv5_ref)
    for ref in (keep_ref, send_ref):
        ref[GRAD_ROWS : GRAD_ROWS + 24, :] = small_ref[...]
        ref[GRAD_ROWS + 24 :, :] = sums
    means = sums / cell_count
    for b in range(2):
        clear_frame(frame_ref.at[b])
    for step in range(STEPS):
        parts = []
        for b in range(2):
            lanes = slice(b * LANE, (b + 1) * LANE)
            normal = first_ref[chunk_rows(step), lanes] * term(terms1, b, 2) + term(terms1, b, 3)
            parts.append(term(terms1, b, 4) * (
                du_ref[chunk_rows(step), lanes] - means[2 * b : 2 * b + 1, :] - normal * means[2 * b + 1 : 2 * b + 2, :]
            ))
        pair = jnp.concatenate(parts, axis=1)
        for b in range(2):
            frame_line(frame_ref.at[b], step * DEEP, parts[b])
        product = dot_rows(pair.astype(BF16), taps(low_ref, step, (-1, 0, 1)))
        gacc[...] = product if step == 0 else gacc[...] + product
    keep_and_send(
        keep_ref, send_ref,
        [[gacc[b * LANE : b * LANE + CH, tap * LANE : tap * LANE + CH] for tap in range(TAPS)] for b in range(2)],
    )


def back_stem_kernel(frame_ref, moved_ref, dmix_ref, w_ref, stem_ref):
    carry = blank_line()
    total = 0.0
    products = []
    for step in range(STEPS):
        if step % 2 == 0:
            products = [[dot(taps(frame_ref.at[b], step + k, (0, 1)), w_ref[b]) for k in range(2)] for b in range(2)]
        both = products[0][step % 2] + products[1][step % 2]
        dstem, carry = fold_lines(both, carry)
        dstem = (dstem.reshape(CHUNK // 8, 8, LANE) + dmix_ref[...][None]).reshape(CHUNK, LANE)
        total += dot(image_taps(moved_ref, step * DEEP, DEEP), dstem.astype(BF16))
    rows = [total[stem_row(tap) : stem_row(tap) + 3, :] for tap in range(TAPS)]
    stem_ref[...] = jnp.concatenate(rows, axis=0)


def code(values):
    top = jnp.max(jnp.abs(values), axis=0, keepdims=True)
    power = jnp.clip(jnp.ceil(jnp.log2(jnp.maximum(top, 1e-30)) + 0.01), -100.0, 100.0)
    counted = jnp.round(values * (jnp.exp2(-power) * CODE_TOP))
    return counted, power


def unit(power):
    return jnp.exp2(power) * (1.0 / CODE_TOP)


def coded_rows(values, rows):
    counted, power = code(values)
    parts = [counted, power]
    if rows - values.shape[0] - 1:
        parts.append(jnp.zeros((rows - values.shape[0] - 1, LANE), F32))
    return jnp.concatenate(parts, axis=0).astype(jnp.int32).astype(jnp.int16)


def decoded(values, count):
    whole_part = values.astype(jnp.int32).astype(F32)
    return whole_part[:count] * unit(whole_part[count : count + 1])


def encode_kernel(keep2, recv2, keep1, recv1, *refs):
    outs, total = refs[:-1], refs[-1]
    for k, (keep, recv) in enumerate(((keep1, recv1), (keep2, recv2))):
        total[k] = keep[0:GRAD_ROWS, :] + recv[0:GRAD_ROWS, :]
    mine = lax.axis_index("dp") & (QUARTERS - 1)
    for offset, out in enumerate(outs):
        place = pl.multiple_of((mine ^ offset) * SHARE, 8)
        for k in range(2):
            out[k * PIECE : (k + 1) * PIECE, :] = coded_rows(total[k, pl.ds(place, SHARE), :], PIECE)


def summed(refs, first, count, rows):
    total = decoded(refs[0][first : first + rows, :], count)
    for ref in refs[1:]:
        total += decoded(ref[first : first + rows, :], count)
    return total


def combine_kernel(recv_refs, stem_ref, out_ref):
    for k in range(2):
        out_ref[k * PIECE : (k + 1) * PIECE, :] = coded_rows(summed(recv_refs, k * PIECE, SHARE, PIECE), PIECE)
    out_ref[2 * PIECE :, :] = coded_rows(stem_ref[...], SIDE)


def recode_kernel(recv_refs, out_ref):
    for k in range(2):
        out_ref[k * PIECE : (k + 1) * PIECE, :] = coded_rows(summed(recv_refs, k * PIECE, SHARE, PIECE), PIECE)
    out_ref[2 * PIECE :, :] = coded_rows(summed(recv_refs, 2 * PIECE, 27, SIDE), SIDE)


def stack_kernel(inner, parts, out_ref):
    count = parts[0].shape[0]
    for k, part in enumerate(parts):
        if inner:
            for entry in range(count):
                out_ref[entry * len(parts) + k] = part[entry]
        else:
            out_ref[k * count : (k + 1) * count] = part[...]


def adam_terms(gradient, factor, weight, first, second, teacher):
    clipped = gradient * factor
    first_new = BETA_FIRST * first + (1.0 - BETA_FIRST) * clipped
    second_new = BETA_SECOND * second + (1.0 - BETA_SECOND) * (clipped * clipped)
    second_hat = second_new * (1.0 / (1.0 - BETA_SECOND**STEP))
    weight_new = weight * (1.0 - LEARN_RATE * WEIGHT_DECAY) - (
        first_new * (LEARN_RATE / (1.0 - BETA_FIRST**STEP)) / (jnp.sqrt(second_hat) + ADAM_EPS)
    )
    return weight_new, first_new, second_new, TEACHER_KEEP * teacher + (1.0 - TEACHER_KEEP) * weight_new


def update_kernel(
    own_codes, other_codes, own_facts, other_facts,
    cw, cf, cs, ct, sw, sf, ss, st, hw, hf, hs, ht, nw, nf, ns, nt,
    cw_o, cf_o, cs_o, ct_o, cb_o, sw_o, sf_o, ss_o, st_o, sb_o, hw_o, hf_o, hs_o, ht_o, hb_o,
    nw_o, nf_o, ns_o, nt_o, norm_o, cross_o, count_o, consistency_o,
    factor_ref, own_ref, other_ref,
):
    conv = pl.program_id(0)
    view = lax.axis_index("view")

    @pl.when(conv == 0)
    def _():
        facts = own_facts[...] + other_facts[...]
        small, sums = facts[:24], facts[24:]
        mine = lax.axis_index("dp") & (QUARTERS - 1)
        stem = jnp.zeros((27, LANE), F32)
        for codes, ref in ((own_codes, own_ref), (other_codes, other_ref)):
            for offset, source in enumerate(codes):
                place = pl.multiple_of((mine ^ offset) * SHARE, 8)
                for k in range(2):
                    ref[k, pl.ds(place, SHARE), :] = decoded(source[k * PIECE : (k + 1) * PIECE, :], SHARE)
            stem += summed(codes, 2 * PIECE, 27, SIDE)
        stem = stem[:, :CH]
        head = small[:CLASSES, :CH]
        gains = jnp.concatenate([sums[1:2], small[17:18], sums[3:4], small[19:20]], axis=0)[:, :CH]
        shifts = jnp.concatenate([sums[0:1], small[16:17], sums[2:3], small[18:19]], axis=0)[:, :CH]
        total = jnp.zeros((1, 1), F32)
        for part in (stem, head, gains, shifts):
            total += jnp.sum(jnp.sum(part * part, axis=1, keepdims=True), axis=0, keepdims=True)
        for ref in (own_ref, other_ref):
            for k in range(2):
                values = ref[k, 0:GRAD_ROWS, :]
                column = jnp.sum(values * values, axis=0, keepdims=True)
                total += jnp.sum(column, axis=1, keepdims=True)
        norm = jnp.sqrt(total)
        factor = CLIP_LIMIT / jnp.maximum(norm, CLIP_LIMIT)
        factor_ref[...] = jnp.broadcast_to(factor, factor_ref.shape)
        norm_o[...] = norm
        cross_o[...] = small[20:21, 0:1]
        consistency_o[...] = small[20:21, 1:2]
        count_o[...] = own_facts[20:21, 2:3]
        sw_o[...], sf_o[...], ss_o[...], st_o[...] = adam_terms(stem, factor, sw[...], sf[...], ss[...], st[...])
        sb_o[...] = sw_o[...].astype(BF16)
        hw_o[...], hf_o[...], hs_o[...], ht_o[...] = adam_terms(head, factor, hw[...], hf[...], hs[...], ht[...])
        hb_o[...] = hw_o[...].astype(BF16)
        for k, part in enumerate((gains, shifts)):
            nw_o[k], nf_o[k], ns_o[k], nt_o[k] = adam_terms(part, factor, nw[k], nf[k], ns[k], nt[k])

    def update(ref, second):
        factor = factor_ref[0:1, 0:1]
        for k in range(BLOCKS):
            lanes = slice(k * LANE, min((k + 1) * LANE, WIDE))
            gradient = ref[second, k * CH : (k + 1) * CH, 0 : lanes.stop - lanes.start]
            weight, first, second_moment, teacher = adam_terms(
                gradient, factor, cw[:, lanes], cf[:, lanes], cs[:, lanes], ct[:, lanes]
            )
            cw_o[:, lanes] = weight
            cf_o[:, lanes] = first
            cs_o[:, lanes] = second_moment
            ct_o[:, lanes] = teacher
            cb_o[:, lanes] = weight.astype(BF16)

    mine = conv // 2 == view

    @pl.when(mine)
    def _():
        update(own_ref, conv & 1)

    @pl.when(jnp.logical_not(mine))
    def _():
        update(other_ref, conv & 1)


def whole(shape):
    return pl.BlockSpec(shape, lambda i: (0,) * len(shape))


def scalars():
    return pl.BlockSpec(memory_space=pltpu.SMEM)


def conv_part(k):
    return pl.BlockSpec((None, CH, WIDE), lambda i: (k, 0, 0))


def held():
    return pl.BlockSpec(memory_space=pltpu.VMEM)


def hold(values):
    return pltpu.with_memory_space_constraint(values, pltpu.VMEM)


def struct(shape, kind=F32):
    return jax.ShapeDtypeStruct(shape, kind)


def from_partners(values, shift, ways):
    size = lax.axis_size("dp")
    return [values] + [
        lax.ppermute(values, "dp", [(i, i ^ (offset << shift)) for i in range(size)]) for offset in range(1, ways)
    ]


def stages():
    size = lax.axis_size("dp")
    groups = []
    shift = 0
    while (1 << shift) < size:
        ways = min(4, size >> shift)
        groups.append((shift, ways))
        shift += 2
    return groups


def sum_parts(values, beside=None):
    groups = stages()
    for shift, ways in groups[:-1]:
        parts = from_partners(values, shift, ways)
        if beside is not None:
            parts, beside = lax.optimization_barrier((parts, beside))
        values = sum(parts)
    return tuple(from_partners(values, *groups[-1])), beside


def stack(parts, inner):
    shape = (len(parts) * parts[0].shape[0],) + parts[0].shape[1:]
    return pl.pallas_call(
        functools.partial(stack_kernel, inner), out_shape=struct(shape, parts[0].dtype), compiler_params=PARAMS, name="stack"
    )(tuple(parts))


def gather_parts(values, groups):
    inner = groups[0][0] > 0
    for shift, ways in groups[:-1]:
        values = stack(from_partners(values, shift, ways), inner)
    return tuple(from_partners(values, *groups[-1]))


def swap_view(values):
    return lax.ppermute(values, "view", [(0, 1), (1, 0)])


def forward_weights(conv):
    shape = (2, 6 * LANE, 2 * LANE)
    return pl.pallas_call(
        forward_weight_kernel,
        grid=(2,),
        in_specs=[pl.BlockSpec((None, CH, WIDE), lambda i: (2 * i + 1, 0, 0))],
        out_specs=pl.BlockSpec((None,) + shape[1:], lambda i: (i, 0, 0)),
        out_shape=struct(shape, BF16),
        compiler_params=PARAMS,
        cost_estimate=pl.CostEstimate(flops=2_000_000_000, bytes_accessed=4_000_000, transcendentals=0),
        name="forward_weight",
    )(conv)


def backward_weights(conv):
    return pl.pallas_call(
        backward_weight_kernel,
        grid=(1,),
        in_specs=[conv_part(k) for k in range(4)],
        out_specs=[whole((2, 6 * LANE, 2 * LANE))] * 2,
        out_shape=[struct((2, 6 * LANE, 2 * LANE), BF16)] * 2,
        compiler_params=PARAMS,
        cost_estimate=pl.CostEstimate(flops=4_000_000_000, bytes_accessed=8_000_000, transcendentals=0),
        name="backward_weight",
    )(conv, conv, conv, conv)


def shards(
    augmented, shake_ratio, labels, labelled, view_order,
    stem_weight, conv_weight, head_weight, norm_param,
    teacher_stem, teacher_conv, teacher_head, teacher_norm,
    first_stem, first_conv, first_head, first_norm,
    second_stem, second_conv, second_head, second_norm,
):
    dp = lax.axis_size("dp")
    all_images = IMAGES * dp
    cell_count = float(all_images * CELLS)
    rows = dp * 2 * IMAGES
    conv, conv_t, conv_f, conv_s = (
        jnp.transpose(v, (0, 2, 1)) for v in (conv_weight, teacher_conv, first_conv, second_conv)
    )
    head, head_t, head_f, head_s = (v.T for v in (head_weight, teacher_head, first_head, second_head))
    pixels = jnp.transpose(augmented[0], (0, 3, 1, 2))
    msg = struct((8, LANE))
    groups = stages()
    last_ways = groups[-1][1]
    recv_spec = (held(),) * last_ways
    norm_spec = whole((2, 4, CH))
    head_spec = whole((CLASSES, CH))
    moved_shape = (3, (SIDE + 4) * 8, LANE)
    frame_one, frame_two = FRAME + (LANE,), (2,) + FRAME + (LANE,)
    values_shape, grad_shape = (ALL, 2 * LANE), struct((GRAD_ROWS, LANE))
    terms_scratch = pltpu.VMEM((16, LANE), F32)

    first_s, first_t, low, moved, stem_sums, message = pl.pallas_call(
        first_kernel,
        in_specs=[pl.BlockSpec(memory_space=pltpu.HBM)] * 5,
        out_specs=[held()] * 6,
        out_shape=[
            pltpu.VMEM(values_shape, F32), pltpu.VMEM(values_shape, F32), pltpu.VMEM(frame_one, BF16),
            pltpu.VMEM(moved_shape, F32), struct((2, 8, LANE)), msg,
        ],
        scratch_shapes=[
            pltpu.VMEM(moved_shape[1:], F32), pltpu.VMEM((STEM_ROWS, 2 * LANE), F32),
            pltpu.VMEM((STEM_ROWS, 2 * LANE), BF16), pltpu.VMEM((2, 9 * LANE, 2 * LANE), BF16),
            pltpu.VMEM(frame_one, BF16), pltpu.VMEM((IMAGES, 3, SIDE, SIDE), BF16), pltpu.VMEM((27, CH), F32),
            pltpu.VMEM((27, CH), F32), pltpu.VMEM((4, CH, WIDE), F32), pltpu.SemaphoreType.DMA((7,)),
        ],
        compiler_params=PARAMS,
        name="first_conv",
    )(*(pltpu.with_memory_space_constraint(v, pltpu.HBM) for v in (pixels, stem_weight, teacher_stem, conv, conv_t)))
    first_s, first_t, low, moved = (hold(v) for v in (first_s, first_t, low, moved))
    recv1, (weight_s, weight_t) = sum_parts(message, (forward_weights(conv), forward_weights(conv_t)))

    second_s, second_t, hidden, bent_one, message = pl.pallas_call(
        functools.partial(second_kernel, cell_count),
        in_specs=[held()] * 2 + [recv_spec] + [held()] * 4,
        out_specs=[held()] * 5,
        out_shape=[pltpu.VMEM(values_shape, F32)] * 2 + [pltpu.VMEM(frame_two, BF16), pltpu.VMEM(values_shape, F32), msg],
        scratch_shapes=[pltpu.VMEM(frame_two, BF16), terms_scratch, terms_scratch],
        compiler_params=PARAMS,
        name="second_conv",
    )(first_s, first_t, recv1, norm_param, teacher_norm, weight_s, weight_t)
    second_s, second_t, hidden, bent_one = (hold(v) for v in (second_s, second_t, hidden, bent_one))
    recv2, _ = sum_parts(message)

    prob = pl.pallas_call(
        functools.partial(teacher_kernel, cell_count),
        in_specs=[scalars(), held(), recv_spec] + [held()] * 3,
        out_specs=held(),
        out_shape=struct((8, LANE)),
        scratch_shapes=[terms_scratch],
        compiler_params=PARAMS,
        name="teacher_logits",
    )(shake_ratio, second_t, recv2, teacher_norm, head_t, stem_sums)
    prob, conv_later = lax.optimization_barrier((prob, conv))
    other = swap_view(prob)
    back_weight_two, back_weight_one = backward_weights(conv_later)
    other, back_weight_two = lax.optimization_barrier((other, back_weight_two))
    facts, bent_two = pl.pallas_call(
        functools.partial(student_kernel, cell_count),
        in_specs=[scalars()] * 4 + [held(), recv_spec] + [held()] * 4,
        out_specs=[held()] * 2,
        out_shape=[struct((8, 3 * LANE)), pltpu.VMEM(values_shape, F32)],
        scratch_shapes=[terms_scratch],
        compiler_params=PARAMS,
        cost_estimate=pl.CostEstimate(flops=4_000_000_000, bytes_accessed=8_000_000, transcendentals=0),
        name="student_logits",
    )(shake_ratio, labels, labelled, view_order, second_s, recv2, norm_param, head, stem_sums, other)
    bent_two = hold(bent_two)
    recv3 = gather_parts(facts.reshape(1, 8, 3 * LANE), groups[::-1])

    du, dy, message, small, dmix = pl.pallas_call(
        functools.partial(back_second_kernel, cell_count, float(all_images)),
        in_specs=[held()] * 4 + [recv_spec] * 2 + [(held(),) * groups[0][1]] + [held()] * 3,
        out_specs=[held()] * 5,
        out_shape=[
            pltpu.VMEM(values_shape, F32), pltpu.VMEM(frame_two, BF16), msg, struct((24, LANE)), struct((8, LANE)),
        ],
        scratch_shapes=[
            terms_scratch, terms_scratch, pltpu.VMEM((3, rows, LANE), F32), pltpu.VMEM((8, LANE), F32),
        ],
        compiler_params=PARAMS,
        name="back_second",
    )(second_s, first_s, bent_two, bent_one, recv1, recv2, recv3, norm_param, head, back_weight_two)
    du, dy = hold(du), hold(dy)
    keep2, send2 = pl.pallas_call(
        second_weight_kernel,
        in_specs=[held()] * 2,
        out_specs=[held()] * 2,
        out_shape=[grad_shape] * 2,
        scratch_shapes=[pltpu.VMEM((2, 2 * LANE, 6 * LANE), F32)],
        compiler_params=PARAMS,
        cost_estimate=pl.CostEstimate(flops=8_000_000_000, bytes_accessed=16_000_000, transcendentals=0),
        name="second_weight",
    )(hidden, dy)
    recv5, (keep2, send2) = sum_parts(message, (keep2, send2))
    recv_grad2 = swap_view(send2)

    frame, keep1, send1 = pl.pallas_call(
        functools.partial(back_weight_kernel, cell_count),
        in_specs=[held()] * 3 + [recv_spec] * 2 + [held()] * 2,
        out_specs=[held()] * 3,
        out_shape=[pltpu.VMEM(frame_two, BF16)] + [struct((GRAD_ROWS + 32, LANE))] * 2,
        scratch_shapes=[terms_scratch, pltpu.VMEM((2 * LANE, 9 * LANE), F32)],
        compiler_params=PARAMS,
        cost_estimate=pl.CostEstimate(flops=8_000_000_000, bytes_accessed=16_000_000, transcendentals=0),
        name="back_weight",
    )(du, first_s, low, recv1, recv5, norm_param, small)
    frame = hold(frame)
    recv_grad1 = swap_view(send1)
    coded = pl.pallas_call(
        encode_kernel,
        out_shape=[struct((2 * PIECE, LANE), jnp.int16)] * QUARTERS,
        scratch_shapes=[pltpu.VMEM((2, GRAD_ROWS, LANE), F32)],
        compiler_params=PARAMS,
        name="encode",
    )(keep2, recv_grad2, keep1, recv_grad1)
    scattered = (coded[0],) + tuple(
        lax.ppermute(coded[offset], "dp", [(i, i ^ offset) for i in range(dp)]) for offset in range(1, QUARTERS)
    )

    stem_grad = pl.pallas_call(
        back_stem_kernel,
        in_specs=[held()] * 4,
        out_specs=held(),
        out_shape=struct((27, LANE)),
        compiler_params=PARAMS,
        cost_estimate=pl.CostEstimate(flops=8_000_000_000, bytes_accessed=16_000_000, transcendentals=0),
        name="back_stem",
    )(frame, moved, dmix, back_weight_one)

    stem_grad, scattered = lax.optimization_barrier((stem_grad, scattered))
    code_shape = struct((CODE_ROWS, LANE), jnp.int16)
    codes = pl.pallas_call(combine_kernel, out_shape=code_shape, compiler_params=PARAMS, name="combine")(
        scattered, stem_grad
    )
    for group in groups[1:]:
        codes = pl.pallas_call(recode_kernel, out_shape=code_shape, compiler_params=PARAMS, name="recode")(
            tuple(from_partners(codes, *group))
        )
    own = tuple(from_partners(codes, *groups[0]))
    other_grads = tuple(swap_view(part) for part in own)

    conv_block = pl.BlockSpec((None, CH, WIDE), lambda i: (i, 0, 0))
    stem_block, norm_block = whole((27, CH)), norm_spec
    code_spec = (whole((CODE_ROWS, LANE)),) * QUARTERS
    facts_spec = pl.BlockSpec((32, LANE), lambda i: (GRAD_ROWS // 32, 0))
    grads_scratch = pltpu.VMEM((2, GRAD_ROWS, LANE), F32)
    outs = pl.pallas_call(
        update_kernel,
        grid=(4,),
        in_specs=[code_spec] * 2 + [facts_spec] * 2
        + [conv_block] * 4 + [stem_block] * 4 + [head_spec] * 4 + [norm_block] * 4,
        out_specs=[conv_block] * 5 + [stem_block] * 5 + [head_spec] * 5 + [norm_block] * 4 + [whole((1, 1))] * 4,
        out_shape=[struct((4, CH, WIDE))] * 4 + [struct((4, CH, WIDE), BF16)]
        + [struct((27, CH))] * 4 + [struct((27, CH), BF16)]
        + [struct((CLASSES, CH))] * 4 + [struct((CLASSES, CH), BF16)]
        + [struct((2, 4, CH))] * 4 + [struct((1, 1))] * 4,
        scratch_shapes=[pltpu.VMEM((8, LANE), F32), grads_scratch, grads_scratch],
        compiler_params=PARAMS,
        name="update",
    )(
        own, other_grads, keep1, recv_grad1,
        conv, conv_f, conv_s, conv_t, stem_weight, first_stem, second_stem, teacher_stem,
        head, head_f, head_s, head_t, norm_param, first_norm, second_norm, teacher_norm,
    )
    convs = [jnp.transpose(v, (0, 2, 1)) for v in outs[:5]]
    stems = outs[5:10]
    heads = [v.T for v in outs[10:15]]
    norms = outs[15:19]
    return (
        *(v.reshape(()) for v in outs[19:23]),
        *stems[:4], *convs[:4], *heads[:4], *norms, stems[4], convs[4], heads[4],
    )


def solution(mesh):
    in_specs = (
        (P("view", "dp", None, None, None), P("view", "dp"), P("dp"), P("dp")) + (P(),) * 17
    )
    return jax.shard_map(shards, mesh=mesh, in_specs=in_specs, out_specs=(P(),) * 23, check_vma=False)
```

profile of v0, /device:TPU:0, one launch (start us, length us, event | category | flops | bytes accessed | tf_op | source)
XLA Modules:
  0.0 123.2 jit_solution(5796558623388527841)
XLA Ops:
  0.7 8.3 %first_conv.1 = (f32[4096,256]{1,0:T(8,128)S(1)}, f32[4096,256]{1,0:T(8,128)S(1)}, bf16[34,10,16,128]{3,2,1,0:T(8,128)(2,1)S(1)}, f32[3,288,128]{2,1,0:T(8,128)S...) custom-call(bf16[4,3,32,32]{3,2,1,0:T(8,128)(2,1)} %bitcast.49, f32[27,96]{1,0:T(8,128)} %sw.1, f32[27,96]{1,0:T(8,128)} %st.1, ...), custom_call_target="tpu_custom_call" | custom-call | tf_op jit(solution)/shard_map/first_conv/pallas_call | solution.py:893
  9.0 4.0 %collective-permute-start.2 = (f32[8,128]{1,0:T(8,128)S(1)}, f32[8,128]{1,0:T(8,128)S(1)}, u32[]{:S(2)}, u32[]{:S(2)}) collective-permute-start(f32[8,128]{1,0:T(8,128)S(1)} %get-tuple-element.99), channel_id=1, source_target_pairs={{0,3},{1,2},{2,1},{3,0},{4,7},{5,6},{6,5},{7,4},{8,11},{9,10},{10,... | collective-permute-start | bytes 12296 | tf_op jit(solution)/shard_map/ppermute | solution.py:796
  14.9 1.6 %collective-permute-done.1 = f32[8,128]{1,0:T(8,128)S(1)} collective-permute-done((f32[8,128]{1,0:T(8,128)S(1)}, f32[8,128]{1,0:T(8,128)S(1)}, u32[]{:S(2)}, u32[]{:S(2)}) %collective-permute-start.1) | collective-permute-done | bytes 4128 | tf_op jit(solution)/shard_map/ppermute | solution.py:796
  17.0 3.6 %collective-permute-start.5 = (f32[8,128]{1,0:T(8,128)S(1)}, f32[8,128]{1,0:T(8,128)S(1)}, u32[]{:S(2)}, u32[]{:S(2)}) collective-permute-start(f32[8,128]{1,0:T(8,128)S(1)} %add_add_fusion.2.recv_ref_0_.recv1_ref_0_), channel_id=1, source_target_pairs={{0,12},{1,13},{2,14},{3,15},{4,8},{5,9},{6,10},{7,11},{8,4},{9,5},... | collective-permute-start | bytes 12296 | tf_op jit(solution)/shard_map/ppermute | solution.py:796
  22.5 2.7 %collective-permute-done.4.recv_ref_2_.recv1_ref_2_ = f32[8,128]{1,0:T(8,128)S(1)} collective-permute-done((f32[8,128]{1,0:T(8,128)S(1)}, f32[8,128]{1,0:T(8,128)S(1)}, u32[]{:S(2)}, u32[]{:S(2)}) %collective-permute-start.4) | collective-permute-done | bytes 4128 | tf_op jit(solution)/shard_map/ppermute | solution.py:796
  25.2 8.2 %second_conv.1 = (f32[4096,256]{1,0:T(8,128)S(1)}, f32[4096,256]{1,0:T(8,128)S(1)}, bf16[2,34,10,16,128]{4,3,2,1,0:T(8,128)(2,1)S(1)}, f32[4096,256]{1,0:T(8,128)S(1)}, f32[8,128]{1,0:T(8,128)S(1)}) custom-call(f32[4096,256]{1,0:T(8,128)S(1)} %get-tuple-element.96.first_s.first_ref, f32[4096,256]{1,0:T(8,128)S(1)} %get-tuple-element.97.first_t, ...), custom_call_target="tpu_custom_call" | custom-call | tf_op jit(solution)/shard_map/second_conv/pallas_call | solution.py:913
  33.4 1.6 %collective-permute-start.8 = (f32[8,128]{1,0:T(8,128)S(1)}, f32[8,128]{1,0:T(8,128)S(1)}, u32[]{:S(2)}, u32[]{:S(2)}) collective-permute-start(f32[8,128]{1,0:T(8,128)S(1)} %get-tuple-element.106), channel_id=1, source_target_pairs={{0,3},{1,2},{2,1},{3,0},{4,7},{5,6},{6,5},{7,4},{8,11},{9,10},{10,... | collective-permute-start | bytes 12296 | tf_op jit(solution)/shard_map/ppermute | solution.py:796
  35.5 1.5 %collective-permute-start.6 = (f32[8,128]{1,0:T(8,128)S(1)}, f32[8,128]{1,0:T(8,128)S(1)}, u32[]{:S(2)}, u32[]{:S(2)}) collective-permute-start(f32[8,128]{1,0:T(8,128)S(1)} %get-tuple-element.106), channel_id=1, source_target_pairs={{0,1},{1,0},{2,3},{3,2},{4,5},{5,4},{6,7},{7,6},{8,9},{9,8},{10,11... | collective-permute-start | bytes 12296 | tf_op jit(solution)/shard_map/ppermute | solution.py:796
  39.1 1.4 %collective-permute-start.11 = (f32[8,128]{1,0:T(8,128)S(1)}, f32[8,128]{1,0:T(8,128)S(1)}, u32[]{:S(2)}, u32[]{:S(2)}) collective-permute-start(f32[8,128]{1,0:T(8,128)S(1)} %add_add_fusion.1.recv_ref_0_.recv2_ref_0_), channel_id=1, source_target_pairs={{0,12},{1,13},{2,14},{3,15},{4,8},{5,9},{6,10},{7,11},{8,4},{9,5},... | collective-permute-start | bytes 12296 | tf_op jit(solution)/shard_map/ppermute | solution.py:796
  41.2 2.3 %collective-permute-start.9 = (f32[8,128]{1,0:T(8,128)S(1)}, f32[8,128]{1,0:T(8,128)S(1)}, u32[]{:S(2)}, u32[]{:S(2)}) collective-permute-start(f32[8,128]{1,0:T(8,128)S(1)} %add_add_fusion.1.recv_ref_0_.recv2_ref_0_), channel_id=1, source_target_pairs={{0,4},{1,5},{2,6},{3,7},{4,0},{5,1},{6,2},{7,3},{8,12},{9,13},{10,... | collective-permute-start | bytes 12296 | tf_op jit(solution)/shard_map/ppermute | solution.py:796
  45.1 1.7 %teacher_logits.1 = f32[8,128]{1,0:T(8,128)S(1)} custom-call(s32[1,4]{1,0:T(1,128)S(1)} %copy-done.16, f32[4096,256]{1,0:T(8,128)S(1)} %get-tuple-element.108.second_ref, f32[8,128]{1,0:T(8,128)S(1)} %add_add_fusion.1.recv_ref_0_.recv2_ref_0_, f32[8,128]{1,0:T(8,128)S(1)} %collective-permute-done.9.recv_ref_1_.recv2_ref_1_, ...), custom_call_target="tpu_custom_call" | custom-call | tf_op jit(solution)/shard_map/teacher_logits/pallas_call | solution.py:925
  48.1 2.4 %student_logits.1 = (f32[8,384]{1,0:T(8,128)S(1)}, f32[4096,256]{1,0:T(8,128)S(1)}) custom-call(s32[1,4]{1,0:T(1,128)S(1)} %copy-done.16, s32[4]{0:T(128)S(1)} %copy-done.19, s32[4]{0:T(128)S(1)} %copy-done.20, s32[64]{0:T(128)S(1)} %copy-done.21, f32[4096,256]{1,0:T(8,128)S(1)} %get-tuple-element.105.second_ref, ...), custom_call_target="tpu_custom_call" | custom-call | flops 4000000000 | bytes 8000000 | tf_op jit(solution)/shard_map/student_logits/pallas_call | solution.py:938
  50.5 2.6 %collective-permute-start.15 = (f32[1,8,384]{2,1,0:T(8,128)S(1)}, f32[1,8,384]{2,1,0:T(8,128)S(1)}, u32[]{:S(2)}, u32[]{:S(2)}) collective-permute-start(f32[1,8,384]{2,1,0:T(8,128)S(1)} %bitcast.43), channel_id=1, source_target_pairs={{0,12},{1,13},{2,14},{3,15},{4,8},{5,9},{6,10},{7,11},{8,4},{9,5},... | collective-permute-start | bytes 36872 | tf_op jit(solution)/shard_map/ppermute | solution.py:796
  56.2 1.5 %collective-permute-done.14.parts_2_ = f32[1,8,384]{2,1,0:T(8,128)S(1)} collective-permute-done((f32[1,8,384]{2,1,0:T(8,128)S(1)}, f32[1,8,384]{2,1,0:T(8,128)S(1)}, u32[]{:S(2)}, u32[]{:S(2)}) %collective-permute-start.14) | collective-permute-done | bytes 12320 | tf_op jit(solution)/shard_map/ppermute | solution.py:796
  57.9 2.4 %collective-permute-start.18 = (f32[4,8,384]{2,1,0:T(8,128)S(1)}, f32[4,8,384]{2,1,0:T(8,128)S(1)}, u32[]{:S(2)}, u32[]{:S(2)}) collective-permute-start(f32[4,8,384]{2,1,0:T(8,128)S(1)} %stack.1.recv3_ref_0_), channel_id=1, source_target_pairs={{0,3},{1,2},{2,1},{3,0},{4,7},{5,6},{6,5},{7,4},{8,11},{9,10},{10,... | collective-permute-start | bytes 147464 | tf_op jit(solution)/shard_map/ppermute | solution.py:796
  61.4 1.9 %collective-permute-done.18.recv3_ref_3_ = f32[4,8,384]{2,1,0:T(8,128)S(1)} collective-permute-done((f32[4,8,384]{2,1,0:T(8,128)S(1)}, f32[4,8,384]{2,1,0:T(8,128)S(1)}, u32[]{:S(2)}, u32[]{:S(2)}) %collective-permute-start.18) | collective-permute-done | bytes 49184 | tf_op jit(solution)/shard_map/ppermute | solution.py:796
  64.9 4.8 %back_second.1 = (f32[4096,256]{1,0:T(8,128)S(1)}, bf16[2,34,10,16,128]{4,3,2,1,0:T(8,128)(2,1)S(1)}, f32[8,128]{1,0:T(8,128)S(1)}, f32[24,128]{1,0:T(8,128)S(1)}, f32[8,128]{1,0:T(8,128)S(1)}) custom-call(f32[4096,256]{1,0:T(8,128)S(1)} %get-tuple-element.105.second_ref, f32[4096,256]{1,0:T(8,128)S(1)} %get-tuple-element.96.first_s.first_ref, ...), custom_call_target="tpu_custom_call" | custom-call | tf_op jit(solution)/shard_map/back_second/pallas_call | solution.py:951
  69.7 1.6 %collective-permute-start.21 = (f32[8,128]{1,0:T(8,128)S(1)}, f32[8,128]{1,0:T(8,128)S(1)}, u32[]{:S(2)}, u32[]{:S(2)}) collective-permute-start(f32[8,128]{1,0:T(8,128)S(1)} %get-tuple-element.124), channel_id=1, source_target_pairs={{0,3},{1,2},{2,1},{3,0},{4,7},{5,6},{6,5},{7,4},{8,11},{9,10},{10,... | collective-permute-start | bytes 12296 | tf_op jit(solution)/shard_map/ppermute | solution.py:796
  71.8 1.5 %collective-permute-start.19 = (f32[8,128]{1,0:T(8,128)S(1)}, f32[8,128]{1,0:T(8,128)S(1)}, u32[]{:S(2)}, u32[]{:S(2)}) collective-permute-start(f32[8,128]{1,0:T(8,128)S(1)} %get-tuple-element.124), channel_id=1, source_target_pairs={{0,1},{1,0},{2,3},{3,2},{4,5},{5,4},{6,7},{7,6},{8,9},{9,8},{10,11... | collective-permute-start | bytes 12296 | tf_op jit(solution)/shard_map/ppermute | solution.py:796
  73.3 3.8 %second_weight.1 = (f32[672,128]{1,0:T(8,128)S(1)}, f32[672,128]{1,0:T(8,128)S(1)}) custom-call(bf16[2,34,10,16,128]{4,3,2,1,0:T(8,128)(2,1)S(1)} %get-tuple-element.120.frame_ref, bf16[2,34,10,16,128]{4,3,2,1,0:T(8,128)(2,1)S(1)} %get-tuple-element.121.dy_ref), custom_call_target="tpu_custom_call" | custom-call | flops 8000000000 | bytes 16000000 | tf_op jit(solution)/shard_map/second_weight/pallas_call | solution.py:965
  79.5 2.1 %collective-permute-start.22 = (f32[8,128]{1,0:T(8,128)S(1)}, f32[8,128]{1,0:T(8,128)S(1)}, u32[]{:S(2)}, u32[]{:S(2)}) collective-permute-start(f32[8,128]{1,0:T(8,128)S(1)} %add_add_fusion.recv5_ref_0_), channel_id=1, source_target_pairs={{0,4},{1,5},{2,6},{3,7},{4,0},{5,1},{6,2},{7,3},{8,12},{9,13},{10,... | collective-permute-start | bytes 12296 | tf_op jit(solution)/shard_map/ppermute | solution.py:796
  83.2 3.6 %back_weight.1 = (bf16[2,34,10,16,128]{4,3,2,1,0:T(8,128)(2,1)S(1)}, f32[704,128]{1,0:T(8,128)S(1)}, f32[704,128]{1,0:T(8,128)S(1)}) custom-call(f32[4096,256]{1,0:T(8,128)S(1)} %get-tuple-element.117.du_ref, f32[4096,256]{1,0:T(8,128)S(1)} %get-tuple-element.96.first_s.first_ref, bf16[34,10,16,128]{3,2,1,0:T(8,128)(2,1)S(1)} %copy-done.18, ...), custom_call_target="tpu_custom_call" | custom-call | flops 8000000000 | bytes 16000000 | tf_op jit(solution)/shard_map/back_weight/pallas_call | solution.py:978
  87.4 1.7 %collective-permute-done.25.recv2 = f32[672,128]{1,0:T(8,128)S(1)} collective-permute-done((f32[672,128]{1,0:T(8,128)S(1)}, f32[672,128]{1,0:T(8,128)S(1)}, u32[]{:S(2)}, u32[]{:S(2)}) %collective-permute-start.25) | collective-permute-done | bytes 344096 | tf_op jit(solution)/shard_map/ppermute | solution.py:836
  89.9 1.5 %collective-permute-start.28 = (s16[352,128]{1,0:T(8,128)(2,1)S(1)}, s16[352,128]{1,0:T(8,128)(2,1)S(1)}, u32[]{:S(2)}, u32[]{:S(2)}) collective-permute-start(s16[352,128]{1,0:T(8,128)(2,1)S(1)} %get-tuple-element.139), channel_id=1, source_target_pairs={{0,2},{1,3},{2,0},{3,1},{4,6},{5,7},{6,4},{7,5},{8,10},{9,11},{10,... | collective-permute-start | bytes 270344 | tf_op jit(solution)/shard_map/ppermute | solution.py:998
  92.9 4.8 %back_stem.1.stem_ref = f32[27,128]{1,0:T(8,128)S(1)} custom-call(bf16[2,34,10,16,128]{4,3,2,1,0:T(8,128)(2,1)S(1)} %get-tuple-element.129.frame_ref, f32[3,288,128]{2,1,0:T(8,128)S(1)} %get-tuple-element.130.moved_ref, f32[8,128]{1,0:T(8,128)S(1)} %get-tuple-element.131.dmix_ref, bf16[2,768,256]{2,1,0:T(8,128)(2,1)S(1)} %get-tuple-element.132.w_ref), custom_call_target="tpu_custom_call" | custom-call | flops 8000000000 | bytes 16000000 | tf_op jit(solution)/shard_map/back_stem/pallas_call | solution.py:1001
  97.9 2.5 %collective-permute-start.32 = (s16[384,128]{1,0:T(8,128)(2,1)S(1)}, s16[384,128]{1,0:T(8,128)(2,1)S(1)}, u32[]{:S(2)}, u32[]{:S(2)}) collective-permute-start(s16[384,128]{1,0:T(8,128)(2,1)S(1)} %combine.1.recv_refs_0_), channel_id=1, source_target_pairs={{0,12},{1,13},{2,14},{3,15},{4,8},{5,9},{6,10},{7,11},{8,4},{9,5},... | collective-permute-start | bytes 294920 | tf_op jit(solution)/shard_map/ppermute | solution.py:796
  102.3 3.1 %collective-permute-done.32.recv_refs_3_ = s16[384,128]{1,0:T(8,128)(2,1)S(1)} collective-permute-done((s16[384,128]{1,0:T(8,128)(2,1)S(1)}, s16[384,128]{1,0:T(8,128)(2,1)S(1)}, u32[]{:S(2)}, u32[]{:S(2)}) %collective-permute-start.32) | collective-permute-done | bytes 98336 | tf_op jit(solution)/shard_map/ppermute | solution.py:796
  105.5 4.2 %collective-permute-done.31.recv_refs_2_ = s16[384,128]{1,0:T(8,128)(2,1)S(1)} collective-permute-done((s16[384,128]{1,0:T(8,128)(2,1)S(1)}, s16[384,128]{1,0:T(8,128)(2,1)S(1)}, u32[]{:S(2)}, u32[]{:S(2)}) %collective-permute-start.31) | collective-permute-done | bytes 98336 | tf_op jit(solution)/shard_map/ppermute | solution.py:796
  109.9 1.6 %collective-permute-start.35 = (s16[384,128]{1,0:T(8,128)(2,1)S(1)}, s16[384,128]{1,0:T(8,128)(2,1)S(1)}, u32[]{:S(2)}, u32[]{:S(2)}) collective-permute-start(s16[384,128]{1,0:T(8,128)(2,1)S(1)} %recode.1.own_codes_0_), channel_id=1, source_target_pairs={{0,3},{1,2},{2,1},{3,0},{4,7},{5,6},{6,5},{7,4},{8,11},{9,10},{10,... | collective-permute-start | bytes 294920 | tf_op jit(solution)/shard_map/ppermute | solution.py:796
  112.0 1.5 %collective-permute-start.33 = (s16[384,128]{1,0:T(8,128)(2,1)S(1)}, s16[384,128]{1,0:T(8,128)(2,1)S(1)}, u32[]{:S(2)}, u32[]{:S(2)}) collective-permute-start(s16[384,128]{1,0:T(8,128)(2,1)S(1)} %recode.1.own_codes_0_), channel_id=1, source_target_pairs={{0,1},{1,0},{2,3},{3,2},{4,5},{5,4},{6,7},{7,6},{8,9},{9,8},{10,11... | collective-permute-start | bytes 294920 | tf_op jit(solution)/shard_map/ppermute | solution.py:796
  113.4 2.9 %collective-permute-done.35.own_codes_3_ = s16[384,128]{1,0:T(8,128)(2,1)S(1)} collective-permute-done((s16[384,128]{1,0:T(8,128)(2,1)S(1)}, s16[384,128]{1,0:T(8,128)(2,1)S(1)}, u32[]{:S(2)}, u32[]{:S(2)}) %collective-permute-start.35) | collective-permute-done | bytes 98336 | tf_op jit(solution)/shard_map/ppermute | solution.py:796
  118.8 4.2 %update.1 = (f32[4,96,864]{2,1,0:T(8,128)}, f32[4,96,864]{2,1,0:T(8,128)}, f32[4,96,864]{2,1,0:T(8,128)}, f32[4,96,864]{2,1,0:T(8,128)}, bf16[4,96,864]{2,1,0:T(...) custom-call(s16[384,128]{1,0:T(8,128)(2,1)S(1)} %recode.1.own_codes_, ...), custom_call_target="tpu_custom_call" | custom-call | tf_op jit(solution)/shard_map/update/pallas_call | solution.py:1028
  (111 shorter events, 28.7 us)
Async XLA Ops:
  9.0 5.9 %collective-permute-start.2 = (f32[8,128]{1,0:T(8,128)S(1)}, f32[8,128]{1,0:T(8,128)S(1)}, u32[]{:S(2)}, u32[]{:S(2)}) collective-permute-start(f32[8,128]{1,0:T(8,128)S(1)} %get-tuple-element.99), channel_id=1, source_target_pairs={{0,3},{1,2},{2,1},{3,0},{4,7},{5,6},{6,5},{7,4},{8,11},{9,10},{10,... | collective-permute-start | bytes 12296 | tf_op jit(solution)/shard_map/ppermute | solution.py:796
  13.4 3.6 %collective-permute-start = (f32[8,128]{1,0:T(8,128)S(1)}, f32[8,128]{1,0:T(8,128)S(1)}, u32[]{:S(2)}, u32[]{:S(2)}) collective-permute-start(f32[8,128]{1,0:T(8,128)S(1)} %get-tuple-element.99), channel_id=1, source_target_pairs={{0,1},{1,0},{2,3},{3,2},{4,5},{5,4},{6,7},{7,6},{8,9},{9,8},{10,11... | collective-permute-start | bytes 12296 | tf_op jit(solution)/shard_map/ppermute | solution.py:796
  17.0 5.4 %collective-permute-start.5 = (f32[8,128]{1,0:T(8,128)S(1)}, f32[8,128]{1,0:T(8,128)S(1)}, u32[]{:S(2)}, u32[]{:S(2)}) collective-permute-start(f32[8,128]{1,0:T(8,128)S(1)} %add_add_fusion.2.recv_ref_0_.recv1_ref_0_), channel_id=1, source_target_pairs={{0,12},{1,13},{2,14},{3,15},{4,8},{5,9},{6,10},{7,11},{8,4},{9,5},... | collective-permute-start | bytes 12296 | tf_op jit(solution)/shard_map/ppermute | solution.py:796
  20.6 4.5 %collective-permute-start.4 = (f32[8,128]{1,0:T(8,128)S(1)}, f32[8,128]{1,0:T(8,128)S(1)}, u32[]{:S(2)}, u32[]{:S(2)}) collective-permute-start(f32[8,128]{1,0:T(8,128)S(1)} %add_add_fusion.2.recv_ref_0_.recv1_ref_0_), channel_id=1, source_target_pairs={{0,8},{1,9},{2,10},{3,11},{4,12},{5,13},{6,14},{7,15},{8,0},{9,1},... | collective-permute-start | bytes 12296 | tf_op jit(solution)/shard_map/ppermute | solution.py:796
  20.7 4.5 %collective-permute-start.3 = (f32[8,128]{1,0:T(8,128)S(1)}, f32[8,128]{1,0:T(8,128)S(1)}, u32[]{:S(2)}, u32[]{:S(2)}) collective-permute-start(f32[8,128]{1,0:T(8,128)S(1)} %add_add_fusion.2.recv_ref_0_.recv1_ref_0_), channel_id=1, source_target_pairs={{0,4},{1,5},{2,6},{3,7},{4,0},{5,1},{6,2},{7,3},{8,12},{9,13},{10,... | collective-permute-start | bytes 12296 | tf_op jit(solution)/shard_map/ppermute | solution.py:796
  33.4 4.6 %collective-permute-start.8 = (f32[8,128]{1,0:T(8,128)S(1)}, f32[8,128]{1,0:T(8,128)S(1)}, u32[]{:S(2)}, u32[]{:S(2)}) collective-permute-start(f32[8,128]{1,0:T(8,128)S(1)} %get-tuple-element.106), channel_id=1, source_target_pairs={{0,3},{1,2},{2,1},{3,0},{4,7},{5,6},{6,5},{7,4},{8,11},{9,10},{10,... | collective-permute-start | bytes 12296 | tf_op jit(solution)/shard_map/ppermute | solution.py:796
  35.5 3.6 %collective-permute-start.6 = (f32[8,128]{1,0:T(8,128)S(1)}, f32[8,128]{1,0:T(8,128)S(1)}, u32[]{:S(2)}, u32[]{:S(2)}) collective-permute-start(f32[8,128]{1,0:T(8,128)S(1)} %get-tuple-element.106), channel_id=1, source_target_pairs={{0,1},{1,0},{2,3},{3,2},{4,5},{5,4},{6,7},{7,6},{8,9},{9,8},{10,11... | collective-permute-start | bytes 12296 | tf_op jit(solution)/shard_map/ppermute | solution.py:796
  39.1 5.4 %collective-permute-start.11 = (f32[8,128]{1,0:T(8,128)S(1)}, f32[8,128]{1,0:T(8,128)S(1)}, u32[]{:S(2)}, u32[]{:S(2)}) collective-permute-start(f32[8,128]{1,0:T(8,128)S(1)} %add_add_fusion.1.recv_ref_0_.recv2_ref_0_), channel_id=1, source_target_pairs={{0,12},{1,13},{2,14},{3,15},{4,8},{5,9},{6,10},{7,11},{8,4},{9,5},... | collective-permute-start | bytes 12296 | tf_op jit(solution)/shard_map/ppermute | solution.py:796
  40.5 4.5 %collective-permute-start.10 = (f32[8,128]{1,0:T(8,128)S(1)}, f32[8,128]{1,0:T(8,128)S(1)}, u32[]{:S(2)}, u32[]{:S(2)}) collective-permute-start(f32[8,128]{1,0:T(8,128)S(1)} %add_add_fusion.1.recv_ref_0_.recv2_ref_0_), channel_id=1, source_target_pairs={{0,8},{1,9},{2,10},{3,11},{4,12},{5,13},{6,14},{7,15},{8,0},{9,1},... | collective-permute-start | bytes 12296 | tf_op jit(solution)/shard_map/ppermute | solution.py:796
  41.2 3.9 %collective-permute-start.9 = (f32[8,128]{1,0:T(8,128)S(1)}, f32[8,128]{1,0:T(8,128)S(1)}, u32[]{:S(2)}, u32[]{:S(2)}) collective-permute-start(f32[8,128]{1,0:T(8,128)S(1)} %add_add_fusion.1.recv_ref_0_.recv2_ref_0_), channel_id=1, source_target_pairs={{0,4},{1,5},{2,6},{3,7},{4,0},{5,1},{6,2},{7,3},{8,12},{9,13},{10,... | collective-permute-start | bytes 12296 | tf_op jit(solution)/shard_map/ppermute | solution.py:796
  50.5 5.7 %collective-permute-start.15 = (f32[1,8,384]{2,1,0:T(8,128)S(1)}, f32[1,8,384]{2,1,0:T(8,128)S(1)}, u32[]{:S(2)}, u32[]{:S(2)}) collective-permute-start(f32[1,8,384]{2,1,0:T(8,128)S(1)} %bitcast.43), channel_id=1, source_target_pairs={{0,12},{1,13},{2,14},{3,15},{4,8},{5,9},{6,10},{7,11},{8,4},{9,5},... | collective-permute-start | bytes 36872 | tf_op jit(solution)/shard_map/ppermute | solution.py:796
  53.1 4.6 %collective-permute-start.14 = (f32[1,8,384]{2,1,0:T(8,128)S(1)}, f32[1,8,384]{2,1,0:T(8,128)S(1)}, u32[]{:S(2)}, u32[]{:S(2)}) collective-permute-start(f32[1,8,384]{2,1,0:T(8,128)S(1)} %bitcast.44), channel_id=1, source_target_pairs={{0,8},{1,9},{2,10},{3,11},{4,12},{5,13},{6,14},{7,15},{8,0},{9,1},... | collective-permute-start | bytes 36872 | tf_op jit(solution)/shard_map/ppermute | solution.py:796
  54.1 3.8 %collective-permute-start.13 = (f32[1,8,384]{2,1,0:T(8,128)S(1)}, f32[1,8,384]{2,1,0:T(8,128)S(1)}, u32[]{:S(2)}, u32[]{:S(2)}) collective-permute-start(f32[1,8,384]{2,1,0:T(8,128)S(1)} %bitcast.45), channel_id=1, source_target_pairs={{0,4},{1,5},{2,6},{3,7},{4,0},{5,1},{6,2},{7,3},{8,12},{9,13},{10,... | collective-permute-start | bytes 36872 | tf_op jit(solution)/shard_map/ppermute | solution.py:796
  57.9 5.4 %collective-permute-start.18 = (f32[4,8,384]{2,1,0:T(8,128)S(1)}, f32[4,8,384]{2,1,0:T(8,128)S(1)}, u32[]{:S(2)}, u32[]{:S(2)}) collective-permute-start(f32[4,8,384]{2,1,0:T(8,128)S(1)} %stack.1.recv3_ref_0_), channel_id=1, source_target_pairs={{0,3},{1,2},{2,1},{3,0},{4,7},{5,6},{6,5},{7,4},{8,11},{9,10},{10,... | collective-permute-start | bytes 147464 | tf_op jit(solution)/shard_map/ppermute | solution.py:796
  60.3 4.1 %collective-permute-start.17 = (f32[4,8,384]{2,1,0:T(8,128)S(1)}, f32[4,8,384]{2,1,0:T(8,128)S(1)}, u32[]{:S(2)}, u32[]{:S(2)}) collective-permute-start(f32[4,8,384]{2,1,0:T(8,128)S(1)} %stack.1.recv3_ref_0_), channel_id=1, source_target_pairs={{0,2},{1,3},{2,0},{3,1},{4,6},{5,7},{6,4},{7,5},{8,10},{9,11},{10,... | collective-permute-start | bytes 147464 | tf_op jit(solution)/shard_map/ppermute | solution.py:796
  60.8 4.1 %collective-permute-start.16 = (f32[4,8,384]{2,1,0:T(8,128)S(1)}, f32[4,8,384]{2,1,0:T(8,128)S(1)}, u32[]{:S(2)}, u32[]{:S(2)}) collective-permute-start(f32[4,8,384]{2,1,0:T(8,128)S(1)} %stack.1.recv3_ref_0_), channel_id=1, source_target_pairs={{0,1},{1,0},{2,3},{3,2},{4,5},{5,4},{6,7},{7,6},{8,9},{9,8},{10,11... | collective-permute-start | bytes 147464 | tf_op jit(solution)/shard_map/ppermute | solution.py:796
  69.7 7.4 %collective-permute-start.21 = (f32[8,128]{1,0:T(8,128)S(1)}, f32[8,128]{1,0:T(8,128)S(1)}, u32[]{:S(2)}, u32[]{:S(2)}) collective-permute-start(f32[8,128]{1,0:T(8,128)S(1)} %get-tuple-element.124), channel_id=1, source_target_pairs={{0,3},{1,2},{2,1},{3,0},{4,7},{5,6},{6,5},{7,4},{8,11},{9,10},{10,... | collective-permute-start | bytes 12296 | tf_op jit(solution)/shard_map/ppermute | solution.py:796
  71.3 5.8 %collective-permute-start.20 = (f32[8,128]{1,0:T(8,128)S(1)}, f32[8,128]{1,0:T(8,128)S(1)}, u32[]{:S(2)}, u32[]{:S(2)}) collective-permute-start(f32[8,128]{1,0:T(8,128)S(1)} %get-tuple-element.124), channel_id=1, source_target_pairs={{0,2},{1,3},{2,0},{3,1},{4,6},{5,7},{6,4},{7,5},{8,10},{9,11},{10,... | collective-permute-start | bytes 12296 | tf_op jit(solution)/shard_map/ppermute | solution.py:796
  71.8 5.3 %collective-permute-start.19 = (f32[8,128]{1,0:T(8,128)S(1)}, f32[8,128]{1,0:T(8,128)S(1)}, u32[]{:S(2)}, u32[]{:S(2)}) collective-permute-start(f32[8,128]{1,0:T(8,128)S(1)} %get-tuple-element.124), channel_id=1, source_target_pairs={{0,1},{1,0},{2,3},{3,2},{4,5},{5,4},{6,7},{7,6},{8,9},{9,8},{10,11... | collective-permute-start | bytes 12296 | tf_op jit(solution)/shard_map/ppermute | solution.py:796
  77.1 5.5 %collective-permute-start.24 = (f32[8,128]{1,0:T(8,128)S(1)}, f32[8,128]{1,0:T(8,128)S(1)}, u32[]{:S(2)}, u32[]{:S(2)}) collective-permute-start(f32[8,128]{1,0:T(8,128)S(1)} %add_add_fusion.recv5_ref_0_), channel_id=1, source_target_pairs={{0,12},{1,13},{2,14},{3,15},{4,8},{5,9},{6,10},{7,11},{8,4},{9,5},... | collective-permute-start | bytes 12296 | tf_op jit(solution)/shard_map/ppermute | solution.py:796
  78.5 4.5 %collective-permute-start.23 = (f32[8,128]{1,0:T(8,128)S(1)}, f32[8,128]{1,0:T(8,128)S(1)}, u32[]{:S(2)}, u32[]{:S(2)}) collective-permute-start(f32[8,128]{1,0:T(8,128)S(1)} %add_add_fusion.recv5_ref_0_), channel_id=1, source_target_pairs={{0,8},{1,9},{2,10},{3,11},{4,12},{5,13},{6,14},{7,15},{8,0},{9,1},... | collective-permute-start | bytes 12296 | tf_op jit(solution)/shard_map/ppermute | solution.py:796
  79.5 3.7 %collective-permute-start.22 = (f32[8,128]{1,0:T(8,128)S(1)}, f32[8,128]{1,0:T(8,128)S(1)}, u32[]{:S(2)}, u32[]{:S(2)}) collective-permute-start(f32[8,128]{1,0:T(8,128)S(1)} %add_add_fusion.recv5_ref_0_), channel_id=1, source_target_pairs={{0,4},{1,5},{2,6},{3,7},{4,0},{5,1},{6,2},{7,3},{8,12},{9,13},{10,... | collective-permute-start | bytes 12296 | tf_op jit(solution)/shard_map/ppermute | solution.py:796
  89.3 8.4 %collective-permute-start.27 = (s16[352,128]{1,0:T(8,128)(2,1)S(1)}, s16[352,128]{1,0:T(8,128)(2,1)S(1)}, u32[]{:S(2)}, u32[]{:S(2)}) collective-permute-start(s16[352,128]{1,0:T(8,128)(2,1)S(1)} %get-tuple-element.138), channel_id=1, source_target_pairs={{0,1},{1,0},{2,3},{3,2},{4,5},{5,4},{6,7},{7,6},{8,9},{9,8},{10,11... | collective-permute-start | bytes 270344 | tf_op jit(solution)/shard_map/ppermute | solution.py:998
  89.9 7.8 %collective-permute-start.28 = (s16[352,128]{1,0:T(8,128)(2,1)S(1)}, s16[352,128]{1,0:T(8,128)(2,1)S(1)}, u32[]{:S(2)}, u32[]{:S(2)}) collective-permute-start(s16[352,128]{1,0:T(8,128)(2,1)S(1)} %get-tuple-element.139), channel_id=1, source_target_pairs={{0,2},{1,3},{2,0},{3,1},{4,6},{5,7},{6,4},{7,5},{8,10},{9,11},{10,... | collective-permute-start | bytes 270344 | tf_op jit(solution)/shard_map/ppermute | solution.py:998
  91.4 6.3 %collective-permute-start.29 = (s16[352,128]{1,0:T(8,128)(2,1)S(1)}, s16[352,128]{1,0:T(8,128)(2,1)S(1)}, u32[]{:S(2)}, u32[]{:S(2)}) collective-permute-start(s16[352,128]{1,0:T(8,128)(2,1)S(1)} %get-tuple-element.140), channel_id=1, source_target_pairs={{0,3},{1,2},{2,1},{3,0},{4,7},{5,6},{6,5},{7,4},{8,11},{9,10},{10,... | collective-permute-start | bytes 270344 | tf_op jit(solution)/shard_map/ppermute | solution.py:998
  97.9 7.6 %collective-permute-start.32 = (s16[384,128]{1,0:T(8,128)(2,1)S(1)}, s16[384,128]{1,0:T(8,128)(2,1)S(1)}, u32[]{:S(2)}, u32[]{:S(2)}) collective-permute-start(s16[384,128]{1,0:T(8,128)(2,1)S(1)} %combine.1.recv_refs_0_), channel_id=1, source_target_pairs={{0,12},{1,13},{2,14},{3,15},{4,8},{5,9},{6,10},{7,11},{8,4},{9,5},... | collective-permute-start | bytes 294920 | tf_op jit(solution)/shard_map/ppermute | solution.py:796
  100.4 9.3 %collective-permute-start.31 = (s16[384,128]{1,0:T(8,128)(2,1)S(1)}, s16[384,128]{1,0:T(8,128)(2,1)S(1)}, u32[]{:S(2)}, u32[]{:S(2)}) collective-permute-start(s16[384,128]{1,0:T(8,128)(2,1)S(1)} %combine.1.recv_refs_0_), channel_id=1, source_target_pairs={{0,8},{1,9},{2,10},{3,11},{4,12},{5,13},{6,14},{7,15},{8,0},{9,1},... | collective-permute-start | bytes 294920 | tf_op jit(solution)/shard_map/ppermute | solution.py:796
  101.4 8.3 %collective-permute-start.30 = (s16[384,128]{1,0:T(8,128)(2,1)S(1)}, s16[384,128]{1,0:T(8,128)(2,1)S(1)}, u32[]{:S(2)}, u32[]{:S(2)}) collective-permute-start(s16[384,128]{1,0:T(8,128)(2,1)S(1)} %combine.1.recv_refs_0_), channel_id=1, source_target_pairs={{0,4},{1,5},{2,6},{3,7},{4,0},{5,1},{6,2},{7,3},{8,12},{9,13},{10,... | collective-permute-start | bytes 294920 | tf_op jit(solution)/shard_map/ppermute | solution.py:796
  109.9 6.5 %collective-permute-start.35 = (s16[384,128]{1,0:T(8,128)(2,1)S(1)}, s16[384,128]{1,0:T(8,128)(2,1)S(1)}, u32[]{:S(2)}, u32[]{:S(2)}) collective-permute-start(s16[384,128]{1,0:T(8,128)(2,1)S(1)} %recode.1.own_codes_0_), channel_id=1, source_target_pairs={{0,3},{1,2},{2,1},{3,0},{4,7},{5,6},{6,5},{7,4},{8,11},{9,10},{10,... | collective-permute-start | bytes 294920 | tf_op jit(solution)/shard_map/ppermute | solution.py:796
  111.5 5.8 %collective-permute-start.34 = (s16[384,128]{1,0:T(8,128)(2,1)S(1)}, s16[384,128]{1,0:T(8,128)(2,1)S(1)}, u32[]{:S(2)}, u32[]{:S(2)}) collective-permute-start(s16[384,128]{1,0:T(8,128)(2,1)S(1)} %recode.1.own_codes_0_), channel_id=1, source_target_pairs={{0,2},{1,3},{2,0},{3,1},{4,6},{5,7},{6,4},{7,5},{8,10},{9,11},{10,... | collective-permute-start | bytes 294920 | tf_op jit(solution)/shard_map/ppermute | solution.py:796
  112.0 5.4 %collective-permute-start.33 = (s16[384,128]{1,0:T(8,128)(2,1)S(1)}, s16[384,128]{1,0:T(8,128)(2,1)S(1)}, u32[]{:S(2)}, u32[]{:S(2)}) collective-permute-start(s16[384,128]{1,0:T(8,128)(2,1)S(1)} %recode.1.own_codes_0_), channel_id=1, source_target_pairs={{0,1},{1,0},{2,3},{3,2},{4,5},{5,4},{6,7},{7,6},{8,9},{9,8},{10,11... | collective-permute-start | bytes 294920 | tf_op jit(solution)/shard_map/ppermute | solution.py:796
  113.4 4.3 %collective-permute-start.36 = (s16[384,128]{1,0:T(8,128)(2,1)S(1)}, s16[384,128]{1,0:T(8,128)(2,1)S(1)}, u32[]{:S(2)}, u32[]{:S(2)}) collective-permute-start(s16[384,128]{1,0:T(8,128)(2,1)S(1)} %recode.1.own_codes_0_), channel_id=1, source_target_pairs={{0,16},{16,0},{1,17},{17,1},{2,18},{18,2},{3,19},{19,3},{4,20},{20... | collective-permute-start | bytes 294920 | tf_op jit(solution)/shard_map/ppermute | solution.py:836
  (30 other events, 375.9 us)
where the time goes:
time: 123 us
  starting transfers between devices  45.5 us (37%)
  Pallas kernels  44 us (36%)
  waiting for transfers between devices  32.2 us (26%)
  between operations  1.27 us (1%)
    ppermute x30, starting transfers between devices, from_partners(): lax.ppermute(values, 'dp', [(i, i ^ offset << shift) for i in range(size)])  40.9 us
    ppermute x30, waiting for transfers between devices, from_partners(): lax.ppermute(values, 'dp', [(i, i ^ offset << shift) for i in range(size)])  28.9 us
    pallas_call x1, Pallas kernels, shards(): pl.pallas_call(first_kernel, in_specs=[pl.BlockSpec(memory_space=pltpu.HB...  8.27 us
    pallas_call x1, Pallas kernels, shards(): pl.pallas_call(functools.partial(second_kernel, cell_count), in_specs=[he...  8.22 us
    pallas_call x1, Pallas kernels, shards(): pl.pallas_call(functools.partial(back_second_kernel, cell_count, float(al...  4.8 us
    pallas_call x1, Pallas kernels, shards(): pl.pallas_call(back_stem_kernel, in_specs=[held()] * 4, out_specs=held(),...  4.77 us
    pallas_call x1, Pallas kernels, shards(): pl.pallas_call(update_kernel, grid=(4,), in_specs=[code_spec] * 2 + [fact...  4.15 us
    pallas_call x1, Pallas kernels, shards(): pl.pallas_call(second_weight_kernel, in_specs=[held()] * 2, out_specs=[he...  3.79 us
  transfers between devices with their start and end apart: 40, of which 27 were waited for; matrix products, arithmetic and copies ran while one was open for 0% of the time, Pallas kernels for 8%

commit v1 on v0

--- a/solution.py
+++ b/solution.py
@@ -370,7 +370,7 @@
 
 def student_kernel(
     cell_count, ratio_ref, labels_ref, labelled_ref, order_ref,
-    second_ref, recv_ref, norm, head_ref, stem_sum_ref, prob_ref,
+    second_ref, recv_ref, norm, head_ref, stem_sum_ref,
     msg_ref, bent_ref,
     terms,
 ):
@@ -415,7 +415,12 @@
         msg_ref[:, b * LANE : (b + 1) * LANE] = jnp.where(
             row < IMAGES, both_halves(sums[2 + b]), both_halves(sums[4 + b])
         )
-    msg_ref[:, 2 * LANE :] = jnp.where(row < IMAGES, info + prob_ref[...], low.astype(F32))
+    msg_ref[:, 2 * LANE :] = jnp.where(row < IMAGES, info, low.astype(F32))
+
+
+def assemble_kernel(facts_ref, prob_ref, out_ref):
+    out_ref[0, :, 0 : 2 * LANE] = facts_ref[:, 0 : 2 * LANE]
+    out_ref[0, :, 2 * LANE :] = facts_ref[:, 2 * LANE :] + prob_ref[...]
 
 
 def loss_part(images, all_images, cell_count, recv_refs, head_ref, rows_ref, means, small_ref):
@@ -551,23 +556,22 @@
     return frame[first_line + 1 : first_line + 1 + DEEP, 1 : ACROSS + 1].reshape(CHUNK, frame.shape[-1])
 
 
-def second_weight_kernel(frame_ref, dy_ref, keep_ref, send_ref, gacc):
-    for b in range(2):
-        for step in range(STEPS):
-            pair = jnp.concatenate(
-                [middle_lines(dy_ref.at[b], step * DEEP), middle_lines(dy_ref.at[b], step * DEEP + 1)], axis=1
-            )
-            product = dot_rows(pair, taps(frame_ref.at[b], step, (0, 1)))
-            gacc[b] = product if step == 0 else gacc[b] + product
+def second_weight_kernel(other, frame_ref, dy_ref, grad_ref, gacc):
+    view = lax.axis_index("view")
+    branch = 1 - view if other else view
+    for step in range(STEPS):
+        pair = jnp.concatenate(
+            [middle_lines(dy_ref.at[branch], step * DEEP), middle_lines(dy_ref.at[branch], step * DEEP + 1)], axis=1
+        )
+        product = dot_rows(pair, taps(frame_ref.at[branch], step, (0, 1)))
+        gacc[...] = product if step == 0 else gacc[...] + product
     blocks = []
-    for b in range(2):
-        blocks.append([])
-        for tap in range(TAPS):
-            ky, kx = tap // 3, tap % 3
-            row = LANE if ky == 0 else 0
-            lane = (ky // 2) * 3 * LANE + kx * LANE
-            blocks[b].append(gacc[b, row : row + CH, lane : lane + CH])
-    keep_and_send(keep_ref, send_ref, blocks)
+    for tap in range(TAPS):
+        ky, kx = tap // 3, tap % 3
+        row = LANE if ky == 0 else 0
+        lane = (ky // 2) * 3 * LANE + kx * LANE
+        blocks.append(gacc[row : row + CH, lane : lane + CH])
+    pack_grad(grad_ref, blocks)
 
 
 def back_weight_kernel(
@@ -705,7 +709,7 @@
 
     @pl.when(conv == 0)
     def _():
-        facts = own_facts[...] + other_facts[...]
+        facts = own_facts[GRAD_ROWS:, :] + other_facts[GRAD_ROWS:, :]
         small, sums = facts[:24], facts[24:]
         mine = lax.axis_index("dp") & (QUARTERS - 1)
         stem = jnp.zeros((27, LANE), F32)
@@ -733,7 +737,7 @@
         norm_o[...] = norm
         cross_o[...] = small[20:21, 0:1]
         consistency_o[...] = small[20:21, 1:2]
-        count_o[...] = own_facts[20:21, 2:3]
+        count_o[...] = own_facts[GRAD_ROWS + 20 : GRAD_ROWS + 21, 2:3]
         sw_o[...], sf_o[...], ss_o[...], st_o[...] = adam_terms(stem, factor, sw[...], sf[...], ss[...], st[...])
         sb_o[...] = sw_o[...].astype(BF16)
         hw_o[...], hf_o[...], hs_o[...], ht_o[...] = adam_terms(head, factor, hw[...], hf[...], hs[...], ht[...])
@@ -747,7 +751,7 @@
             lanes = slice(k * LANE, min((k + 1) * LANE, WIDE))
             gradient = ref[second, k * CH : (k + 1) * CH, 0 : lanes.stop - lanes.start]
             weight, first, second_moment, teacher = adam_terms(
-                gradient, factor, cw[:, lanes], cf[:, lanes], cs[:, lanes], ct[:, lanes]
+                gradient, factor, cw[conv, :, lanes], cf[conv, :, lanes], cs[conv, :, lanes], ct[conv, :, lanes]
             )
             cw_o[:, lanes] = weight
             cf_o[:, lanes] = first
@@ -790,11 +794,20 @@
     return jax.ShapeDtypeStruct(shape, kind)
 
 
+def to_partner(values, difference):
+    size = lax.axis_size("dp")
+    return lax.ppermute(values, ("view", "dp"), [(i, i ^ (difference + size)) for i in range(2 * size)])
+
+
+def far_last(ways):
+    return (1, 3, 2) if ways == 4 else range(1, ways)
+
+
 def from_partners(values, shift, ways):
-    size = lax.axis_size("dp")
-    return [values] + [
-        lax.ppermute(values, "dp", [(i, i ^ (offset << shift)) for i in range(size)]) for offset in range(1, ways)
-    ]
+    parts = [to_partner(values, 0)] + [None] * (ways - 1)
+    for offset in far_last(ways):
+        parts[offset] = to_partner(values, offset << shift)
+    return parts
 
 
 def stages():
@@ -805,6 +818,7 @@
         ways = min(4, size >> shift)
         groups.append((shift, ways))
         shift += 2
+    assert len(groups) % 2 == 0
     return groups
 
 
@@ -908,7 +922,9 @@
         name="first_conv",
     )(*(pltpu.with_memory_space_constraint(v, pltpu.HBM) for v in (pixels, stem_weight, teacher_stem, conv, conv_t)))
     first_s, first_t, low, moved = (hold(v) for v in (first_s, first_t, low, moved))
-    recv1, (weight_s, weight_t) = sum_parts(message, (forward_weights(conv), forward_weights(conv_t)))
+    recv1, (weight_s, weight_t, (back_weight_two, back_weight_one)) = sum_parts(
+        message, (forward_weights(conv), forward_weights(conv_t), backward_weights(conv))
+    )
 
     second_s, second_t, hidden, bent_one, message = pl.pallas_call(
         functools.partial(second_kernel, cell_count),
@@ -931,22 +947,23 @@
         compiler_params=PARAMS,
         name="teacher_logits",
     )(shake_ratio, second_t, recv2, teacher_norm, head_t, stem_sums)
-    prob, conv_later = lax.optimization_barrier((prob, conv))
     other = swap_view(prob)
-    back_weight_two, back_weight_one = backward_weights(conv_later)
-    other, back_weight_two = lax.optimization_barrier((other, back_weight_two))
     facts, bent_two = pl.pallas_call(
         functools.partial(student_kernel, cell_count),
-        in_specs=[scalars()] * 4 + [held(), recv_spec] + [held()] * 4,
+        in_specs=[scalars()] * 4 + [held(), recv_spec] + [held()] * 3,
         out_specs=[held()] * 2,
         out_shape=[struct((8, 3 * LANE)), pltpu.VMEM(values_shape, F32)],
         scratch_shapes=[terms_scratch],
         compiler_params=PARAMS,
         cost_estimate=pl.CostEstimate(flops=4_000_000_000, bytes_accessed=8_000_000, transcendentals=0),
         name="student_logits",
-    )(shake_ratio, labels, labelled, view_order, second_s, recv2, norm_param, head, stem_sums, other)
+    )(shake_ratio, labels, labelled, view_order, second_s, recv2, norm_param, head, stem_sums)
     bent_two = hold(bent_two)
-    recv3 = gather_parts(facts.reshape(1, 8, 3 * LANE), groups[::-1])
+    facts, other = lax.optimization_barrier((facts, other))
+    facts = pl.pallas_call(
+        assemble_kernel, out_shape=struct((1, 8, 3 * LANE)), compiler_params=PARAMS, name="assemble"
+    )(facts, other)
+    recv3 = gather_parts(facts, groups[::-1])
 
     du, dy, message, small, dmix = pl.pallas_call(
         functools.partial(back_second_kernel, cell_count, float(all_images)),
@@ -962,18 +979,23 @@
         name="back_second",
     )(second_s, first_s, bent_two, bent_one, recv1, recv2, recv3, norm_param, head, back_weight_two)
     du, dy = hold(du), hold(dy)
-    keep2, send2 = pl.pallas_call(
-        second_weight_kernel,
-        in_specs=[held()] * 2,
-        out_specs=[held()] * 2,
-        out_shape=[grad_shape] * 2,
-        scratch_shapes=[pltpu.VMEM((2, 2 * LANE, 6 * LANE), F32)],
-        compiler_params=PARAMS,
-        cost_estimate=pl.CostEstimate(flops=8_000_000_000, bytes_accessed=16_000_000, transcendentals=0),
-        name="second_weight",
-    )(hidden, dy)
-    recv5, (keep2, send2) = sum_parts(message, (keep2, send2))
+
+    def second_weight(other):
+        return pl.pallas_call(
+            functools.partial(second_weight_kernel, other),
+            in_specs=[held()] * 2,
+            out_specs=held(),
+            out_shape=grad_shape,
+            scratch_shapes=[pltpu.VMEM((2 * LANE, 6 * LANE), F32)],
+            compiler_params=PARAMS,
+            cost_estimate=pl.CostEstimate(flops=4_000_000_000, bytes_accessed=8_000_000, transcendentals=0),
+            name="second_weight",
+        )(hidden, dy)
+
+    send2, keep2 = second_weight(True), second_weight(False)
+    recv5, send2 = sum_parts(message, send2)
     recv_grad2 = swap_view(send2)
+    recv5, keep2, recv_grad2 = lax.optimization_barrier((recv5, keep2, recv_grad2))
 
     frame, keep1, send1 = pl.pallas_call(
         functools.partial(back_weight_kernel, cell_count),
@@ -994,9 +1016,10 @@
         compiler_params=PARAMS,
         name="encode",
     )(keep2, recv_grad2, keep1, recv_grad1)
-    scattered = (coded[0],) + tuple(
-        lax.ppermute(coded[offset], "dp", [(i, i ^ offset) for i in range(dp)]) for offset in range(1, QUARTERS)
-    )
+    scattered = [to_partner(coded[0], 0)] + [None] * (QUARTERS - 1)
+    for offset in far_last(QUARTERS):
+        scattered[offset] = to_partner(coded[offset], offset)
+    scattered = tuple(scattered)
 
     stem_grad = pl.pallas_call(
         back_stem_kernel,
@@ -1017,19 +1040,17 @@
         codes = pl.pallas_call(recode_kernel, out_shape=code_shape, compiler_params=PARAMS, name="recode")(
             tuple(from_partners(codes, *group))
         )
-    own = tuple(from_partners(codes, *groups[0]))
-    other_grads = tuple(swap_view(part) for part in own)
+    other_grads = tuple(from_partners(codes, *groups[0]))
+    own = tuple(swap_view(part) for part in other_grads)
 
     conv_block = pl.BlockSpec((None, CH, WIDE), lambda i: (i, 0, 0))
     stem_block, norm_block = whole((27, CH)), norm_spec
-    code_spec = (whole((CODE_ROWS, LANE)),) * QUARTERS
-    facts_spec = pl.BlockSpec((32, LANE), lambda i: (GRAD_ROWS // 32, 0))
+    code_spec = (held(),) * QUARTERS
     grads_scratch = pltpu.VMEM((2, GRAD_ROWS, LANE), F32)
     outs = pl.pallas_call(
         update_kernel,
         grid=(4,),
-        in_specs=[code_spec] * 2 + [facts_spec] * 2
-        + [conv_block] * 4 + [stem_block] * 4 + [head_spec] * 4 + [norm_block] * 4,
+        in_specs=[code_spec] * 2 + [held()] * 18,
         out_specs=[conv_block] * 5 + [stem_block] * 5 + [head_spec] * 5 + [norm_block] * 4 + [whole((1, 1))] * 4,
         out_shape=[struct((4, CH, WIDE))] * 4 + [struct((4, CH, WIDE), BF16)]
         + [struct((27, CH))] * 4 + [struct((27, CH), BF16)]

time: 123 us -> 117 us (0.951)
  waiting for transfers between devices: 32.2 us -> 26.2 us
    ppermute x33 -> x44, waiting for transfers between devices: 28.9 us -> 23.7 us  [to_partner(): lax.ppermute(values, ('view', 'dp'), [(i, i ^ difference + size) for i in...]
    ppermute x33 -> x44, starting transfers between devices: 44.4 us -> 42.8 us  [to_partner(): lax.ppermute(values, ('view', 'dp'), [(i, i ^ difference + size) for i in...]
    pallas_call x2 -> x4, Pallas kernels: 7.94 us -> 7.92 us  [the longest x1 4.15 us: shards(): pl.pallas_call(update_kernel, grid=(4,), in_specs=[code_spec] * 2 + [held...]
  transfers between devices with their start and end apart: 40 -> 51, of which waited for: 27 -> 22; matrix products, arithmetic and copies ran while one was open for 0% -> 0% of each run, Pallas kernels for 8% -> 11%
where the time goes in v1:
time: 117 us
  starting transfers between devices  44.3 us (38%)
  Pallas kernels  44.1 us (38%)
  waiting for transfers between devices  26.2 us (22%)
  between operations  1.36 us (1%)
    ppermute x44, starting transfers between devices, to_partner(): lax.ppermute(values, ('view', 'dp'), [(i, i ^ difference + size) for i in...  42.8 us
    ppermute x44, waiting for transfers between devices, to_partner(): lax.ppermute(values, ('view', 'dp'), [(i, i ^ difference + size) for i in...  23.7 us
    pallas_call x1, Pallas kernels, shards(): pl.pallas_call(first_kernel, in_specs=[pl.BlockSpec(memory_space=pltpu.HB...  8.27 us
    pallas_call x1, Pallas kernels, shards(): pl.pallas_call(functools.partial(second_kernel, cell_count), in_specs=[he...  8.23 us
    pallas_call x1, Pallas kernels, shards(): pl.pallas_call(functools.partial(back_second_kernel, cell_count, float(al...  4.93 us
    pallas_call x1, Pallas kernels, shards(): pl.pallas_call(back_stem_kernel, in_specs=[held()] * 4, out_specs=held(),...  4.77 us
    pallas_call x1, Pallas kernels, shards(): pl.pallas_call(update_kernel, grid=(4,), in_specs=[code_spec] * 2 + [held...  4.15 us
    pallas_call x2, Pallas kernels, second_weight(): pl.pallas_call(functools.partial(second_weight_kernel, other), in_specs=[...  3.77 us
  transfers between devices with their start and end apart: 51, of which 22 were waited for; matrix products, arithmetic and copies ran while one was open for 0% of the time, Pallas kernels for 11%

profile of v1, /device:TPU:0, one launch (start us, length us, event | category | flops | bytes accessed | tf_op | source)
XLA Modules:
  0.0 117.0 jit_solution(14010978897050086806)
XLA Ops:
  0.7 8.3 %first_conv.1 = (f32[4096,256]{1,0:T(8,128)S(1)}, f32[4096,256]{1,0:T(8,128)S(1)}, bf16[34,10,16,128]{3,2,1,0:T(8,128)(2,1)S(1)}, f32[3,288,128]{2,1,0:T(8,128)S...) custom-call(bf16[4,3,32,32]{3,2,1,0:T(8,128)(2,1)} %bitcast.44, f32[27,96]{1,0:T(8,128)} %sw.1, f32[27,96]{1,0:T(8,128)} %st.1, ...), custom_call_target="tpu_custom_call" | custom-call | tf_op jit(solution)/shard_map/first_conv/pallas_call | solution.py:907
  9.0 3.4 %collective-permute-start.3 = (f32[8,128]{1,0:T(8,128)S(1)}, f32[8,128]{1,0:T(8,128)S(1)}, u32[]{:S(2)}, u32[]{:S(2)}) collective-permute-start(f32[8,128]{1,0:T(8,128)S(1)} %get-tuple-element.101), channel_id=1, source_target_pairs={{0,19},{1,18},{2,17},{3,16},{4,23},{5,22},{6,21},{7,20},{8,27},{9,... | collective-permute-start | bytes 12296 | tf_op jit(solution)/shard_map/ppermute | solution.py:799
  16.2 3.5 %collective-permute-start.7 = (f32[8,128]{1,0:T(8,128)S(1)}, f32[8,128]{1,0:T(8,128)S(1)}, u32[]{:S(2)}, u32[]{:S(2)}) collective-permute-start(f32[8,128]{1,0:T(8,128)S(1)} %add_add_fusion.2), channel_id=1, source_target_pairs={{0,28},{1,29},{2,30},{3,31},{4,24},{5,25},{6,26},{7,27},{8,20},{9,... | collective-permute-start | bytes 12296 | tf_op jit(solution)/shard_map/ppermute | solution.py:799
  21.1 2.6 %collective-permute-done.6.recv_ref_2_.recv1_ref_2_ = f32[8,128]{1,0:T(8,128)S(1)} collective-permute-done((f32[8,128]{1,0:T(8,128)S(1)}, f32[8,128]{1,0:T(8,128)S(1)}, u32[]{:S(2)}, u32[]{:S(2)}) %collective-permute-start.6) | collective-permute-done | bytes 4128 | tf_op jit(solution)/shard_map/ppermute | solution.py:799
  23.7 8.2 %second_conv.1 = (f32[4096,256]{1,0:T(8,128)S(1)}, f32[4096,256]{1,0:T(8,128)S(1)}, bf16[2,34,10,16,128]{4,3,2,1,0:T(8,128)(2,1)S(1)}, f32[4096,256]{1,0:T(8,128)S(1)}, f32[8,128]{1,0:T(8,128)S(1)}) custom-call(f32[4096,256]{1,0:T(8,128)S(1)} %get-tuple-element.99.first_s.first_ref, f32[4096,256]{1,0:T(8,128)S(1)} %get-tuple-element.100.first_t, ...), custom_call_target="tpu_custom_call" | custom-call | tf_op jit(solution)/shard_map/second_conv/pallas_call | solution.py:929
  32.0 2.6 %collective-permute-start.11 = (f32[8,128]{1,0:T(8,128)S(1)}, f32[8,128]{1,0:T(8,128)S(1)}, u32[]{:S(2)}, u32[]{:S(2)}) collective-permute-start(f32[8,128]{1,0:T(8,128)S(1)} %get-tuple-element.111), channel_id=1, source_target_pairs={{0,19},{1,18},{2,17},{3,16},{4,23},{5,22},{6,21},{7,20},{8,27},{9,... | collective-permute-start | bytes 12296 | tf_op jit(solution)/shard_map/ppermute | solution.py:799
  36.0 1.7 %collective-permute-done.10 = f32[8,128]{1,0:T(8,128)S(1)} collective-permute-done((f32[8,128]{1,0:T(8,128)S(1)}, f32[8,128]{1,0:T(8,128)S(1)}, u32[]{:S(2)}, u32[]{:S(2)}) %collective-permute-start.10) | collective-permute-done | bytes 4128 | tf_op jit(solution)/shard_map/ppermute | solution.py:799
  37.8 1.6 %collective-permute-start.15 = (f32[8,128]{1,0:T(8,128)S(1)}, f32[8,128]{1,0:T(8,128)S(1)}, u32[]{:S(2)}, u32[]{:S(2)}) collective-permute-start(f32[8,128]{1,0:T(8,128)S(1)} %add_add_fusion.1), channel_id=1, source_target_pairs={{0,28},{1,29},{2,30},{3,31},{4,24},{5,25},{6,26},{7,27},{8,20},{9,... | collective-permute-start | bytes 12296 | tf_op jit(solution)/shard_map/ppermute | solution.py:799
  39.8 2.3 %collective-permute-start.13 = (f32[8,128]{1,0:T(8,128)S(1)}, f32[8,128]{1,0:T(8,128)S(1)}, u32[]{:S(2)}, u32[]{:S(2)}) collective-permute-start(f32[8,128]{1,0:T(8,128)S(1)} %add_add_fusion.1), channel_id=1, source_target_pairs={{0,20},{1,21},{2,22},{3,23},{4,16},{5,17},{6,18},{7,19},{8,28},{9,... | collective-permute-start | bytes 12296 | tf_op jit(solution)/shard_map/ppermute | solution.py:799
  43.4 1.7 %teacher_logits.1 = f32[8,128]{1,0:T(8,128)S(1)} custom-call(s32[1,4]{1,0:T(1,128)S(1)} %copy-done.16, f32[4096,256]{1,0:T(8,128)S(1)} %get-tuple-element.116.second_ref, f32[8,128]{1,0:T(8,128)S(1)} %collective-permute-done.12.recv_ref_0_.recv2_ref_0_, f32[8,128]{1,0:T(8,128)S(1)} %collective-permute-done.13.recv_ref_1_.recv2_ref_1_, ...), custom_call_target="tpu_custom_call" | custom-call | tf_op jit(solution)/shard_map/teacher_logits/pallas_call | solution.py:941
  45.3 2.4 %student_logits.1 = (f32[8,384]{1,0:T(8,128)S(1)}, f32[4096,256]{1,0:T(8,128)S(1)}) custom-call(s32[1,4]{1,0:T(1,128)S(1)} %copy-done.16, s32[4]{0:T(128)S(1)} %copy-done.19, s32[4]{0:T(128)S(1)} %copy-done.20, s32[64]{0:T(128)S(1)} %copy-done.21, f32[4096,256]{1,0:T(8,128)S(1)} %get-tuple-element.110.second_ref, ...), custom_call_target="tpu_custom_call" | custom-call | flops 4000000000 | bytes 8000000 | tf_op jit(solution)/shard_map/student_logits/pallas_call | solution.py:951
  47.8 2.4 %collective-permute-start.20 = (f32[1,8,384]{2,1,0:T(8,128)S(1)}, f32[1,8,384]{2,1,0:T(8,128)S(1)}, u32[]{:S(2)}, u32[]{:S(2)}) collective-permute-start(f32[1,8,384]{2,1,0:T(8,128)S(1)} %assemble.1), channel_id=1, source_target_pairs={{0,28},{1,29},{2,30},{3,31},{4,24},{5,25},{6,26},{7,27},{8,20},{9,... | collective-permute-start | bytes 36872 | tf_op jit(solution)/shard_map/ppermute | solution.py:799
  52.8 1.4 %collective-permute-done.19.parts_2_ = f32[1,8,384]{2,1,0:T(8,128)S(1)} collective-permute-done((f32[1,8,384]{2,1,0:T(8,128)S(1)}, f32[1,8,384]{2,1,0:T(8,128)S(1)}, u32[]{:S(2)}, u32[]{:S(2)}) %collective-permute-start.19) | collective-permute-done | bytes 12320 | tf_op jit(solution)/shard_map/ppermute | solution.py:799
  57.7 1.3 %collective-permute-done.24.recv3_ref_3_ = f32[4,8,384]{2,1,0:T(8,128)S(1)} collective-permute-done((f32[4,8,384]{2,1,0:T(8,128)S(1)}, f32[4,8,384]{2,1,0:T(8,128)S(1)}, u32[]{:S(2)}, u32[]{:S(2)}) %collective-permute-start.24) | collective-permute-done | bytes 49184 | tf_op jit(solution)/shard_map/ppermute | solution.py:799
  60.2 4.9 %back_second.1 = (f32[4096,256]{1,0:T(8,128)S(1)}, bf16[2,34,10,16,128]{4,3,2,1,0:T(8,128)(2,1)S(1)}, f32[8,128]{1,0:T(8,128)S(1)}, f32[24,128]{1,0:T(8,128)S(1)}, f32[8,128]{1,0:T(8,128)S(1)}) custom-call(f32[4096,256]{1,0:T(8,128)S(1)} %get-tuple-element.110.second_ref, f32[4096,256]{1,0:T(8,128)S(1)} %get-tuple-element.99.first_s.first_ref, ...), custom_call_target="tpu_custom_call" | custom-call | tf_op jit(solution)/shard_map/back_second/pallas_call | solution.py:968
  65.2 1.8 %collective-permute-start.28 = (f32[8,128]{1,0:T(8,128)S(1)}, f32[8,128]{1,0:T(8,128)S(1)}, u32[]{:S(2)}, u32[]{:S(2)}) collective-permute-start(f32[8,128]{1,0:T(8,128)S(1)} %get-tuple-element.122), channel_id=1, source_target_pairs={{0,19},{1,18},{2,17},{3,16},{4,23},{5,22},{6,21},{7,20},{8,27},{9,... | collective-permute-start | bytes 12296 | tf_op jit(solution)/shard_map/ppermute | solution.py:799
  68.6 1.9 %second_weight.2 = f32[672,128]{1,0:T(8,128)S(1)} custom-call(bf16[2,34,10,16,128]{4,3,2,1,0:T(8,128)(2,1)S(1)} %get-tuple-element.123.frame_ref, bf16[2,34,10,16,128]{4,3,2,1,0:T(8,128)(2,1)S(1)} %get-tuple-element.124.dy_ref), custom_call_target="tpu_custom_call" | custom-call | flops 4000000000 | bytes 8000000 | tf_op jit(solution)/shard_map/second_weight/pallas_call | solution.py:984
  70.6 1.5 %collective-permute-start.32 = (f32[8,128]{1,0:T(8,128)S(1)}, f32[8,128]{1,0:T(8,128)S(1)}, u32[]{:S(2)}, u32[]{:S(2)}) collective-permute-start(f32[8,128]{1,0:T(8,128)S(1)} %add_add_fusion), channel_id=1, source_target_pairs={{0,28},{1,29},{2,30},{3,31},{4,24},{5,25},{6,26},{7,27},{8,20},{9,... | collective-permute-start | bytes 12296 | tf_op jit(solution)/shard_map/ppermute | solution.py:799
  72.7 1.8 %collective-permute-start.30 = (f32[8,128]{1,0:T(8,128)S(1)}, f32[8,128]{1,0:T(8,128)S(1)}, u32[]{:S(2)}, u32[]{:S(2)}) collective-permute-start(f32[8,128]{1,0:T(8,128)S(1)} %add_add_fusion), channel_id=1, source_target_pairs={{0,20},{1,21},{2,22},{3,23},{4,16},{5,17},{6,18},{7,19},{8,28},{9,... | collective-permute-start | bytes 12296 | tf_op jit(solution)/shard_map/ppermute | solution.py:799
  75.0 1.9 %second_weight.3.keep2 = f32[672,128]{1,0:T(8,128)S(1)} custom-call(bf16[2,34,10,16,128]{4,3,2,1,0:T(8,128)(2,1)S(1)} %get-tuple-element.123.frame_ref, bf16[2,34,10,16,128]{4,3,2,1,0:T(8,128)(2,1)S(1)} %get-tuple-element.124.dy_ref), custom_call_target="tpu_custom_call" | custom-call | flops 4000000000 | bytes 8000000 | tf_op jit(solution)/shard_map/second_weight/pallas_call | solution.py:984
  77.0 3.6 %back_weight.1 = (bf16[2,34,10,16,128]{4,3,2,1,0:T(8,128)(2,1)S(1)}, f32[704,128]{1,0:T(8,128)S(1)}, f32[704,128]{1,0:T(8,128)S(1)}) custom-call(f32[4096,256]{1,0:T(8,128)S(1)} %get-tuple-element.120.du_ref, f32[4096,256]{1,0:T(8,128)S(1)} %get-tuple-element.99.first_s.first_ref, bf16[34,10,16,128]{3,2,1,0:T(8,128)(2,1)S(1)} %copy-done.18, ...), custom_call_target="tpu_custom_call" | custom-call | flops 8000000000 | bytes 16000000 | tf_op jit(solution)/shard_map/back_weight/pallas_call | solution.py:1000
  81.0 1.3 %collective-permute-done.34.recv1.other_facts = f32[704,128]{1,0:T(8,128)S(1)} collective-permute-done((f32[704,128]{1,0:T(8,128)S(1)}, f32[704,128]{1,0:T(8,128)S(1)}, u32[]{:S(2)}, u32[]{:S(2)}) %collective-permute-start.34) | collective-permute-done | bytes 360480 | tf_op jit(solution)/shard_map/ppermute | solution.py:850
  83.8 1.5 %collective-permute-start.37 = (s16[352,128]{1,0:T(8,128)(2,1)S(1)}, s16[352,128]{1,0:T(8,128)(2,1)S(1)}, u32[]{:S(2)}, u32[]{:S(2)}) collective-permute-start(s16[352,128]{1,0:T(8,128)(2,1)S(1)} %get-tuple-element.145), channel_id=1, source_target_pairs={{0,18},{1,19},{2,16},{3,17},{4,22},{5,23},{6,20},{7,21},{8,26},{9,... | collective-permute-start | bytes 270344 | tf_op jit(solution)/shard_map/ppermute | solution.py:799
  86.0 4.8 %back_stem.1.stem_ref = f32[27,128]{1,0:T(8,128)S(1)} custom-call(bf16[2,34,10,16,128]{4,3,2,1,0:T(8,128)(2,1)S(1)} %get-tuple-element.135.frame_ref, f32[3,288,128]{2,1,0:T(8,128)S(1)} %get-tuple-element.136.moved_ref, f32[8,128]{1,0:T(8,128)S(1)} %get-tuple-element.137.dmix_ref, bf16[2,768,256]{2,1,0:T(8,128)(2,1)S(1)} %get-tuple-element.138.w_ref), custom_call_target="tpu_custom_call" | custom-call | flops 8000000000 | bytes 16000000 | tf_op jit(solution)/shard_map/back_stem/pallas_call | solution.py:1024
  91.0 1.7 %collective-permute-start.42 = (s16[384,128]{1,0:T(8,128)(2,1)S(1)}, s16[384,128]{1,0:T(8,128)(2,1)S(1)}, u32[]{:S(2)}, u32[]{:S(2)}) collective-permute-start(s16[384,128]{1,0:T(8,128)(2,1)S(1)} %combine.1), channel_id=1, source_target_pairs={{0,28},{1,29},{2,30},{3,31},{4,24},{5,25},{6,26},{7,27},{8,20},{9,... | collective-permute-start | bytes 294920 | tf_op jit(solution)/shard_map/ppermute | solution.py:799
  93.1 2.1 %collective-permute-start.40 = (s16[384,128]{1,0:T(8,128)(2,1)S(1)}, s16[384,128]{1,0:T(8,128)(2,1)S(1)}, u32[]{:S(2)}, u32[]{:S(2)}) collective-permute-start(s16[384,128]{1,0:T(8,128)(2,1)S(1)} %combine.1), channel_id=1, source_target_pairs={{0,20},{1,21},{2,22},{3,23},{4,16},{5,17},{6,18},{7,19},{8,28},{9,... | collective-permute-start | bytes 294920 | tf_op jit(solution)/shard_map/ppermute | solution.py:799
  95.3 2.4 %collective-permute-done.42.recv_refs_3_ = s16[384,128]{1,0:T(8,128)(2,1)S(1)} collective-permute-done((s16[384,128]{1,0:T(8,128)(2,1)S(1)}, s16[384,128]{1,0:T(8,128)(2,1)S(1)}, u32[]{:S(2)}, u32[]{:S(2)}) %collective-permute-start.42) | collective-permute-done | bytes 98336 | tf_op jit(solution)/shard_map/ppermute | solution.py:799
  97.7 4.7 %collective-permute-done.41.recv_refs_2_ = s16[384,128]{1,0:T(8,128)(2,1)S(1)} collective-permute-done((s16[384,128]{1,0:T(8,128)(2,1)S(1)}, s16[384,128]{1,0:T(8,128)(2,1)S(1)}, u32[]{:S(2)}, u32[]{:S(2)}) %collective-permute-start.41) | collective-permute-done | bytes 98336 | tf_op jit(solution)/shard_map/ppermute | solution.py:799
  102.6 1.8 %collective-permute-start.49 = (s16[384,128]{1,0:T(8,128)(2,1)S(1)}, s16[384,128]{1,0:T(8,128)(2,1)S(1)}, u32[]{:S(2)}, u32[]{:S(2)}) collective-permute-start(s16[384,128]{1,0:T(8,128)(2,1)S(1)} %recode.1), channel_id=1, source_target_pairs={{0,19},{1,18},{2,17},{3,16},{4,23},{5,22},{6,21},{7,20},{8,27},{9,... | collective-permute-start | bytes 294920 | tf_op jit(solution)/shard_map/ppermute | solution.py:799
  106.1 2.4 %collective-permute-done.49.other_codes_3_ = s16[384,128]{1,0:T(8,128)(2,1)S(1)} collective-permute-done((s16[384,128]{1,0:T(8,128)(2,1)S(1)}, s16[384,128]{1,0:T(8,128)(2,1)S(1)}, u32[]{:S(2)}, u32[]{:S(2)}) %collective-permute-start.49) | collective-permute-done | bytes 98336 | tf_op jit(solution)/shard_map/ppermute | solution.py:799
  108.6 2.1 %collective-permute-done.47.other_codes_2_ = s16[384,128]{1,0:T(8,128)(2,1)S(1)} collective-permute-done((s16[384,128]{1,0:T(8,128)(2,1)S(1)}, s16[384,128]{1,0:T(8,128)(2,1)S(1)}, u32[]{:S(2)}, u32[]{:S(2)}) %collective-permute-start.47) | collective-permute-done | bytes 98336 | tf_op jit(solution)/shard_map/ppermute | solution.py:799
  112.7 4.1 %update.1 = (f32[4,96,864]{2,1,0:T(8,128)}, f32[4,96,864]{2,1,0:T(8,128)}, f32[4,96,864]{2,1,0:T(8,128)}, f32[4,96,864]{2,1,0:T(8,128)}, bf16[4,96,864]{2,1,0:T(...) custom-call(s16[384,128]{1,0:T(8,128)(2,1)S(1)} %collective-permute-, ...), custom_call_target="tpu_custom_call" | custom-call | tf_op jit(solution)/shard_map/update/pallas_call | solution.py:1050
  (135 shorter events, 25.7 us)
Async XLA Ops:
  9.0 6.9 %collective-permute-start.3 = (f32[8,128]{1,0:T(8,128)S(1)}, f32[8,128]{1,0:T(8,128)S(1)}, u32[]{:S(2)}, u32[]{:S(2)}) collective-permute-start(f32[8,128]{1,0:T(8,128)S(1)} %get-tuple-element.101), channel_id=1, source_target_pairs={{0,19},{1,18},{2,17},{3,16},{4,23},{5,22},{6,21},{7,20},{8,27},{9,... | collective-permute-start | bytes 12296 | tf_op jit(solution)/shard_map/ppermute | solution.py:799
  12.4 3.5 %collective-permute-start.2 = (f32[8,128]{1,0:T(8,128)S(1)}, f32[8,128]{1,0:T(8,128)S(1)}, u32[]{:S(2)}, u32[]{:S(2)}) collective-permute-start(f32[8,128]{1,0:T(8,128)S(1)} %get-tuple-element.101), channel_id=1, source_target_pairs={{0,18},{1,19},{2,16},{3,17},{4,22},{5,23},{6,20},{7,21},{8,26},{9,... | collective-permute-start | bytes 12296 | tf_op jit(solution)/shard_map/ppermute | solution.py:799
  16.2 4.9 %collective-permute-start.7 = (f32[8,128]{1,0:T(8,128)S(1)}, f32[8,128]{1,0:T(8,128)S(1)}, u32[]{:S(2)}, u32[]{:S(2)}) collective-permute-start(f32[8,128]{1,0:T(8,128)S(1)} %add_add_fusion.2), channel_id=1, source_target_pairs={{0,28},{1,29},{2,30},{3,31},{4,24},{5,25},{6,26},{7,27},{8,20},{9,... | collective-permute-start | bytes 12296 | tf_op jit(solution)/shard_map/ppermute | solution.py:799
  19.7 3.9 %collective-permute-start.6 = (f32[8,128]{1,0:T(8,128)S(1)}, f32[8,128]{1,0:T(8,128)S(1)}, u32[]{:S(2)}, u32[]{:S(2)}) collective-permute-start(f32[8,128]{1,0:T(8,128)S(1)} %add_add_fusion.2), channel_id=1, source_target_pairs={{0,24},{1,25},{2,26},{3,27},{4,28},{5,29},{6,30},{7,31},{8,16},{9,... | collective-permute-start | bytes 12296 | tf_op jit(solution)/shard_map/ppermute | solution.py:799
  19.7 3.9 %collective-permute-start.5 = (f32[8,128]{1,0:T(8,128)S(1)}, f32[8,128]{1,0:T(8,128)S(1)}, u32[]{:S(2)}, u32[]{:S(2)}) collective-permute-start(f32[8,128]{1,0:T(8,128)S(1)} %add_add_fusion.2), channel_id=1, source_target_pairs={{0,20},{1,21},{2,22},{3,23},{4,16},{5,17},{6,18},{7,19},{8,28},{9,... | collective-permute-start | bytes 12296 | tf_op jit(solution)/shard_map/ppermute | solution.py:799
  32.0 4.0 %collective-permute-start.11 = (f32[8,128]{1,0:T(8,128)S(1)}, f32[8,128]{1,0:T(8,128)S(1)}, u32[]{:S(2)}, u32[]{:S(2)}) collective-permute-start(f32[8,128]{1,0:T(8,128)S(1)} %get-tuple-element.111), channel_id=1, source_target_pairs={{0,19},{1,18},{2,17},{3,16},{4,23},{5,22},{6,21},{7,20},{8,27},{9,... | collective-permute-start | bytes 12296 | tf_op jit(solution)/shard_map/ppermute | solution.py:799
  37.8 4.9 %collective-permute-start.15 = (f32[8,128]{1,0:T(8,128)S(1)}, f32[8,128]{1,0:T(8,128)S(1)}, u32[]{:S(2)}, u32[]{:S(2)}) collective-permute-start(f32[8,128]{1,0:T(8,128)S(1)} %add_add_fusion.1), channel_id=1, source_target_pairs={{0,28},{1,29},{2,30},{3,31},{4,24},{5,25},{6,26},{7,27},{8,20},{9,... | collective-permute-start | bytes 12296 | tf_op jit(solution)/shard_map/ppermute | solution.py:799
  39.4 3.9 %collective-permute-start.14 = (f32[8,128]{1,0:T(8,128)S(1)}, f32[8,128]{1,0:T(8,128)S(1)}, u32[]{:S(2)}, u32[]{:S(2)}) collective-permute-start(f32[8,128]{1,0:T(8,128)S(1)} %add_add_fusion.1), channel_id=1, source_target_pairs={{0,24},{1,25},{2,26},{3,27},{4,28},{5,29},{6,30},{7,31},{8,16},{9,... | collective-permute-start | bytes 12296 | tf_op jit(solution)/shard_map/ppermute | solution.py:799
  39.8 3.6 %collective-permute-start.13 = (f32[8,128]{1,0:T(8,128)S(1)}, f32[8,128]{1,0:T(8,128)S(1)}, u32[]{:S(2)}, u32[]{:S(2)}) collective-permute-start(f32[8,128]{1,0:T(8,128)S(1)} %add_add_fusion.1), channel_id=1, source_target_pairs={{0,20},{1,21},{2,22},{3,23},{4,16},{5,17},{6,18},{7,19},{8,28},{9,... | collective-permute-start | bytes 12296 | tf_op jit(solution)/shard_map/ppermute | solution.py:799
  47.8 5.0 %collective-permute-start.20 = (f32[1,8,384]{2,1,0:T(8,128)S(1)}, f32[1,8,384]{2,1,0:T(8,128)S(1)}, u32[]{:S(2)}, u32[]{:S(2)}) collective-permute-start(f32[1,8,384]{2,1,0:T(8,128)S(1)} %assemble.1), channel_id=1, source_target_pairs={{0,28},{1,29},{2,30},{3,31},{4,24},{5,25},{6,26},{7,27},{8,20},{9,... | collective-permute-start | bytes 36872 | tf_op jit(solution)/shard_map/ppermute | solution.py:799
  50.1 4.1 %collective-permute-start.19 = (f32[1,8,384]{2,1,0:T(8,128)S(1)}, f32[1,8,384]{2,1,0:T(8,128)S(1)}, u32[]{:S(2)}, u32[]{:S(2)}) collective-permute-start(f32[1,8,384]{2,1,0:T(8,128)S(1)} %assemble.1), channel_id=1, source_target_pairs={{0,24},{1,25},{2,26},{3,27},{4,28},{5,29},{6,30},{7,31},{8,16},{9,... | collective-permute-start | bytes 36872 | tf_op jit(solution)/shard_map/ppermute | solution.py:799
  51.0 3.3 %collective-permute-start.18 = (f32[1,8,384]{2,1,0:T(8,128)S(1)}, f32[1,8,384]{2,1,0:T(8,128)S(1)}, u32[]{:S(2)}, u32[]{:S(2)}) collective-permute-start(f32[1,8,384]{2,1,0:T(8,128)S(1)} %assemble.1), channel_id=1, source_target_pairs={{0,20},{1,21},{2,22},{3,23},{4,16},{5,17},{6,18},{7,19},{8,28},{9,... | collective-permute-start | bytes 36872 | tf_op jit(solution)/shard_map/ppermute | solution.py:799
  54.2 4.8 %collective-permute-start.24 = (f32[4,8,384]{2,1,0:T(8,128)S(1)}, f32[4,8,384]{2,1,0:T(8,128)S(1)}, u32[]{:S(2)}, u32[]{:S(2)}) collective-permute-start(f32[4,8,384]{2,1,0:T(8,128)S(1)} %stack.1), channel_id=1, source_target_pairs={{0,19},{1,18},{2,17},{3,16},{4,23},{5,22},{6,21},{7,20},{8,27},{9,... | collective-permute-start | bytes 147464 | tf_op jit(solution)/shard_map/ppermute | solution.py:799
  55.5 4.7 %collective-permute-start.23 = (f32[4,8,384]{2,1,0:T(8,128)S(1)}, f32[4,8,384]{2,1,0:T(8,128)S(1)}, u32[]{:S(2)}, u32[]{:S(2)}) collective-permute-start(f32[4,8,384]{2,1,0:T(8,128)S(1)} %stack.1), channel_id=1, source_target_pairs={{0,18},{1,19},{2,16},{3,17},{4,22},{5,23},{6,20},{7,21},{8,26},{9,... | collective-permute-start | bytes 147464 | tf_op jit(solution)/shard_map/ppermute | solution.py:799
  56.0 4.2 %collective-permute-start.22 = (f32[4,8,384]{2,1,0:T(8,128)S(1)}, f32[4,8,384]{2,1,0:T(8,128)S(1)}, u32[]{:S(2)}, u32[]{:S(2)}) collective-permute-start(f32[4,8,384]{2,1,0:T(8,128)S(1)} %stack.1), channel_id=1, source_target_pairs={{0,17},{1,16},{2,19},{3,18},{4,21},{5,20},{6,23},{7,22},{8,25},{9,... | collective-permute-start | bytes 147464 | tf_op jit(solution)/shard_map/ppermute | solution.py:799
  65.2 5.3 %collective-permute-start.28 = (f32[8,128]{1,0:T(8,128)S(1)}, f32[8,128]{1,0:T(8,128)S(1)}, u32[]{:S(2)}, u32[]{:S(2)}) collective-permute-start(f32[8,128]{1,0:T(8,128)S(1)} %get-tuple-element.122), channel_id=1, source_target_pairs={{0,19},{1,18},{2,17},{3,16},{4,23},{5,22},{6,21},{7,20},{8,27},{9,... | collective-permute-start | bytes 12296 | tf_op jit(solution)/shard_map/ppermute | solution.py:799
  67.0 3.5 %collective-permute-start.27 = (f32[8,128]{1,0:T(8,128)S(1)}, f32[8,128]{1,0:T(8,128)S(1)}, u32[]{:S(2)}, u32[]{:S(2)}) collective-permute-start(f32[8,128]{1,0:T(8,128)S(1)} %get-tuple-element.122), channel_id=1, source_target_pairs={{0,18},{1,19},{2,16},{3,17},{4,22},{5,23},{6,20},{7,21},{8,26},{9,... | collective-permute-start | bytes 12296 | tf_op jit(solution)/shard_map/ppermute | solution.py:799
  70.6 6.4 %collective-permute-start.32 = (f32[8,128]{1,0:T(8,128)S(1)}, f32[8,128]{1,0:T(8,128)S(1)}, u32[]{:S(2)}, u32[]{:S(2)}) collective-permute-start(f32[8,128]{1,0:T(8,128)S(1)} %add_add_fusion), channel_id=1, source_target_pairs={{0,28},{1,29},{2,30},{3,31},{4,24},{5,25},{6,26},{7,27},{8,20},{9,... | collective-permute-start | bytes 12296 | tf_op jit(solution)/shard_map/ppermute | solution.py:799
  72.1 4.9 %collective-permute-start.31 = (f32[8,128]{1,0:T(8,128)S(1)}, f32[8,128]{1,0:T(8,128)S(1)}, u32[]{:S(2)}, u32[]{:S(2)}) collective-permute-start(f32[8,128]{1,0:T(8,128)S(1)} %add_add_fusion), channel_id=1, source_target_pairs={{0,24},{1,25},{2,26},{3,27},{4,28},{5,29},{6,30},{7,31},{8,16},{9,... | collective-permute-start | bytes 12296 | tf_op jit(solution)/shard_map/ppermute | solution.py:799
  72.7 4.2 %collective-permute-start.30 = (f32[8,128]{1,0:T(8,128)S(1)}, f32[8,128]{1,0:T(8,128)S(1)}, u32[]{:S(2)}, u32[]{:S(2)}) collective-permute-start(f32[8,128]{1,0:T(8,128)S(1)} %add_add_fusion), channel_id=1, source_target_pairs={{0,20},{1,21},{2,22},{3,23},{4,16},{5,17},{6,18},{7,19},{8,28},{9,... | collective-permute-start | bytes 12296 | tf_op jit(solution)/shard_map/ppermute | solution.py:799
  82.6 8.3 %collective-permute-start.35 = (s16[352,128]{1,0:T(8,128)(2,1)S(1)}, s16[352,128]{1,0:T(8,128)(2,1)S(1)}, u32[]{:S(2)}, u32[]{:S(2)}) collective-permute-start(s16[352,128]{1,0:T(8,128)(2,1)S(1)} %get-tuple-element.143), channel_id=1, source_target_pairs={{0,16},{1,17},{2,18},{3,19},{4,20},{5,21},{6,22},{7,23},{8,24},{9,... | collective-permute-start | bytes 270344 | tf_op jit(solution)/shard_map/ppermute | solution.py:799
  83.0 7.8 %collective-permute-start.36 = (s16[352,128]{1,0:T(8,128)(2,1)S(1)}, s16[352,128]{1,0:T(8,128)(2,1)S(1)}, u32[]{:S(2)}, u32[]{:S(2)}) collective-permute-start(s16[352,128]{1,0:T(8,128)(2,1)S(1)} %get-tuple-element.144), channel_id=1, source_target_pairs={{0,17},{1,16},{2,19},{3,18},{4,21},{5,20},{6,23},{7,22},{8,25},{9,... | collective-permute-start | bytes 270344 | tf_op jit(solution)/shard_map/ppermute | solution.py:799
  83.8 7.0 %collective-permute-start.37 = (s16[352,128]{1,0:T(8,128)(2,1)S(1)}, s16[352,128]{1,0:T(8,128)(2,1)S(1)}, u32[]{:S(2)}, u32[]{:S(2)}) collective-permute-start(s16[352,128]{1,0:T(8,128)(2,1)S(1)} %get-tuple-element.145), channel_id=1, source_target_pairs={{0,18},{1,19},{2,16},{3,17},{4,22},{5,23},{6,20},{7,21},{8,26},{9,... | collective-permute-start | bytes 270344 | tf_op jit(solution)/shard_map/ppermute | solution.py:799
  85.3 5.5 %collective-permute-start.38 = (s16[352,128]{1,0:T(8,128)(2,1)S(1)}, s16[352,128]{1,0:T(8,128)(2,1)S(1)}, u32[]{:S(2)}, u32[]{:S(2)}) collective-permute-start(s16[352,128]{1,0:T(8,128)(2,1)S(1)} %get-tuple-element.146), channel_id=1, source_target_pairs={{0,19},{1,18},{2,17},{3,16},{4,23},{5,22},{6,21},{7,20},{8,27},{9,... | collective-permute-start | bytes 270344 | tf_op jit(solution)/shard_map/ppermute | solution.py:799
  91.0 6.7 %collective-permute-start.42 = (s16[384,128]{1,0:T(8,128)(2,1)S(1)}, s16[384,128]{1,0:T(8,128)(2,1)S(1)}, u32[]{:S(2)}, u32[]{:S(2)}) collective-permute-start(s16[384,128]{1,0:T(8,128)(2,1)S(1)} %combine.1), channel_id=1, source_target_pairs={{0,28},{1,29},{2,30},{3,31},{4,24},{5,25},{6,26},{7,27},{8,20},{9,... | collective-permute-start | bytes 294920 | tf_op jit(solution)/shard_map/ppermute | solution.py:799
  92.7 9.7 %collective-permute-start.41 = (s16[384,128]{1,0:T(8,128)(2,1)S(1)}, s16[384,128]{1,0:T(8,128)(2,1)S(1)}, u32[]{:S(2)}, u32[]{:S(2)}) collective-permute-start(s16[384,128]{1,0:T(8,128)(2,1)S(1)} %combine.1), channel_id=1, source_target_pairs={{0,24},{1,25},{2,26},{3,27},{4,28},{5,29},{6,30},{7,31},{8,16},{9,... | collective-permute-start | bytes 294920 | tf_op jit(solution)/shard_map/ppermute | solution.py:799
  93.1 9.4 %collective-permute-start.40 = (s16[384,128]{1,0:T(8,128)(2,1)S(1)}, s16[384,128]{1,0:T(8,128)(2,1)S(1)}, u32[]{:S(2)}, u32[]{:S(2)}) collective-permute-start(s16[384,128]{1,0:T(8,128)(2,1)S(1)} %combine.1), channel_id=1, source_target_pairs={{0,20},{1,21},{2,22},{3,23},{4,16},{5,17},{6,18},{7,19},{8,28},{9,... | collective-permute-start | bytes 294920 | tf_op jit(solution)/shard_map/ppermute | solution.py:799
  95.1 7.3 %collective-permute-start.39 = (s16[384,128]{1,0:T(8,128)(2,1)S(1)}, s16[384,128]{1,0:T(8,128)(2,1)S(1)}, u32[]{:S(2)}, u32[]{:S(2)}) collective-permute-start(s16[384,128]{1,0:T(8,128)(2,1)S(1)} %combine.1), channel_id=1, source_target_pairs={{0,16},{1,17},{2,18},{3,19},{4,20},{5,21},{6,22},{7,23},{8,24},{9,... | collective-permute-start | bytes 294920 | tf_op jit(solution)/shard_map/ppermute | solution.py:799
  102.6 5.9 %collective-permute-start.49 = (s16[384,128]{1,0:T(8,128)(2,1)S(1)}, s16[384,128]{1,0:T(8,128)(2,1)S(1)}, u32[]{:S(2)}, u32[]{:S(2)}) collective-permute-start(s16[384,128]{1,0:T(8,128)(2,1)S(1)} %recode.1), channel_id=1, source_target_pairs={{0,19},{1,18},{2,17},{3,16},{4,23},{5,22},{6,21},{7,20},{8,27},{9,... | collective-permute-start | bytes 294920 | tf_op jit(solution)/shard_map/ppermute | solution.py:799
  104.4 6.3 %collective-permute-start.47 = (s16[384,128]{1,0:T(8,128)(2,1)S(1)}, s16[384,128]{1,0:T(8,128)(2,1)S(1)}, u32[]{:S(2)}, u32[]{:S(2)}) collective-permute-start(s16[384,128]{1,0:T(8,128)(2,1)S(1)} %recode.1), channel_id=1, source_target_pairs={{0,18},{1,19},{2,16},{3,17},{4,22},{5,23},{6,20},{7,21},{8,26},{9,... | collective-permute-start | bytes 294920 | tf_op jit(solution)/shard_map/ppermute | solution.py:799
  105.0 5.9 %collective-permute-start.45 = (s16[384,128]{1,0:T(8,128)(2,1)S(1)}, s16[384,128]{1,0:T(8,128)(2,1)S(1)}, u32[]{:S(2)}, u32[]{:S(2)}) collective-permute-start(s16[384,128]{1,0:T(8,128)(2,1)S(1)} %recode.1), channel_id=1, source_target_pairs={{0,17},{1,16},{2,19},{3,18},{4,21},{5,20},{6,23},{7,22},{8,25},{9,... | collective-permute-start | bytes 294920 | tf_op jit(solution)/shard_map/ppermute | solution.py:799
  105.6 5.6 %collective-permute-start.43 = (s16[384,128]{1,0:T(8,128)(2,1)S(1)}, s16[384,128]{1,0:T(8,128)(2,1)S(1)}, u32[]{:S(2)}, u32[]{:S(2)}) collective-permute-start(s16[384,128]{1,0:T(8,128)(2,1)S(1)} %recode.1), channel_id=1, source_target_pairs={{0,16},{1,17},{2,18},{3,19},{4,20},{5,21},{6,22},{7,23},{8,24},{9,... | collective-permute-start | bytes 294920 | tf_op jit(solution)/shard_map/ppermute | solution.py:799
  (41 other events, 446.7 us)

commit v2 on v1

--- a/solution.py
+++ b/solution.py
@@ -45,7 +45,7 @@
 STEM_ROWS = 80
 CODE_TOP = 32000.0
 FRAME = (SIDE + 2, ACROSS + 2, TILE)
-PARAMS = pltpu.CompilerParams(vmem_limit_bytes=24 * 1024 * 1024)
+PARAMS = pltpu.CompilerParams(vmem_limit_bytes=14 * 1024 * 1024)
 
 
 def dot(a, b):
@@ -281,7 +281,7 @@
 
 def second_kernel(
     cell_count, first_s, first_t, recv_ref, norm_s, norm_t, ws_ref, wt_ref,
-    second_s, second_t, frame_s, bent_ref, msg_ref,
+    second_s, second_t, frame_s, bent_ref, plain_ref, msg_ref,
     frame_t, terms_s, terms_t,
 ):
     received = total_of(recv_ref)
@@ -309,6 +309,8 @@
                 target[chunk_rows(step), lanes] = out
                 sums[2 * k] += eight(out)
                 sums[2 * k + 1] += eight(out * out)
+    for k in range(4):
+        plain_ref[k] = sums[2 * k]
     spread_sums(msg_ref, sums)
 
 
@@ -340,27 +342,43 @@
     return moved - jnp.log(total)
 
 
-def pooled_low(ratio_ref, sums, stem_sums):
-    alpha = alpha_rows(ratio_ref)
+def facts_kernel(ratio_ref, labels_ref, labelled_ref, order_ref, facts_ref):
+    dp_index = lax.axis_index("dp")
+    facts_ref[0] = alpha_rows(ratio_ref)
+    lane = lax.broadcasted_iota(jnp.int32, (2 * IMAGES, LANE), 1)
+    row = lax.broadcasted_iota(jnp.int32, (2 * IMAGES, LANE), 0)
+    info = jnp.zeros((2 * IMAGES, LANE), F32)
+    for k in range(IMAGES):
+        facts = (
+            alpha_of(ratio_ref, k),
+            labels_ref[k].astype(F32),
+            labelled_ref[k].astype(F32),
+            order_ref[dp_index * IMAGES + k].astype(F32),
+        )
+        for place, fact in enumerate(facts):
+            info = jnp.where((row == k) & (lane == 32 + place), fact, info)
+    facts_ref[1] = info
+
+
+def pooled_low(alpha, sums, stem_sums):
     total = alpha * both_halves(sums[0]) + (1.0 - alpha) * both_halves(sums[1])
     return ((total + stem_sums) / CELLS).astype(BF16)
 
 
 def teacher_kernel(
-    cell_count, ratio_ref, second_ref, recv_ref, norm, head_ref, stem_sum_ref,
+    cell_count, facts_ref, second_ref, recv_ref, norm, head_ref, stem_sum_ref, image_sum_ref,
     prob_ref,
     terms,
 ):
     norm_rows(total_of(recv_ref), norm, terms, 4, 1, cell_count)
-    plain, curved = [0.0] * 2, [0.0] * 2
+    plain, curved = [image_sum_ref[2 + b] for b in range(2)], [0.0] * 2
     for block in range(ALL // BLOCK):
         for b in range(2):
             values = second_ref[block * BLOCK : (block + 1) * BLOCK, b * LANE : (b + 1) * LANE]
             half = values * term(terms, b, 0) + term(terms, b, 1)
-            plain[b] += eight(values)
             curved[b] += eight(half * jnp.tanh(half))
     sums = [plain[b] * term(terms, b, 0) + (CELLS // 2) * term(terms, b, 1) + curved[b] for b in range(2)]
-    low = pooled_low(ratio_ref, sums, stem_sum_ref[1])
+    low = pooled_low(facts_ref[0], sums, stem_sum_ref[1])
     logits = dot_lanes(low, head_rows(head_ref))
     valid = class_lanes(2 * IMAGES)
     first_rows = lax.broadcasted_iota(jnp.int32, (2 * IMAGES, LANE), 0) < IMAGES
@@ -369,13 +387,13 @@
 
 
 def student_kernel(
-    cell_count, ratio_ref, labels_ref, labelled_ref, order_ref,
-    second_ref, recv_ref, norm, head_ref, stem_sum_ref,
+    cell_count, facts_ref, second_ref, recv_ref, norm, head_ref, stem_sum_ref, image_sum_ref,
     msg_ref, bent_ref,
     terms,
 ):
     norm_rows(total_of(recv_ref), norm, terms, 0, 1, cell_count)
-    plain, curved, bent, bent_values = ([0.0] * 2 for _ in range(4))
+    plain = [image_sum_ref[b] for b in range(2)]
+    curved, bent, bent_values = ([0.0] * 2 for _ in range(3))
     for block in range(ALL // BLOCK):
         for b in range(2):
             values = second_ref[block * BLOCK : (block + 1) * BLOCK, b * LANE : (b + 1) * LANE]
@@ -384,7 +402,6 @@
             product = half * tanh
             slope = slope_rest(half, tanh, product)
             bent_ref[block * BLOCK : (block + 1) * BLOCK, b * LANE : (b + 1) * LANE] = slope
-            plain[b] += eight(values)
             curved[b] += eight(product)
             bent[b] += eight(slope)
             bent_values[b] += eight(slope * values)
@@ -395,22 +412,11 @@
     sums += [
         term(terms, b, 2) * (0.5 * (plain[b] + bent_values[b])) + term(terms, b, 3) * slopes[b] for b in range(2)
     ]
-    dp_index = lax.axis_index("dp")
-    low = pooled_low(ratio_ref, sums, stem_sum_ref[0])
+    low = pooled_low(facts_ref[0], sums, stem_sum_ref[0])
     logits = dot_lanes(low, head_rows(head_ref))
     rows = 2 * IMAGES
-    info = jnp.where(class_lanes(rows), logits, 0.0)
-    lane = lax.broadcasted_iota(jnp.int32, (rows, LANE), 1)
+    info = jnp.where(class_lanes(rows), logits, facts_ref[1])
     row = lax.broadcasted_iota(jnp.int32, (rows, LANE), 0)
-    for k in range(IMAGES):
-        facts = (
-            alpha_of(ratio_ref, k),
-            labels_ref[k].astype(F32),
-            labelled_ref[k].astype(F32),
-            order_ref[dp_index * IMAGES + k].astype(F32),
-        )
-        for place, fact in enumerate(facts):
-            info = jnp.where((row == k) & (lane == 32 + place), fact, info)
     for b in range(2):
         msg_ref[:, b * LANE : (b + 1) * LANE] = jnp.where(
             row < IMAGES, both_halves(sums[2 + b]), both_halves(sums[4 + b])
@@ -586,16 +592,21 @@
         ref[GRAD_ROWS : GRAD_ROWS + 24, :] = small_ref[...]
         ref[GRAD_ROWS + 24 :, :] = sums
     means = sums / cell_count
+    linears, offsets = [], []
+    for b in range(2):
+        mean, slant = means[2 * b : 2 * b + 1, :], means[2 * b + 1 : 2 * b + 2, :]
+        linears.append(-term(terms1, b, 4) * slant * term(terms1, b, 2))
+        offsets.append(-term(terms1, b, 4) * (mean + slant * term(terms1, b, 3)))
     for b in range(2):
         clear_frame(frame_ref.at[b])
     for step in range(STEPS):
         parts = []
         for b in range(2):
             lanes = slice(b * LANE, (b + 1) * LANE)
-            normal = first_ref[chunk_rows(step), lanes] * term(terms1, b, 2) + term(terms1, b, 3)
-            parts.append(term(terms1, b, 4) * (
-                du_ref[chunk_rows(step), lanes] - means[2 * b : 2 * b + 1, :] - normal * means[2 * b + 1 : 2 * b + 2, :]
-            ))
+            parts.append(
+                du_ref[chunk_rows(step), lanes] * term(terms1, b, 4)
+                + (first_ref[chunk_rows(step), lanes] * linears[b] + offsets[b])
+            )
         pair = jnp.concatenate(parts, axis=1)
         for b in range(2):
             frame_line(frame_ref.at[b], step * DEEP, parts[b])
@@ -795,6 +806,10 @@
 
 
 def to_partner(values, difference):
+    return lax.ppermute(values, "dp", [(i, i ^ difference) for i in range(lax.axis_size("dp"))])
+
+
+def to_other_core(values, difference):
     size = lax.axis_size("dp")
     return lax.ppermute(values, ("view", "dp"), [(i, i ^ (difference + size)) for i in range(2 * size)])
 
@@ -803,10 +818,11 @@
     return (1, 3, 2) if ways == 4 else range(1, ways)
 
 
-def from_partners(values, shift, ways):
-    parts = [to_partner(values, 0)] + [None] * (ways - 1)
+def from_partners(values, shift, ways, crossing=True):
+    send = to_other_core if crossing else to_partner
+    parts = [to_other_core(values, 0) if crossing else values] + [None] * (ways - 1)
     for offset in far_last(ways):
-        parts[offset] = to_partner(values, offset << shift)
+        parts[offset] = send(values, offset << shift)
     return parts
 
 
@@ -922,42 +938,50 @@
         name="first_conv",
     )(*(pltpu.with_memory_space_constraint(v, pltpu.HBM) for v in (pixels, stem_weight, teacher_stem, conv, conv_t)))
     first_s, first_t, low, moved = (hold(v) for v in (first_s, first_t, low, moved))
-    recv1, (weight_s, weight_t, (back_weight_two, back_weight_one)) = sum_parts(
-        message, (forward_weights(conv), forward_weights(conv_t), backward_weights(conv))
-    )
-
-    second_s, second_t, hidden, bent_one, message = pl.pallas_call(
+    recv1, weight_s = sum_parts(message, forward_weights(conv))
+    known = pl.pallas_call(
+        facts_kernel,
+        in_specs=[scalars()] * 4,
+        out_specs=held(),
+        out_shape=struct((2, 8, LANE)),
+        compiler_params=PARAMS,
+        name="facts",
+    )(shake_ratio, labels, labelled, view_order)
+    recv1, weight_t, known = lax.optimization_barrier((recv1, forward_weights(conv_t), known))
+
+    second_s, second_t, hidden, bent_one, image_sums, message = pl.pallas_call(
         functools.partial(second_kernel, cell_count),
         in_specs=[held()] * 2 + [recv_spec] + [held()] * 4,
-        out_specs=[held()] * 5,
-        out_shape=[pltpu.VMEM(values_shape, F32)] * 2 + [pltpu.VMEM(frame_two, BF16), pltpu.VMEM(values_shape, F32), msg],
+        out_specs=[held()] * 6,
+        out_shape=[pltpu.VMEM(values_shape, F32)] * 2
+        + [pltpu.VMEM(frame_two, BF16), pltpu.VMEM(values_shape, F32), struct((4, 8, LANE)), msg],
         scratch_shapes=[pltpu.VMEM(frame_two, BF16), terms_scratch, terms_scratch],
         compiler_params=PARAMS,
         name="second_conv",
     )(first_s, first_t, recv1, norm_param, teacher_norm, weight_s, weight_t)
     second_s, second_t, hidden, bent_one = (hold(v) for v in (second_s, second_t, hidden, bent_one))
-    recv2, _ = sum_parts(message)
+    recv2, (back_weight_two, back_weight_one) = sum_parts(message, backward_weights(conv))
 
     prob = pl.pallas_call(
         functools.partial(teacher_kernel, cell_count),
-        in_specs=[scalars(), held(), recv_spec] + [held()] * 3,
+        in_specs=[held()] * 2 + [recv_spec] + [held()] * 4,
         out_specs=held(),
         out_shape=struct((8, LANE)),
         scratch_shapes=[terms_scratch],
         compiler_params=PARAMS,
         name="teacher_logits",
-    )(shake_ratio, second_t, recv2, teacher_norm, head_t, stem_sums)
+    )(known, second_t, recv2, teacher_norm, head_t, stem_sums, image_sums)
     other = swap_view(prob)
     facts, bent_two = pl.pallas_call(
         functools.partial(student_kernel, cell_count),
-        in_specs=[scalars()] * 4 + [held(), recv_spec] + [held()] * 3,
+        in_specs=[held()] * 2 + [recv_spec] + [held()] * 4,
         out_specs=[held()] * 2,
         out_shape=[struct((8, 3 * LANE)), pltpu.VMEM(values_shape, F32)],
         scratch_shapes=[terms_scratch],
         compiler_params=PARAMS,
         cost_estimate=pl.CostEstimate(flops=4_000_000_000, bytes_accessed=8_000_000, transcendentals=0),
         name="student_logits",
-    )(shake_ratio, labels, labelled, view_order, second_s, recv2, norm_param, head, stem_sums)
+    )(known, second_s, recv2, norm_param, head, stem_sums, image_sums)
     bent_two = hold(bent_two)
     facts, other = lax.optimization_barrier((facts, other))
     facts = pl.pallas_call(
@@ -1016,7 +1040,7 @@
         compiler_params=PARAMS,
         name="encode",
     )(keep2, recv_grad2, keep1, recv_grad1)
-    scattered = [to_partner(coded[0], 0)] + [None] * (QUARTERS - 1)
+    scattered = [coded[0]] + [None] * (QUARTERS - 1)
     for offset in far_last(QUARTERS):
         scattered[offset] = to_partner(coded[offset], offset)
     scattered = tuple(scattered)
@@ -1038,10 +1062,10 @@
     )
     for group in groups[1:]:
         codes = pl.pallas_call(recode_kernel, out_shape=code_shape, compiler_params=PARAMS, name="recode")(
-            tuple(from_partners(codes, *group))
+            tuple(from_partners(codes, *group, crossing=False))
         )
-    other_grads = tuple(from_partners(codes, *groups[0]))
-    own = tuple(swap_view(part) for part in other_grads)
+    own = tuple(from_partners(codes, *groups[0], crossing=False))
+    other_grads = tuple(swap_view(part) for part in own)
 
     conv_block = pl.BlockSpec((None, CH, WIDE), lambda i: (i, 0, 0))
     stem_block, norm_block = whole((27, CH)), norm_spec

time: 117 us -> 114 us (0.974)
  waiting for transfers between devices: 26.2 us -> 24 us
    ppermute x44 -> x41, waiting for transfers between devices: 23.7 us -> 21.8 us  [the longest x32 11.3 us: to_other_core(): lax.ppermute(values, ('view', 'dp'), [(i, i ^ difference + size) for i in...]
    pallas_call x2 -> x3, Pallas kernels: 4.16 us -> 3.35 us  [the longest x1 1.7 us: shards(): pl.pallas_call(functools.partial(student_kernel, cell_count), in_specs=[h...]
    ppermute x44 -> x41, starting transfers between devices: 42.8 us -> 43.2 us  [the longest x32 31.7 us: to_other_core(): lax.ppermute(values, ('view', 'dp'), [(i, i ^ difference + size) for i in...]
  transfers between devices with their start and end apart: 51 -> 48, of which waited for: 22 -> 21; matrix products, arithmetic and copies ran while one was open for 0% -> 0% of each run, Pallas kernels for 11% -> 11%
where the time goes in v2:
time: 114 us; the launch traced here: 113 us
  starting transfers between devices  44.5 us (39%)
  Pallas kernels  43.4 us (38%)
  waiting for transfers between devices  24 us (21%)
  between operations  1.37 us (1%)
    ppermute x32, starting transfers between devices, to_other_core(): lax.ppermute(values, ('view', 'dp'), [(i, i ^ difference + size) for i in...  31.7 us
    ppermute x9, starting transfers between devices, to_partner(): lax.ppermute(values, 'dp', [(i, i ^ difference) for i in range(lax.axis_s...  11.6 us
    ppermute x32, waiting for transfers between devices, to_other_core(): lax.ppermute(values, ('view', 'dp'), [(i, i ^ difference + size) for i in...  11.3 us
    ppermute x9, waiting for transfers between devices, to_partner(): lax.ppermute(values, 'dp', [(i, i ^ difference) for i in range(lax.axis_s...  10.5 us
    pallas_call x1, Pallas kernels, shards(): pl.pallas_call(first_kernel, in_specs=[pl.BlockSpec(memory_space=pltpu.HB...  8.3 us
    pallas_call x1, Pallas kernels, shards(): pl.pallas_call(functools.partial(second_kernel, cell_count), in_specs=[he...  8.29 us
    pallas_call x1, Pallas kernels, shards(): pl.pallas_call(functools.partial(back_second_kernel, cell_count, float(al...  4.94 us
    pallas_call x1, Pallas kernels, shards(): pl.pallas_call(back_stem_kernel, in_specs=[held()] * 4, out_specs=held(),...  4.78 us
  transfers between devices with their start and end apart: 48, of which 21 were waited for; matrix products, arithmetic and copies ran while one was open for 0% of the time, Pallas kernels for 11%

profile of v2, /device:TPU:0, one launch (start us, length us, event | category | flops | bytes accessed | tf_op | source)
XLA Modules:
  0.0 113.5 jit_solution(9229768864588519942)
XLA Ops:
  0.7 8.3 %first_conv.1 = (f32[4096,256]{1,0:T(8,128)S(1)}, f32[4096,256]{1,0:T(8,128)S(1)}, bf16[34,10,16,128]{3,2,1,0:T(8,128)(2,1)S(1)}, f32[3,288,128]{2,1,0:T(8,128)S...) custom-call(bf16[4,3,32,32]{3,2,1,0:T(8,128)(2,1)} %bitcast.44, f32[27,96]{1,0:T(8,128)} %sw.1, f32[27,96]{1,0:T(8,128)} %st.1, ...), custom_call_target="tpu_custom_call" | custom-call | tf_op jit(solution)/shard_map/first_conv/pallas_call | solution.py:923
  9.0 3.4 %collective-permute-start.3 = (f32[8,128]{1,0:T(8,128)S(1)}, f32[8,128]{1,0:T(8,128)S(1)}, u32[]{:S(2)}, u32[]{:S(2)}) collective-permute-start(f32[8,128]{1,0:T(8,128)S(1)} %get-tuple-element.111), channel_id=1, source_target_pairs={{0,19},{1,18},{2,17},{3,16},{4,23},{5,22},{6,21},{7,20},{8,27},{9,... | collective-permute-start | bytes 12296 | tf_op jit(solution)/shard_map/ppermute | solution.py:814
  13.9 1.6 %collective-permute-done.2 = f32[8,128]{1,0:T(8,128)S(1)} collective-permute-done((f32[8,128]{1,0:T(8,128)S(1)}, f32[8,128]{1,0:T(8,128)S(1)}, u32[]{:S(2)}, u32[]{:S(2)}) %collective-permute-start.2) | collective-permute-done | bytes 4128 | tf_op jit(solution)/shard_map/ppermute | solution.py:814
  16.3 3.4 %collective-permute-start.7 = (f32[8,128]{1,0:T(8,128)S(1)}, f32[8,128]{1,0:T(8,128)S(1)}, u32[]{:S(2)}, u32[]{:S(2)}) collective-permute-start(f32[8,128]{1,0:T(8,128)S(1)} %add_add_fusion.2), channel_id=1, source_target_pairs={{0,28},{1,29},{2,30},{3,31},{4,24},{5,25},{6,26},{7,27},{8,20},{9,... | collective-permute-start | bytes 12296 | tf_op jit(solution)/shard_map/ppermute | solution.py:814
  21.9 1.7 %collective-permute-done.6.recv_ref_2_.recv1_ref_2_ = f32[8,128]{1,0:T(8,128)S(1)} collective-permute-done((f32[8,128]{1,0:T(8,128)S(1)}, f32[8,128]{1,0:T(8,128)S(1)}, u32[]{:S(2)}, u32[]{:S(2)}) %collective-permute-start.6) | collective-permute-done | bytes 4128 | tf_op jit(solution)/shard_map/ppermute | solution.py:814
  23.7 8.3 %second_conv.1 = (f32[4096,256]{1,0:T(8,128)S(1)}, f32[4096,256]{1,0:T(8,128)S(1)}, bf16[2,34,10,16,128]{4,3,2,1,0:T(8,128)(2,1)S(1)}, f32[4096,256]{1,0:T(8,128...) custom-call(f32[4096,256]{1,0:T(8,128)S(1)} %get-tuple-element.109.first_s.first_ref, ...), custom_call_target="tpu_custom_call" | custom-call | tf_op jit(solution)/shard_map/second_conv/pallas_call | solution.py:952
  32.0 1.6 %collective-permute-start.11 = (f32[8,128]{1,0:T(8,128)S(1)}, f32[8,128]{1,0:T(8,128)S(1)}, u32[]{:S(2)}, u32[]{:S(2)}) collective-permute-start(f32[8,128]{1,0:T(8,128)S(1)} %get-tuple-element.124), channel_id=1, source_target_pairs={{0,19},{1,18},{2,17},{3,16},{4,23},{5,22},{6,21},{7,20},{8,27},{9,... | collective-permute-start | bytes 12296 | tf_op jit(solution)/shard_map/ppermute | solution.py:814
  33.8 1.4 %collective-permute-start.9 = (f32[8,128]{1,0:T(8,128)S(1)}, f32[8,128]{1,0:T(8,128)S(1)}, u32[]{:S(2)}, u32[]{:S(2)}) collective-permute-start(f32[8,128]{1,0:T(8,128)S(1)} %get-tuple-element.124), channel_id=1, source_target_pairs={{0,17},{1,16},{2,19},{3,18},{4,21},{5,20},{6,23},{7,22},{8,25},{9,... | collective-permute-start | bytes 12296 | tf_op jit(solution)/shard_map/ppermute | solution.py:814
  36.8 1.7 %collective-permute-start.15 = (f32[8,128]{1,0:T(8,128)S(1)}, f32[8,128]{1,0:T(8,128)S(1)}, u32[]{:S(2)}, u32[]{:S(2)}) collective-permute-start(f32[8,128]{1,0:T(8,128)S(1)} %add_add_fusion.1), channel_id=1, source_target_pairs={{0,28},{1,29},{2,30},{3,31},{4,24},{5,25},{6,26},{7,27},{8,20},{9,... | collective-permute-start | bytes 12296 | tf_op jit(solution)/shard_map/ppermute | solution.py:814
  38.7 2.2 %collective-permute-start.13 = (f32[8,128]{1,0:T(8,128)S(1)}, f32[8,128]{1,0:T(8,128)S(1)}, u32[]{:S(2)}, u32[]{:S(2)}) collective-permute-start(f32[8,128]{1,0:T(8,128)S(1)} %add_add_fusion.1), channel_id=1, source_target_pairs={{0,20},{1,21},{2,22},{3,23},{4,16},{5,17},{6,18},{7,19},{8,28},{9,... | collective-permute-start | bytes 12296 | tf_op jit(solution)/shard_map/ppermute | solution.py:814
  44.0 1.7 %student_logits.1 = (f32[8,384]{1,0:T(8,128)S(1)}, f32[4096,256]{1,0:T(8,128)S(1)}) custom-call(f32[2,8,128]{2,1,0:T(8,128)S(1)} %facts.1.facts_ref, f32[4096,256]{1,0:T(8,128)S(1)} %get-tuple-element.122.second_ref, f32[8,128]{1,0:T(8,128)S(1)} %collective-permute-done.12.recv_ref_0_.recv2_ref_0_, ...), custom_call_target="tpu_custom_call" | custom-call | flops 4000000000 | bytes 8000000 | tf_op jit(solution)/shard_map/student_logits/pallas_call | solution.py:975
  45.7 1.9 %collective-permute-start.20 = (f32[1,8,384]{2,1,0:T(8,128)S(1)}, f32[1,8,384]{2,1,0:T(8,128)S(1)}, u32[]{:S(2)}, u32[]{:S(2)}) collective-permute-start(f32[1,8,384]{2,1,0:T(8,128)S(1)} %assemble.1), channel_id=1, source_target_pairs={{0,28},{1,29},{2,30},{3,31},{4,24},{5,25},{6,26},{7,27},{8,20},{9,... | collective-permute-start | bytes 36872 | tf_op jit(solution)/shard_map/ppermute | solution.py:814
  48.4 1.2 %collective-permute-start.18 = (f32[1,8,384]{2,1,0:T(8,128)S(1)}, f32[1,8,384]{2,1,0:T(8,128)S(1)}, u32[]{:S(2)}, u32[]{:S(2)}) collective-permute-start(f32[1,8,384]{2,1,0:T(8,128)S(1)} %assemble.1), channel_id=1, source_target_pairs={{0,20},{1,21},{2,22},{3,23},{4,16},{5,17},{6,18},{7,19},{8,28},{9,... | collective-permute-start | bytes 36872 | tf_op jit(solution)/shard_map/ppermute | solution.py:814
  51.6 2.3 %collective-permute-start.24 = (f32[4,8,384]{2,1,0:T(8,128)S(1)}, f32[4,8,384]{2,1,0:T(8,128)S(1)}, u32[]{:S(2)}, u32[]{:S(2)}) collective-permute-start(f32[4,8,384]{2,1,0:T(8,128)S(1)} %stack.1), channel_id=1, source_target_pairs={{0,19},{1,18},{2,17},{3,16},{4,23},{5,22},{6,21},{7,20},{8,27},{9,... | collective-permute-start | bytes 147464 | tf_op jit(solution)/shard_map/ppermute | solution.py:814
  55.0 1.3 %collective-permute-done.24.recv3_ref_3_ = f32[4,8,384]{2,1,0:T(8,128)S(1)} collective-permute-done((f32[4,8,384]{2,1,0:T(8,128)S(1)}, f32[4,8,384]{2,1,0:T(8,128)S(1)}, u32[]{:S(2)}, u32[]{:S(2)}) %collective-permute-start.24) | collective-permute-done | bytes 49184 | tf_op jit(solution)/shard_map/ppermute | solution.py:814
  58.2 4.9 %back_second.1 = (f32[4096,256]{1,0:T(8,128)S(1)}, bf16[2,34,10,16,128]{4,3,2,1,0:T(8,128)(2,1)S(1)}, f32[8,128]{1,0:T(8,128)S(1)}, f32[24,128]{1,0:T(8,128)S(1)}, f32[8,128]{1,0:T(8,128)S(1)}) custom-call(f32[4096,256]{1,0:T(8,128)S(1)} %get-tuple-element.122.second_ref, f32[4096,256]{1,0:T(8,128)S(1)} %get-tuple-element.109.first_s.first_ref, ...), custom_call_target="tpu_custom_call" | custom-call | tf_op jit(solution)/shard_map/back_second/pallas_call | solution.py:992
  63.1 1.4 %collective-permute-start.28 = (f32[8,128]{1,0:T(8,128)S(1)}, f32[8,128]{1,0:T(8,128)S(1)}, u32[]{:S(2)}, u32[]{:S(2)}) collective-permute-start(f32[8,128]{1,0:T(8,128)S(1)} %get-tuple-element.142), channel_id=1, source_target_pairs={{0,19},{1,18},{2,17},{3,16},{4,23},{5,22},{6,21},{7,20},{8,27},{9,... | collective-permute-start | bytes 12296 | tf_op jit(solution)/shard_map/ppermute | solution.py:814
  66.5 1.9 %second_weight.2 = f32[672,128]{1,0:T(8,128)S(1)} custom-call(bf16[2,34,10,16,128]{4,3,2,1,0:T(8,128)(2,1)S(1)} %get-tuple-element.143.frame_ref, bf16[2,34,10,16,128]{4,3,2,1,0:T(8,128)(2,1)S(1)} %get-tuple-element.144.dy_ref), custom_call_target="tpu_custom_call" | custom-call | flops 4000000000 | bytes 8000000 | tf_op jit(solution)/shard_map/second_weight/pallas_call | solution.py:1008
  68.5 1.6 %collective-permute-start.32 = (f32[8,128]{1,0:T(8,128)S(1)}, f32[8,128]{1,0:T(8,128)S(1)}, u32[]{:S(2)}, u32[]{:S(2)}) collective-permute-start(f32[8,128]{1,0:T(8,128)S(1)} %add_add_fusion), channel_id=1, source_target_pairs={{0,28},{1,29},{2,30},{3,31},{4,24},{5,25},{6,26},{7,27},{8,20},{9,... | collective-permute-start | bytes 12296 | tf_op jit(solution)/shard_map/ppermute | solution.py:814
  70.9 1.4 %collective-permute-start.30 = (f32[8,128]{1,0:T(8,128)S(1)}, f32[8,128]{1,0:T(8,128)S(1)}, u32[]{:S(2)}, u32[]{:S(2)}) collective-permute-start(f32[8,128]{1,0:T(8,128)S(1)} %add_add_fusion), channel_id=1, source_target_pairs={{0,20},{1,21},{2,22},{3,23},{4,16},{5,17},{6,18},{7,19},{8,28},{9,... | collective-permute-start | bytes 12296 | tf_op jit(solution)/shard_map/ppermute | solution.py:814
  72.9 1.9 %second_weight.3.keep2 = f32[672,128]{1,0:T(8,128)S(1)} custom-call(bf16[2,34,10,16,128]{4,3,2,1,0:T(8,128)(2,1)S(1)} %get-tuple-element.143.frame_ref, bf16[2,34,10,16,128]{4,3,2,1,0:T(8,128)(2,1)S(1)} %get-tuple-element.144.dy_ref), custom_call_target="tpu_custom_call" | custom-call | flops 4000000000 | bytes 8000000 | tf_op jit(solution)/shard_map/second_weight/pallas_call | solution.py:1008
  74.8 3.6 %back_weight.1 = (bf16[2,34,10,16,128]{4,3,2,1,0:T(8,128)(2,1)S(1)}, f32[704,128]{1,0:T(8,128)S(1)}, f32[704,128]{1,0:T(8,128)S(1)}) custom-call(f32[4096,256]{1,0:T(8,128)S(1)} %get-tuple-element.140.du_ref, f32[4096,256]{1,0:T(8,128)S(1)} %get-tuple-element.109.first_s.first_ref, bf16[34,10,16,128]{3,2,1,0:T(8,128)(2,1)S(1)} %get-tuple-element.141.low_ref, ...), custom_call_target="tpu_custom_call" | custom-call | flops 8000000000 | bytes 16000000 | tf_op jit(solution)/shard_map/back_weight/pallas_call | solution.py:1024
  79.0 1.3 %collective-permute-done.34.recv1.other_facts = f32[704,128]{1,0:T(8,128)S(1)} collective-permute-done((f32[704,128]{1,0:T(8,128)S(1)}, f32[704,128]{1,0:T(8,128)S(1)}, u32[]{:S(2)}, u32[]{:S(2)}) %collective-permute-start.34) | collective-permute-done | bytes 360480 | tf_op jit(solution)/shard_map/ppermute | solution.py:866
  81.5 1.6 %collective-permute-start.36 = (s16[352,128]{1,0:T(8,128)(2,1)S(1)}, s16[352,128]{1,0:T(8,128)(2,1)S(1)}, u32[]{:S(2)}, u32[]{:S(2)}) collective-permute-start(s16[352,128]{1,0:T(8,128)(2,1)S(1)} %get-tuple-element.165), channel_id=1, source_target_pairs={{0,2},{1,3},{2,0},{3,1},{4,6},{5,7},{6,4},{7,5},{8,10},{9,11},{10,... | collective-permute-start | bytes 270344 | tf_op jit(solution)/shard_map/ppermute | solution.py:809
  84.1 4.8 %back_stem.1.stem_ref = f32[27,128]{1,0:T(8,128)S(1)} custom-call(bf16[2,34,10,16,128]{4,3,2,1,0:T(8,128)(2,1)S(1)} %get-tuple-element.155.frame_ref, f32[3,288,128]{2,1,0:T(8,128)S(1)} %get-tuple-element.156.moved_ref, f32[8,128]{1,0:T(8,128)S(1)} %get-tuple-element.157.dmix_ref, bf16[2,768,256]{2,1,0:T(8,128)(2,1)S(1)} %get-tuple-element.158.w_ref), custom_call_target="tpu_custom_call" | custom-call | flops 8000000000 | bytes 16000000 | tf_op jit(solution)/shard_map/back_stem/pallas_call | solution.py:1048
  89.1 1.9 %collective-permute-start.40 = (s16[384,128]{1,0:T(8,128)(2,1)S(1)}, s16[384,128]{1,0:T(8,128)(2,1)S(1)}, u32[]{:S(2)}, u32[]{:S(2)}) collective-permute-start(s16[384,128]{1,0:T(8,128)(2,1)S(1)} %combine.1.recv_refs_0_), channel_id=1, source_target_pairs={{0,12},{1,13},{2,14},{3,15},{4,8},{5,9},{6,10},{7,11},{8,4},{9,5},... | collective-permute-start | bytes 294920 | tf_op jit(solution)/shard_map/ppermute | solution.py:809
  91.4 2.1 %collective-permute-start.38 = (s16[384,128]{1,0:T(8,128)(2,1)S(1)}, s16[384,128]{1,0:T(8,128)(2,1)S(1)}, u32[]{:S(2)}, u32[]{:S(2)}) collective-permute-start(s16[384,128]{1,0:T(8,128)(2,1)S(1)} %combine.1.recv_refs_0_), channel_id=1, source_target_pairs={{0,4},{1,5},{2,6},{3,7},{4,0},{5,1},{6,2},{7,3},{8,12},{9,13},{10,... | collective-permute-start | bytes 294920 | tf_op jit(solution)/shard_map/ppermute | solution.py:809
  93.6 3.1 %collective-permute-done.40.recv_refs_3_ = s16[384,128]{1,0:T(8,128)(2,1)S(1)} collective-permute-done((s16[384,128]{1,0:T(8,128)(2,1)S(1)}, s16[384,128]{1,0:T(8,128)(2,1)S(1)}, u32[]{:S(2)}, u32[]{:S(2)}) %collective-permute-start.40) | collective-permute-done | bytes 98336 | tf_op jit(solution)/shard_map/ppermute | solution.py:809
  96.7 3.7 %collective-permute-done.39.recv_refs_2_ = s16[384,128]{1,0:T(8,128)(2,1)S(1)} collective-permute-done((s16[384,128]{1,0:T(8,128)(2,1)S(1)}, s16[384,128]{1,0:T(8,128)(2,1)S(1)}, u32[]{:S(2)}, u32[]{:S(2)}) %collective-permute-start.39) | collective-permute-done | bytes 98336 | tf_op jit(solution)/shard_map/ppermute | solution.py:809
  100.5 2.1 %collective-permute-start.43 = (s16[384,128]{1,0:T(8,128)(2,1)S(1)}, s16[384,128]{1,0:T(8,128)(2,1)S(1)}, u32[]{:S(2)}, u32[]{:S(2)}) collective-permute-start(s16[384,128]{1,0:T(8,128)(2,1)S(1)} %recode.1.own_codes_0_), channel_id=1, source_target_pairs={{0,3},{1,2},{2,1},{3,0},{4,7},{5,6},{6,5},{7,4},{8,11},{9,10},{10,... | collective-permute-start | bytes 294920 | tf_op jit(solution)/shard_map/ppermute | solution.py:809
  104.1 2.8 %collective-permute-done.43.own_codes_3_ = s16[384,128]{1,0:T(8,128)(2,1)S(1)} collective-permute-done((s16[384,128]{1,0:T(8,128)(2,1)S(1)}, s16[384,128]{1,0:T(8,128)(2,1)S(1)}, u32[]{:S(2)}, u32[]{:S(2)}) %collective-permute-start.43) | collective-permute-done | bytes 98336 | tf_op jit(solution)/shard_map/ppermute | solution.py:809
  109.1 4.1 %update.1 = (f32[4,96,864]{2,1,0:T(8,128)}, f32[4,96,864]{2,1,0:T(8,128)}, f32[4,96,864]{2,1,0:T(8,128)}, f32[4,96,864]{2,1,0:T(8,128)}, bf16[4,96,864]{2,1,0:T(...) custom-call(s16[384,128]{1,0:T(8,128)(2,1)S(1)} %recode.1.own_codes_, ...), custom_call_target="tpu_custom_call" | custom-call | tf_op jit(solution)/shard_map/update/pallas_call | solution.py:1074
  (126 shorter events, 25.9 us)
Async XLA Ops:
  9.0 4.9 %collective-permute-start.3 = (f32[8,128]{1,0:T(8,128)S(1)}, f32[8,128]{1,0:T(8,128)S(1)}, u32[]{:S(2)}, u32[]{:S(2)}) collective-permute-start(f32[8,128]{1,0:T(8,128)S(1)} %get-tuple-element.111), channel_id=1, source_target_pairs={{0,19},{1,18},{2,17},{3,16},{4,23},{5,22},{6,21},{7,20},{8,27},{9,... | collective-permute-start | bytes 12296 | tf_op jit(solution)/shard_map/ppermute | solution.py:814
  16.3 5.6 %collective-permute-start.7 = (f32[8,128]{1,0:T(8,128)S(1)}, f32[8,128]{1,0:T(8,128)S(1)}, u32[]{:S(2)}, u32[]{:S(2)}) collective-permute-start(f32[8,128]{1,0:T(8,128)S(1)} %add_add_fusion.2), channel_id=1, source_target_pairs={{0,28},{1,29},{2,30},{3,31},{4,24},{5,25},{6,26},{7,27},{8,20},{9,... | collective-permute-start | bytes 12296 | tf_op jit(solution)/shard_map/ppermute | solution.py:814
  19.7 4.0 %collective-permute-start.6 = (f32[8,128]{1,0:T(8,128)S(1)}, f32[8,128]{1,0:T(8,128)S(1)}, u32[]{:S(2)}, u32[]{:S(2)}) collective-permute-start(f32[8,128]{1,0:T(8,128)S(1)} %add_add_fusion.2), channel_id=1, source_target_pairs={{0,24},{1,25},{2,26},{3,27},{4,28},{5,29},{6,30},{7,31},{8,16},{9,... | collective-permute-start | bytes 12296 | tf_op jit(solution)/shard_map/ppermute | solution.py:814
  19.7 4.0 %collective-permute-start.5 = (f32[8,128]{1,0:T(8,128)S(1)}, f32[8,128]{1,0:T(8,128)S(1)}, u32[]{:S(2)}, u32[]{:S(2)}) collective-permute-start(f32[8,128]{1,0:T(8,128)S(1)} %add_add_fusion.2), channel_id=1, source_target_pairs={{0,20},{1,21},{2,22},{3,23},{4,16},{5,17},{6,18},{7,19},{8,28},{9,... | collective-permute-start | bytes 12296 | tf_op jit(solution)/shard_map/ppermute | solution.py:814
  20.3 3.3 %collective-permute-start.4 = (f32[8,128]{1,0:T(8,128)S(1)}, f32[8,128]{1,0:T(8,128)S(1)}, u32[]{:S(2)}, u32[]{:S(2)}) collective-permute-start(f32[8,128]{1,0:T(8,128)S(1)} %add_add_fusion.2), channel_id=1, source_target_pairs={{0,16},{1,17},{2,18},{3,19},{4,20},{5,21},{6,22},{7,23},{8,24},{9,... | collective-permute-start | bytes 12296 | tf_op jit(solution)/shard_map/ppermute | solution.py:814
  32.0 4.0 %collective-permute-start.11 = (f32[8,128]{1,0:T(8,128)S(1)}, f32[8,128]{1,0:T(8,128)S(1)}, u32[]{:S(2)}, u32[]{:S(2)}) collective-permute-start(f32[8,128]{1,0:T(8,128)S(1)} %get-tuple-element.124), channel_id=1, source_target_pairs={{0,19},{1,18},{2,17},{3,16},{4,23},{5,22},{6,21},{7,20},{8,27},{9,... | collective-permute-start | bytes 12296 | tf_op jit(solution)/shard_map/ppermute | solution.py:814
  36.8 4.9 %collective-permute-start.15 = (f32[8,128]{1,0:T(8,128)S(1)}, f32[8,128]{1,0:T(8,128)S(1)}, u32[]{:S(2)}, u32[]{:S(2)}) collective-permute-start(f32[8,128]{1,0:T(8,128)S(1)} %add_add_fusion.1), channel_id=1, source_target_pairs={{0,28},{1,29},{2,30},{3,31},{4,24},{5,25},{6,26},{7,27},{8,20},{9,... | collective-permute-start | bytes 12296 | tf_op jit(solution)/shard_map/ppermute | solution.py:814
  38.6 3.9 %collective-permute-start.14 = (f32[8,128]{1,0:T(8,128)S(1)}, f32[8,128]{1,0:T(8,128)S(1)}, u32[]{:S(2)}, u32[]{:S(2)}) collective-permute-start(f32[8,128]{1,0:T(8,128)S(1)} %add_add_fusion.1), channel_id=1, source_target_pairs={{0,24},{1,25},{2,26},{3,27},{4,28},{5,29},{6,30},{7,31},{8,16},{9,... | collective-permute-start | bytes 12296 | tf_op jit(solution)/shard_map/ppermute | solution.py:814
  38.7 3.8 %collective-permute-start.13 = (f32[8,128]{1,0:T(8,128)S(1)}, f32[8,128]{1,0:T(8,128)S(1)}, u32[]{:S(2)}, u32[]{:S(2)}) collective-permute-start(f32[8,128]{1,0:T(8,128)S(1)} %add_add_fusion.1), channel_id=1, source_target_pairs={{0,20},{1,21},{2,22},{3,23},{4,16},{5,17},{6,18},{7,19},{8,28},{9,... | collective-permute-start | bytes 12296 | tf_op jit(solution)/shard_map/ppermute | solution.py:814
  45.7 4.9 %collective-permute-start.20 = (f32[1,8,384]{2,1,0:T(8,128)S(1)}, f32[1,8,384]{2,1,0:T(8,128)S(1)}, u32[]{:S(2)}, u32[]{:S(2)}) collective-permute-start(f32[1,8,384]{2,1,0:T(8,128)S(1)} %assemble.1), channel_id=1, source_target_pairs={{0,28},{1,29},{2,30},{3,31},{4,24},{5,25},{6,26},{7,27},{8,20},{9,... | collective-permute-start | bytes 36872 | tf_op jit(solution)/shard_map/ppermute | solution.py:814
  47.5 4.1 %collective-permute-start.19 = (f32[1,8,384]{2,1,0:T(8,128)S(1)}, f32[1,8,384]{2,1,0:T(8,128)S(1)}, u32[]{:S(2)}, u32[]{:S(2)}) collective-permute-start(f32[1,8,384]{2,1,0:T(8,128)S(1)} %assemble.1), channel_id=1, source_target_pairs={{0,24},{1,25},{2,26},{3,27},{4,28},{5,29},{6,30},{7,31},{8,16},{9,... | collective-permute-start | bytes 36872 | tf_op jit(solution)/shard_map/ppermute | solution.py:814
  48.4 3.3 %collective-permute-start.18 = (f32[1,8,384]{2,1,0:T(8,128)S(1)}, f32[1,8,384]{2,1,0:T(8,128)S(1)}, u32[]{:S(2)}, u32[]{:S(2)}) collective-permute-start(f32[1,8,384]{2,1,0:T(8,128)S(1)} %assemble.1), channel_id=1, source_target_pairs={{0,20},{1,21},{2,22},{3,23},{4,16},{5,17},{6,18},{7,19},{8,28},{9,... | collective-permute-start | bytes 36872 | tf_op jit(solution)/shard_map/ppermute | solution.py:814
  51.6 4.7 %collective-permute-start.24 = (f32[4,8,384]{2,1,0:T(8,128)S(1)}, f32[4,8,384]{2,1,0:T(8,128)S(1)}, u32[]{:S(2)}, u32[]{:S(2)}) collective-permute-start(f32[4,8,384]{2,1,0:T(8,128)S(1)} %stack.1), channel_id=1, source_target_pairs={{0,19},{1,18},{2,17},{3,16},{4,23},{5,22},{6,21},{7,20},{8,27},{9,... | collective-permute-start | bytes 147464 | tf_op jit(solution)/shard_map/ppermute | solution.py:814
  54.0 3.5 %collective-permute-start.23 = (f32[4,8,384]{2,1,0:T(8,128)S(1)}, f32[4,8,384]{2,1,0:T(8,128)S(1)}, u32[]{:S(2)}, u32[]{:S(2)}) collective-permute-start(f32[4,8,384]{2,1,0:T(8,128)S(1)} %stack.1), channel_id=1, source_target_pairs={{0,18},{1,19},{2,16},{3,17},{4,22},{5,23},{6,20},{7,21},{8,26},{9,... | collective-permute-start | bytes 147464 | tf_op jit(solution)/shard_map/ppermute | solution.py:814
  54.4 3.8 %collective-permute-start.22 = (f32[4,8,384]{2,1,0:T(8,128)S(1)}, f32[4,8,384]{2,1,0:T(8,128)S(1)}, u32[]{:S(2)}, u32[]{:S(2)}) collective-permute-start(f32[4,8,384]{2,1,0:T(8,128)S(1)} %stack.1), channel_id=1, source_target_pairs={{0,17},{1,16},{2,19},{3,18},{4,21},{5,20},{6,23},{7,22},{8,25},{9,... | collective-permute-start | bytes 147464 | tf_op jit(solution)/shard_map/ppermute | solution.py:814
  54.7 3.5 %collective-permute-start.21 = (f32[4,8,384]{2,1,0:T(8,128)S(1)}, f32[4,8,384]{2,1,0:T(8,128)S(1)}, u32[]{:S(2)}, u32[]{:S(2)}) collective-permute-start(f32[4,8,384]{2,1,0:T(8,128)S(1)} %stack.1), channel_id=1, source_target_pairs={{0,16},{1,17},{2,18},{3,19},{4,20},{5,21},{6,22},{7,23},{8,24},{9,... | collective-permute-start | bytes 147464 | tf_op jit(solution)/shard_map/ppermute | solution.py:814
  63.1 5.3 %collective-permute-start.28 = (f32[8,128]{1,0:T(8,128)S(1)}, f32[8,128]{1,0:T(8,128)S(1)}, u32[]{:S(2)}, u32[]{:S(2)}) collective-permute-start(f32[8,128]{1,0:T(8,128)S(1)} %get-tuple-element.142), channel_id=1, source_target_pairs={{0,19},{1,18},{2,17},{3,16},{4,23},{5,22},{6,21},{7,20},{8,27},{9,... | collective-permute-start | bytes 12296 | tf_op jit(solution)/shard_map/ppermute | solution.py:814
  64.5 4.0 %collective-permute-start.27 = (f32[8,128]{1,0:T(8,128)S(1)}, f32[8,128]{1,0:T(8,128)S(1)}, u32[]{:S(2)}, u32[]{:S(2)}) collective-permute-start(f32[8,128]{1,0:T(8,128)S(1)} %get-tuple-element.142), channel_id=1, source_target_pairs={{0,18},{1,19},{2,16},{3,17},{4,22},{5,23},{6,20},{7,21},{8,26},{9,... | collective-permute-start | bytes 12296 | tf_op jit(solution)/shard_map/ppermute | solution.py:814
  65.4 3.1 %collective-permute-start.26 = (f32[8,128]{1,0:T(8,128)S(1)}, f32[8,128]{1,0:T(8,128)S(1)}, u32[]{:S(2)}, u32[]{:S(2)}) collective-permute-start(f32[8,128]{1,0:T(8,128)S(1)} %get-tuple-element.142), channel_id=1, source_target_pairs={{0,17},{1,16},{2,19},{3,18},{4,21},{5,20},{6,23},{7,22},{8,25},{9,... | collective-permute-start | bytes 12296 | tf_op jit(solution)/shard_map/ppermute | solution.py:814
  68.5 6.3 %collective-permute-start.32 = (f32[8,128]{1,0:T(8,128)S(1)}, f32[8,128]{1,0:T(8,128)S(1)}, u32[]{:S(2)}, u32[]{:S(2)}) collective-permute-start(f32[8,128]{1,0:T(8,128)S(1)} %add_add_fusion), channel_id=1, source_target_pairs={{0,28},{1,29},{2,30},{3,31},{4,24},{5,25},{6,26},{7,27},{8,20},{9,... | collective-permute-start | bytes 12296 | tf_op jit(solution)/shard_map/ppermute | solution.py:814
  70.0 4.7 %collective-permute-start.31 = (f32[8,128]{1,0:T(8,128)S(1)}, f32[8,128]{1,0:T(8,128)S(1)}, u32[]{:S(2)}, u32[]{:S(2)}) collective-permute-start(f32[8,128]{1,0:T(8,128)S(1)} %add_add_fusion), channel_id=1, source_target_pairs={{0,24},{1,25},{2,26},{3,27},{4,28},{5,29},{6,30},{7,31},{8,16},{9,... | collective-permute-start | bytes 12296 | tf_op jit(solution)/shard_map/ppermute | solution.py:814
  70.9 3.9 %collective-permute-start.30 = (f32[8,128]{1,0:T(8,128)S(1)}, f32[8,128]{1,0:T(8,128)S(1)}, u32[]{:S(2)}, u32[]{:S(2)}) collective-permute-start(f32[8,128]{1,0:T(8,128)S(1)} %add_add_fusion), channel_id=1, source_target_pairs={{0,20},{1,21},{2,22},{3,23},{4,16},{5,17},{6,18},{7,19},{8,28},{9,... | collective-permute-start | bytes 12296 | tf_op jit(solution)/shard_map/ppermute | solution.py:814
  80.5 8.4 %collective-permute-start.35 = (s16[352,128]{1,0:T(8,128)(2,1)S(1)}, s16[352,128]{1,0:T(8,128)(2,1)S(1)}, u32[]{:S(2)}, u32[]{:S(2)}) collective-permute-start(s16[352,128]{1,0:T(8,128)(2,1)S(1)} %get-tuple-element.164), channel_id=1, source_target_pairs={{0,1},{1,0},{2,3},{3,2},{4,5},{5,4},{6,7},{7,6},{8,9},{9,8},{10,11... | collective-permute-start | bytes 270344 | tf_op jit(solution)/shard_map/ppermute | solution.py:809
  81.5 7.4 %collective-permute-start.36 = (s16[352,128]{1,0:T(8,128)(2,1)S(1)}, s16[352,128]{1,0:T(8,128)(2,1)S(1)}, u32[]{:S(2)}, u32[]{:S(2)}) collective-permute-start(s16[352,128]{1,0:T(8,128)(2,1)S(1)} %get-tuple-element.165), channel_id=1, source_target_pairs={{0,2},{1,3},{2,0},{3,1},{4,6},{5,7},{6,4},{7,5},{8,10},{9,11},{10,... | collective-permute-start | bytes 270344 | tf_op jit(solution)/shard_map/ppermute | solution.py:809
  83.2 5.8 %collective-permute-start.37 = (s16[352,128]{1,0:T(8,128)(2,1)S(1)}, s16[352,128]{1,0:T(8,128)(2,1)S(1)}, u32[]{:S(2)}, u32[]{:S(2)}) collective-permute-start(s16[352,128]{1,0:T(8,128)(2,1)S(1)} %get-tuple-element.166), channel_id=1, source_target_pairs={{0,3},{1,2},{2,1},{3,0},{4,7},{5,6},{6,5},{7,4},{8,11},{9,10},{10,... | collective-permute-start | bytes 270344 | tf_op jit(solution)/shard_map/ppermute | solution.py:809
  89.1 7.6 %collective-permute-start.40 = (s16[384,128]{1,0:T(8,128)(2,1)S(1)}, s16[384,128]{1,0:T(8,128)(2,1)S(1)}, u32[]{:S(2)}, u32[]{:S(2)}) collective-permute-start(s16[384,128]{1,0:T(8,128)(2,1)S(1)} %combine.1.recv_refs_0_), channel_id=1, source_target_pairs={{0,12},{1,13},{2,14},{3,15},{4,8},{5,9},{6,10},{7,11},{8,4},{9,5},... | collective-permute-start | bytes 294920 | tf_op jit(solution)/shard_map/ppermute | solution.py:809
  90.9 9.4 %collective-permute-start.39 = (s16[384,128]{1,0:T(8,128)(2,1)S(1)}, s16[384,128]{1,0:T(8,128)(2,1)S(1)}, u32[]{:S(2)}, u32[]{:S(2)}) collective-permute-start(s16[384,128]{1,0:T(8,128)(2,1)S(1)} %combine.1.recv_refs_0_), channel_id=1, source_target_pairs={{0,8},{1,9},{2,10},{3,11},{4,12},{5,13},{6,14},{7,15},{8,0},{9,1},... | collective-permute-start | bytes 294920 | tf_op jit(solution)/shard_map/ppermute | solution.py:809
  91.4 8.9 %collective-permute-start.38 = (s16[384,128]{1,0:T(8,128)(2,1)S(1)}, s16[384,128]{1,0:T(8,128)(2,1)S(1)}, u32[]{:S(2)}, u32[]{:S(2)}) collective-permute-start(s16[384,128]{1,0:T(8,128)(2,1)S(1)} %combine.1.recv_refs_0_), channel_id=1, source_target_pairs={{0,4},{1,5},{2,6},{3,7},{4,0},{5,1},{6,2},{7,3},{8,12},{9,13},{10,... | collective-permute-start | bytes 294920 | tf_op jit(solution)/shard_map/ppermute | solution.py:809
  100.5 6.3 %collective-permute-start.43 = (s16[384,128]{1,0:T(8,128)(2,1)S(1)}, s16[384,128]{1,0:T(8,128)(2,1)S(1)}, u32[]{:S(2)}, u32[]{:S(2)}) collective-permute-start(s16[384,128]{1,0:T(8,128)(2,1)S(1)} %recode.1.own_codes_0_), channel_id=1, source_target_pairs={{0,3},{1,2},{2,1},{3,0},{4,7},{5,6},{6,5},{7,4},{8,11},{9,10},{10,... | collective-permute-start | bytes 294920 | tf_op jit(solution)/shard_map/ppermute | solution.py:809
  102.6 4.9 %collective-permute-start.42 = (s16[384,128]{1,0:T(8,128)(2,1)S(1)}, s16[384,128]{1,0:T(8,128)(2,1)S(1)}, u32[]{:S(2)}, u32[]{:S(2)}) collective-permute-start(s16[384,128]{1,0:T(8,128)(2,1)S(1)} %recode.1.own_codes_0_), channel_id=1, source_target_pairs={{0,2},{1,3},{2,0},{3,1},{4,6},{5,7},{6,4},{7,5},{8,10},{9,11},{10,... | collective-permute-start | bytes 294920 | tf_op jit(solution)/shard_map/ppermute | solution.py:809
  103.0 4.7 %collective-permute-start.41 = (s16[384,128]{1,0:T(8,128)(2,1)S(1)}, s16[384,128]{1,0:T(8,128)(2,1)S(1)}, u32[]{:S(2)}, u32[]{:S(2)}) collective-permute-start(s16[384,128]{1,0:T(8,128)(2,1)S(1)} %recode.1.own_codes_0_), channel_id=1, source_target_pairs={{0,1},{1,0},{2,3},{3,2},{4,5},{5,4},{6,7},{7,6},{8,9},{9,8},{10,11... | collective-permute-start | bytes 294920 | tf_op jit(solution)/shard_map/ppermute | solution.py:809
  104.1 4.0 %collective-permute-start.44 = (s16[384,128]{1,0:T(8,128)(2,1)S(1)}, s16[384,128]{1,0:T(8,128)(2,1)S(1)}, u32[]{:S(2)}, u32[]{:S(2)}) collective-permute-start(s16[384,128]{1,0:T(8,128)(2,1)S(1)} %recode.1.own_codes_0_), channel_id=1, source_target_pairs={{0,16},{16,0},{1,17},{17,1},{2,18},{18,2},{3,19},{19,3},{4,20},{20... | collective-permute-start | bytes 294920 | tf_op jit(solution)/shard_map/ppermute | solution.py:866
  (36 other events, 362.9 us)

commit v3 on v2

--- a/solution.py
+++ b/solution.py
@@ -618,19 +618,24 @@
     )
 
 
-def back_stem_kernel(frame_ref, moved_ref, dmix_ref, w_ref, stem_ref):
-    carry = blank_line()
-    total = 0.0
-    products = []
-    for step in range(STEPS):
-        if step % 2 == 0:
-            products = [[dot(taps(frame_ref.at[b], step + k, (0, 1)), w_ref[b]) for k in range(2)] for b in range(2)]
-        both = products[0][step % 2] + products[1][step % 2]
+def back_stem_steps(steps, frame_ref, moved_ref, dmix_ref, w_ref, carry, total):
+    for step in steps:
+        both = dot(taps(frame_ref.at[0], step, (0, 1)), w_ref[0]) + dot(taps(frame_ref.at[1], step, (0, 1)), w_ref[1])
         dstem, carry = fold_lines(both, carry)
         dstem = (dstem.reshape(CHUNK // 8, 8, LANE) + dmix_ref[...][None]).reshape(CHUNK, LANE)
         total += dot(image_taps(moved_ref, step * DEEP, DEEP), dstem.astype(BF16))
-    rows = [total[stem_row(tap) : stem_row(tap) + 3, :] for tap in range(TAPS)]
-    stem_ref[...] = jnp.concatenate(rows, axis=0)
+    return carry, total
+
+
+def back_stem_kernel(step, frame_ref, moved_ref, dmix_ref, w_ref, *refs):
+    carry, total = (blank_line(), 0.0) if step == 0 else (refs[0][...], refs[1][...])
+    carry, total = back_stem_steps((step,), frame_ref, moved_ref, dmix_ref, w_ref, carry, total)
+    if step < STEPS - 1:
+        refs[-2][...] = carry
+        refs[-1][...] = total
+    else:
+        rows = [total[stem_row(tap) : stem_row(tap) + 3, :] for tap in range(TAPS)]
+        refs[-1][...] = jnp.concatenate(rows, axis=0)
 
 
 def code(values):
@@ -708,12 +713,30 @@
     return weight_new, first_new, second_new, TEACHER_KEEP * teacher + (1.0 - TEACHER_KEEP) * weight_new
 
 
+def place_codes(codes, grads):
+    mine = lax.axis_index("dp") & (QUARTERS - 1)
+    for offset, source in enumerate(codes):
+        place = pl.multiple_of((mine ^ offset) * SHARE, 8)
+        for k in range(2):
+            grads[k, pl.ds(place, SHARE), :] = decoded(source[k * PIECE : (k + 1) * PIECE, :], SHARE)
+
+
+def square_sums(grads):
+    return sum(eight(grads[k] * grads[k]) for k in range(2))
+
+
+def decode_kernel(codes, grads_ref, stem_ref, squares_ref):
+    place_codes(codes, grads_ref)
+    stem_ref[...] = summed(codes, 2 * PIECE, 27, SIDE)
+    squares_ref[...] = square_sums(grads_ref)
+
+
 def update_kernel(
-    own_codes, other_codes, own_facts, other_facts,
+    own_ref, own_stem, own_squares, other_codes, own_facts, other_facts,
     cw, cf, cs, ct, sw, sf, ss, st, hw, hf, hs, ht, nw, nf, ns, nt,
     cw_o, cf_o, cs_o, ct_o, cb_o, sw_o, sf_o, ss_o, st_o, sb_o, hw_o, hf_o, hs_o, ht_o, hb_o,
     nw_o, nf_o, ns_o, nt_o, norm_o, cross_o, count_o, consistency_o,
-    factor_ref, own_ref, other_ref,
+    factor_ref, other_ref,
 ):
     conv = pl.program_id(0)
     view = lax.axis_index("view")
@@ -722,14 +745,8 @@
     def _():
         facts = own_facts[GRAD_ROWS:, :] + other_facts[GRAD_ROWS:, :]
         small, sums = facts[:24], facts[24:]
-        mine = lax.axis_index("dp") & (QUARTERS - 1)
-        stem = jnp.zeros((27, LANE), F32)
-        for codes, ref in ((own_codes, own_ref), (other_codes, other_ref)):
-            for offset, source in enumerate(codes):
-                place = pl.multiple_of((mine ^ offset) * SHARE, 8)
-                for k in range(2):
-                    ref[k, pl.ds(place, SHARE), :] = decoded(source[k * PIECE : (k + 1) * PIECE, :], SHARE)
-            stem += summed(codes, 2 * PIECE, 27, SIDE)
+        place_codes(other_codes, other_ref)
+        stem = own_stem[...] + summed(other_codes, 2 * PIECE, 27, SIDE)
         stem = stem[:, :CH]
         head = small[:CLASSES, :CH]
         gains = jnp.concatenate([sums[1:2], small[17:18], sums[3:4], small[19:20]], axis=0)[:, :CH]
@@ -737,11 +754,8 @@
         total = jnp.zeros((1, 1), F32)
         for part in (stem, head, gains, shifts):
             total += jnp.sum(jnp.sum(part * part, axis=1, keepdims=True), axis=0, keepdims=True)
-        for ref in (own_ref, other_ref):
-            for k in range(2):
-                values = ref[k, 0:GRAD_ROWS, :]
-                column = jnp.sum(values * values, axis=0, keepdims=True)
-                total += jnp.sum(column, axis=1, keepdims=True)
+        squares = own_squares[...] + square_sums(other_ref)
+        total += jnp.sum(jnp.sum(squares, axis=0, keepdims=True), axis=1, keepdims=True)
         norm = jnp.sqrt(total)
         factor = CLIP_LIMIT / jnp.maximum(norm, CLIP_LIMIT)
         factor_ref[...] = jnp.broadcast_to(factor, factor_ref.shape)
@@ -1033,6 +1047,21 @@
     )(du, first_s, low, recv1, recv5, norm_param, small)
     frame = hold(frame)
     recv_grad1 = swap_view(send1)
+
+    def back_stem(step, before=()):
+        going = step < STEPS - 1
+        return pl.pallas_call(
+            functools.partial(back_stem_kernel, step),
+            in_specs=[held()] * (4 + len(before)),
+            out_specs=[held()] * 2 if going else held(),
+            out_shape=[struct((LINE, LANE)), struct((STEM_ROWS, LANE))] if going else struct((27, LANE)),
+            compiler_params=PARAMS,
+            cost_estimate=pl.CostEstimate(flops=2_000_000_000, bytes_accessed=4_000_000, transcendentals=0),
+            name="back_stem",
+        )(frame, moved, dmix, back_weight_one, *before)
+
+    started = back_stem(0)
+    recv_grad1, started = lax.optimization_barrier((recv_grad1, started))
     coded = pl.pallas_call(
         encode_kernel,
         out_shape=[struct((2 * PIECE, LANE), jnp.int16)] * QUARTERS,
@@ -1045,15 +1074,9 @@
         scattered[offset] = to_partner(coded[offset], offset)
     scattered = tuple(scattered)
 
-    stem_grad = pl.pallas_call(
-        back_stem_kernel,
-        in_specs=[held()] * 4,
-        out_specs=held(),
-        out_shape=struct((27, LANE)),
-        compiler_params=PARAMS,
-        cost_estimate=pl.CostEstimate(flops=8_000_000_000, bytes_accessed=16_000_000, transcendentals=0),
-        name="back_stem",
-    )(frame, moved, dmix, back_weight_one)
+    stem_grad = started
+    for step in range(1, STEPS):
+        stem_grad = back_stem(step, tuple(stem_grad))
 
     stem_grad, scattered = lax.optimization_barrier((stem_grad, scattered))
     code_shape = struct((CODE_ROWS, LANE), jnp.int16)
@@ -1066,6 +1089,13 @@
         )
     own = tuple(from_partners(codes, *groups[0], crossing=False))
     other_grads = tuple(swap_view(part) for part in own)
+    own_parts = pl.pallas_call(
+        decode_kernel,
+        out_shape=[struct((2, GRAD_ROWS, LANE)), struct((27, LANE)), struct((8, LANE))],
+        compiler_params=PARAMS,
+        name="decode",
+    )(own)
+    own_parts, other_grads = lax.optimization_barrier((own_parts, other_grads))
 
     conv_block = pl.BlockSpec((None, CH, WIDE), lambda i: (i, 0, 0))
     stem_block, norm_block = whole((27, CH)), norm_spec
@@ -1074,17 +1104,17 @@
     outs = pl.pallas_call(
         update_kernel,
         grid=(4,),
-        in_specs=[code_spec] * 2 + [held()] * 18,
+        in_specs=[held()] * 3 + [code_spec] + [held()] * 18,
         out_specs=[conv_block] * 5 + [stem_block] * 5 + [head_spec] * 5 + [norm_block] * 4 + [whole((1, 1))] * 4,
         out_shape=[struct((4, CH, WIDE))] * 4 + [struct((4, CH, WIDE), BF16)]
         + [struct((27, CH))] * 4 + [struct((27, CH), BF16)]
         + [struct((CLASSES, CH))] * 4 + [struct((CLASSES, CH), BF16)]
         + [struct((2, 4, CH))] * 4 + [struct((1, 1))] * 4,
-        scratch_shapes=[pltpu.VMEM((8, LANE), F32), grads_scratch, grads_scratch],
+        scratch_shapes=[pltpu.VMEM((8, LANE), F32), grads_scratch],
         compiler_params=PARAMS,
         name="update",
     )(
-        own, other_grads, keep1, recv_grad1,
+        *own_parts, other_grads, keep1, recv_grad1,
         conv, conv_f, conv_s, conv_t, stem_weight, first_stem, second_stem, teacher_stem,
         head, head_f, head_s, head_t, norm_param, first_norm, second_norm, teacher_norm,
     )

time: 114 us -> 112 us (0.982)
  waiting for transfers between devices: 24 us -> 22.8 us
    ppermute x7, waiting for transfers between devices: 2.26 us -> 0.93 us  [swap_view(): return lax.ppermute(values, 'view', [(0, 1), (1, 0)])]
    pallas_call x2 -> x6, Pallas kernels: 8.92 us -> 8.77 us  [the longest x4 4.66 us: back_stem(): pl.pallas_call(functools.partial(back_stem_kernel, step), in_specs=[held(...]
where the time goes in v3:
time: 112 us
  starting transfers between devices  44.7 us (40%)
  Pallas kernels  43.2 us (39%)
  waiting for transfers between devices  22.8 us (20%)
  between operations  1.41 us (1%)
    ppermute x32, starting transfers between devices, to_other_core(): lax.ppermute(values, ('view', 'dp'), [(i, i ^ difference + size) for i in...  31.7 us
    ppermute x9, starting transfers between devices, to_partner(): lax.ppermute(values, 'dp', [(i, i ^ difference) for i in range(lax.axis_s...  11.6 us
    ppermute x32, waiting for transfers between devices, to_other_core(): lax.ppermute(values, ('view', 'dp'), [(i, i ^ difference + size) for i in...  11.3 us
    ppermute x9, waiting for transfers between devices, to_partner(): lax.ppermute(values, 'dp', [(i, i ^ difference) for i in range(lax.axis_s...  10.5 us
    pallas_call x1, Pallas kernels, shards(): pl.pallas_call(first_kernel, in_specs=[pl.BlockSpec(memory_space=pltpu.HB...  8.3 us
    pallas_call x1, Pallas kernels, shards(): pl.pallas_call(functools.partial(second_kernel, cell_count), in_specs=[he...  8.29 us
    pallas_call x1, Pallas kernels, shards(): pl.pallas_call(functools.partial(back_second_kernel, cell_count, float(al...  4.94 us
    pallas_call x4, Pallas kernels, back_stem(): pl.pallas_call(functools.partial(back_stem_kernel, step), in_specs=[held(...  4.66 us
  transfers between devices with their start and end apart: 48, of which 21 were waited for; matrix products, arithmetic and copies ran while one was open for 0% of the time, Pallas kernels for 11%

profile of v3, /device:TPU:0, one launch (start us, length us, event | category | flops | bytes accessed | tf_op | source)
XLA Modules:
  0.0 112.3 jit_solution(3069697956645762030)
XLA Ops:
  0.7 8.3 %first_conv.1 = (f32[4096,256]{1,0:T(8,128)S(1)}, f32[4096,256]{1,0:T(8,128)S(1)}, bf16[34,10,16,128]{3,2,1,0:T(8,128)(2,1)S(1)}, f32[3,288,128]{2,1,0:T(8,128)S...) custom-call(bf16[4,3,32,32]{3,2,1,0:T(8,128)(2,1)} %bitcast.44, f32[27,96]{1,0:T(8,128)} %sw.1, f32[27,96]{1,0:T(8,128)} %st.1, ...), custom_call_target="tpu_custom_call" | custom-call | tf_op jit(solution)/shard_map/first_conv/pallas_call | solution.py:937
  9.0 3.4 %collective-permute-start.3 = (f32[8,128]{1,0:T(8,128)S(1)}, f32[8,128]{1,0:T(8,128)S(1)}, u32[]{:S(2)}, u32[]{:S(2)}) collective-permute-start(f32[8,128]{1,0:T(8,128)S(1)} %get-tuple-element.130), channel_id=1, source_target_pairs={{0,19},{1,18},{2,17},{3,16},{4,23},{5,22},{6,21},{7,20},{8,27},{9,... | collective-permute-start | bytes 12296 | tf_op jit(solution)/shard_map/ppermute | solution.py:828
  13.9 1.6 %collective-permute-done.2 = f32[8,128]{1,0:T(8,128)S(1)} collective-permute-done((f32[8,128]{1,0:T(8,128)S(1)}, f32[8,128]{1,0:T(8,128)S(1)}, u32[]{:S(2)}, u32[]{:S(2)}) %collective-permute-start.2) | collective-permute-done | bytes 4128 | tf_op jit(solution)/shard_map/ppermute | solution.py:828
  16.3 3.4 %collective-permute-start.7 = (f32[8,128]{1,0:T(8,128)S(1)}, f32[8,128]{1,0:T(8,128)S(1)}, u32[]{:S(2)}, u32[]{:S(2)}) collective-permute-start(f32[8,128]{1,0:T(8,128)S(1)} %add_add_fusion.2), channel_id=1, source_target_pairs={{0,28},{1,29},{2,30},{3,31},{4,24},{5,25},{6,26},{7,27},{8,20},{9,... | collective-permute-start | bytes 12296 | tf_op jit(solution)/shard_map/ppermute | solution.py:828
  21.9 1.7 %collective-permute-done.6.recv_ref_2_.recv1_ref_2_ = f32[8,128]{1,0:T(8,128)S(1)} collective-permute-done((f32[8,128]{1,0:T(8,128)S(1)}, f32[8,128]{1,0:T(8,128)S(1)}, u32[]{:S(2)}, u32[]{:S(2)}) %collective-permute-start.6) | collective-permute-done | bytes 4128 | tf_op jit(solution)/shard_map/ppermute | solution.py:828
  23.7 8.3 %second_conv.1 = (f32[4096,256]{1,0:T(8,128)S(1)}, f32[4096,256]{1,0:T(8,128)S(1)}, bf16[2,34,10,16,128]{4,3,2,1,0:T(8,128)(2,1)S(1)}, f32[4096,256]{1,0:T(8,128...) custom-call(f32[4096,256]{1,0:T(8,128)S(1)} %get-tuple-element.128.first_s.first_ref, ...), custom_call_target="tpu_custom_call" | custom-call | tf_op jit(solution)/shard_map/second_conv/pallas_call | solution.py:966
  32.0 1.6 %collective-permute-start.11 = (f32[8,128]{1,0:T(8,128)S(1)}, f32[8,128]{1,0:T(8,128)S(1)}, u32[]{:S(2)}, u32[]{:S(2)}) collective-permute-start(f32[8,128]{1,0:T(8,128)S(1)} %get-tuple-element.143), channel_id=1, source_target_pairs={{0,19},{1,18},{2,17},{3,16},{4,23},{5,22},{6,21},{7,20},{8,27},{9,... | collective-permute-start | bytes 12296 | tf_op jit(solution)/shard_map/ppermute | solution.py:828
  33.8 1.4 %collective-permute-start.9 = (f32[8,128]{1,0:T(8,128)S(1)}, f32[8,128]{1,0:T(8,128)S(1)}, u32[]{:S(2)}, u32[]{:S(2)}) collective-permute-start(f32[8,128]{1,0:T(8,128)S(1)} %get-tuple-element.143), channel_id=1, source_target_pairs={{0,17},{1,16},{2,19},{3,18},{4,21},{5,20},{6,23},{7,22},{8,25},{9,... | collective-permute-start | bytes 12296 | tf_op jit(solution)/shard_map/ppermute | solution.py:828
  36.8 1.7 %collective-permute-start.15 = (f32[8,128]{1,0:T(8,128)S(1)}, f32[8,128]{1,0:T(8,128)S(1)}, u32[]{:S(2)}, u32[]{:S(2)}) collective-permute-start(f32[8,128]{1,0:T(8,128)S(1)} %add_add_fusion.1), channel_id=1, source_target_pairs={{0,28},{1,29},{2,30},{3,31},{4,24},{5,25},{6,26},{7,27},{8,20},{9,... | collective-permute-start | bytes 12296 | tf_op jit(solution)/shard_map/ppermute | solution.py:828
  38.7 2.2 %collective-permute-start.13 = (f32[8,128]{1,0:T(8,128)S(1)}, f32[8,128]{1,0:T(8,128)S(1)}, u32[]{:S(2)}, u32[]{:S(2)}) collective-permute-start(f32[8,128]{1,0:T(8,128)S(1)} %add_add_fusion.1), channel_id=1, source_target_pairs={{0,20},{1,21},{2,22},{3,23},{4,16},{5,17},{6,18},{7,19},{8,28},{9,... | collective-permute-start | bytes 12296 | tf_op jit(solution)/shard_map/ppermute | solution.py:828
  44.0 1.7 %student_logits.1 = (f32[8,384]{1,0:T(8,128)S(1)}, f32[4096,256]{1,0:T(8,128)S(1)}) custom-call(f32[2,8,128]{2,1,0:T(8,128)S(1)} %facts.1.facts_ref, f32[4096,256]{1,0:T(8,128)S(1)} %get-tuple-element.141.second_ref, f32[8,128]{1,0:T(8,128)S(1)} %collective-permute-done.12.recv_ref_0_.recv2_ref_0_, ...), custom_call_target="tpu_custom_call" | custom-call | flops 4000000000 | bytes 8000000 | tf_op jit(solution)/shard_map/student_logits/pallas_call | solution.py:989
  45.7 1.9 %collective-permute-start.20 = (f32[1,8,384]{2,1,0:T(8,128)S(1)}, f32[1,8,384]{2,1,0:T(8,128)S(1)}, u32[]{:S(2)}, u32[]{:S(2)}) collective-permute-start(f32[1,8,384]{2,1,0:T(8,128)S(1)} %assemble.1), channel_id=1, source_target_pairs={{0,28},{1,29},{2,30},{3,31},{4,24},{5,25},{6,26},{7,27},{8,20},{9,... | collective-permute-start | bytes 36872 | tf_op jit(solution)/shard_map/ppermute | solution.py:828
  48.4 1.2 %collective-permute-start.18 = (f32[1,8,384]{2,1,0:T(8,128)S(1)}, f32[1,8,384]{2,1,0:T(8,128)S(1)}, u32[]{:S(2)}, u32[]{:S(2)}) collective-permute-start(f32[1,8,384]{2,1,0:T(8,128)S(1)} %assemble.1), channel_id=1, source_target_pairs={{0,20},{1,21},{2,22},{3,23},{4,16},{5,17},{6,18},{7,19},{8,28},{9,... | collective-permute-start | bytes 36872 | tf_op jit(solution)/shard_map/ppermute | solution.py:828
  51.6 2.3 %collective-permute-start.24 = (f32[4,8,384]{2,1,0:T(8,128)S(1)}, f32[4,8,384]{2,1,0:T(8,128)S(1)}, u32[]{:S(2)}, u32[]{:S(2)}) collective-permute-start(f32[4,8,384]{2,1,0:T(8,128)S(1)} %stack.1), channel_id=1, source_target_pairs={{0,19},{1,18},{2,17},{3,16},{4,23},{5,22},{6,21},{7,20},{8,27},{9,... | collective-permute-start | bytes 147464 | tf_op jit(solution)/shard_map/ppermute | solution.py:828
  55.0 1.3 %collective-permute-done.24.recv3_ref_3_ = f32[4,8,384]{2,1,0:T(8,128)S(1)} collective-permute-done((f32[4,8,384]{2,1,0:T(8,128)S(1)}, f32[4,8,384]{2,1,0:T(8,128)S(1)}, u32[]{:S(2)}, u32[]{:S(2)}) %collective-permute-start.24) | collective-permute-done | bytes 49184 | tf_op jit(solution)/shard_map/ppermute | solution.py:828
  58.2 4.9 %back_second.1 = (f32[4096,256]{1,0:T(8,128)S(1)}, bf16[2,34,10,16,128]{4,3,2,1,0:T(8,128)(2,1)S(1)}, f32[8,128]{1,0:T(8,128)S(1)}, f32[24,128]{1,0:T(8,128)S(1)}, f32[8,128]{1,0:T(8,128)S(1)}) custom-call(f32[4096,256]{1,0:T(8,128)S(1)} %get-tuple-element.141.second_ref, f32[4096,256]{1,0:T(8,128)S(1)} %get-tuple-element.128.first_s.first_ref, ...), custom_call_target="tpu_custom_call" | custom-call | tf_op jit(solution)/shard_map/back_second/pallas_call | solution.py:1006
  63.1 1.4 %collective-permute-start.28 = (f32[8,128]{1,0:T(8,128)S(1)}, f32[8,128]{1,0:T(8,128)S(1)}, u32[]{:S(2)}, u32[]{:S(2)}) collective-permute-start(f32[8,128]{1,0:T(8,128)S(1)} %get-tuple-element.161), channel_id=1, source_target_pairs={{0,19},{1,18},{2,17},{3,16},{4,23},{5,22},{6,21},{7,20},{8,27},{9,... | collective-permute-start | bytes 12296 | tf_op jit(solution)/shard_map/ppermute | solution.py:828
  66.5 1.9 %second_weight.2 = f32[672,128]{1,0:T(8,128)S(1)} custom-call(bf16[2,34,10,16,128]{4,3,2,1,0:T(8,128)(2,1)S(1)} %get-tuple-element.162.frame_ref, bf16[2,34,10,16,128]{4,3,2,1,0:T(8,128)(2,1)S(1)} %get-tuple-element.163.dy_ref), custom_call_target="tpu_custom_call" | custom-call | flops 4000000000 | bytes 8000000 | tf_op jit(solution)/shard_map/second_weight/pallas_call | solution.py:1022
  68.5 1.6 %collective-permute-start.32 = (f32[8,128]{1,0:T(8,128)S(1)}, f32[8,128]{1,0:T(8,128)S(1)}, u32[]{:S(2)}, u32[]{:S(2)}) collective-permute-start(f32[8,128]{1,0:T(8,128)S(1)} %add_add_fusion), channel_id=1, source_target_pairs={{0,28},{1,29},{2,30},{3,31},{4,24},{5,25},{6,26},{7,27},{8,20},{9,... | collective-permute-start | bytes 12296 | tf_op jit(solution)/shard_map/ppermute | solution.py:828
  70.9 1.4 %collective-permute-start.30 = (f32[8,128]{1,0:T(8,128)S(1)}, f32[8,128]{1,0:T(8,128)S(1)}, u32[]{:S(2)}, u32[]{:S(2)}) collective-permute-start(f32[8,128]{1,0:T(8,128)S(1)} %add_add_fusion), channel_id=1, source_target_pairs={{0,20},{1,21},{2,22},{3,23},{4,16},{5,17},{6,18},{7,19},{8,28},{9,... | collective-permute-start | bytes 12296 | tf_op jit(solution)/shard_map/ppermute | solution.py:828
  72.9 1.9 %second_weight.3.keep2 = f32[672,128]{1,0:T(8,128)S(1)} custom-call(bf16[2,34,10,16,128]{4,3,2,1,0:T(8,128)(2,1)S(1)} %get-tuple-element.162.frame_ref, bf16[2,34,10,16,128]{4,3,2,1,0:T(8,128)(2,1)S(1)} %get-tuple-element.163.dy_ref), custom_call_target="tpu_custom_call" | custom-call | flops 4000000000 | bytes 8000000 | tf_op jit(solution)/shard_map/second_weight/pallas_call | solution.py:1022
  74.8 3.6 %back_weight.1 = (bf16[2,34,10,16,128]{4,3,2,1,0:T(8,128)(2,1)S(1)}, f32[704,128]{1,0:T(8,128)S(1)}, f32[704,128]{1,0:T(8,128)S(1)}) custom-call(f32[4096,256]{1,0:T(8,128)S(1)} %get-tuple-element.159.du_ref, f32[4096,256]{1,0:T(8,128)S(1)} %get-tuple-element.128.first_s.first_ref, bf16[34,10,16,128]{3,2,1,0:T(8,128)(2,1)S(1)} %get-tuple-element.160.low_ref, ...), custom_call_target="tpu_custom_call" | custom-call | flops 8000000000 | bytes 16000000 | tf_op jit(solution)/shard_map/back_weight/pallas_call | solution.py:1038
  81.5 1.6 %collective-permute-start.36 = (s16[352,128]{1,0:T(8,128)(2,1)S(1)}, s16[352,128]{1,0:T(8,128)(2,1)S(1)}, u32[]{:S(2)}, u32[]{:S(2)}) collective-permute-start(s16[352,128]{1,0:T(8,128)(2,1)S(1)} %get-tuple-element.193), channel_id=1, source_target_pairs={{0,2},{1,3},{2,0},{3,1},{4,6},{5,7},{6,4},{7,5},{8,10},{9,11},{10,... | collective-permute-start | bytes 270344 | tf_op jit(solution)/shard_map/ppermute | solution.py:823
  85.2 1.2 %back_stem.6 = (f32[128,128]{1,0:T(8,128)S(1)}, f32[80,128]{1,0:T(8,128)S(1)}) custom-call(bf16[2,34,10,16,128]{4,3,2,1,0:T(8,128)(2,1)S(1)} %get-tuple-element.174.frame_ref, f32[3,288,128]{2,1,0:T(8,128)S(1)} %get-tuple-element.175.moved_ref, f32[8,128]{1,0:T(8,128)S(1)} %get-tuple-element.176.dmix_ref, bf16[2,768,256]{2,1,0:T(8,128)(2,1)S(1)} %get-tuple-element.177.w_ref, ...), custom_call_target="tpu_custom_call" | custom-call | flops 2000000000 | bytes 4000000 | tf_op jit(solution)/shard_map/back_stem/pallas_call | solution.py:1053
  86.5 1.2 %back_stem.7.stem_ref = f32[27,128]{1,0:T(8,128)S(1)} custom-call(bf16[2,34,10,16,128]{4,3,2,1,0:T(8,128)(2,1)S(1)} %get-tuple-element.174.frame_ref, f32[3,288,128]{2,1,0:T(8,128)S(1)} %get-tuple-element.175.moved_ref, f32[8,128]{1,0:T(8,128)S(1)} %get-tuple-element.176.dmix_ref, bf16[2,768,256]{2,1,0:T(8,128)(2,1)S(1)} %get-tuple-element.177.w_ref, ...), custom_call_target="tpu_custom_call" | custom-call | flops 2000000000 | bytes 4000000 | tf_op jit(solution)/shard_map/back_stem/pallas_call | solution.py:1053
  88.7 1.7 %collective-permute-start.40 = (s16[384,128]{1,0:T(8,128)(2,1)S(1)}, s16[384,128]{1,0:T(8,128)(2,1)S(1)}, u32[]{:S(2)}, u32[]{:S(2)}) collective-permute-start(s16[384,128]{1,0:T(8,128)(2,1)S(1)} %combine.1.recv_refs_0_), channel_id=1, source_target_pairs={{0,12},{1,13},{2,14},{3,15},{4,8},{5,9},{6,10},{7,11},{8,4},{9,5},... | collective-permute-start | bytes 294920 | tf_op jit(solution)/shard_map/ppermute | solution.py:823
  91.1 2.1 %collective-permute-start.38 = (s16[384,128]{1,0:T(8,128)(2,1)S(1)}, s16[384,128]{1,0:T(8,128)(2,1)S(1)}, u32[]{:S(2)}, u32[]{:S(2)}) collective-permute-start(s16[384,128]{1,0:T(8,128)(2,1)S(1)} %combine.1.recv_refs_0_), channel_id=1, source_target_pairs={{0,4},{1,5},{2,6},{3,7},{4,0},{5,1},{6,2},{7,3},{8,12},{9,13},{10,... | collective-permute-start | bytes 294920 | tf_op jit(solution)/shard_map/ppermute | solution.py:823
  93.2 2.9 %collective-permute-done.40.recv_refs_3_ = s16[384,128]{1,0:T(8,128)(2,1)S(1)} collective-permute-done((s16[384,128]{1,0:T(8,128)(2,1)S(1)}, s16[384,128]{1,0:T(8,128)(2,1)S(1)}, u32[]{:S(2)}, u32[]{:S(2)}) %collective-permute-start.40) | collective-permute-done | bytes 98336 | tf_op jit(solution)/shard_map/ppermute | solution.py:823
  96.1 3.1 %collective-permute-done.39.recv_refs_2_ = s16[384,128]{1,0:T(8,128)(2,1)S(1)} collective-permute-done((s16[384,128]{1,0:T(8,128)(2,1)S(1)}, s16[384,128]{1,0:T(8,128)(2,1)S(1)}, u32[]{:S(2)}, u32[]{:S(2)}) %collective-permute-start.39) | collective-permute-done | bytes 98336 | tf_op jit(solution)/shard_map/ppermute | solution.py:823
  99.4 2.1 %collective-permute-start.43 = (s16[384,128]{1,0:T(8,128)(2,1)S(1)}, s16[384,128]{1,0:T(8,128)(2,1)S(1)}, u32[]{:S(2)}, u32[]{:S(2)}) collective-permute-start(s16[384,128]{1,0:T(8,128)(2,1)S(1)} %recode.1.codes_0_), channel_id=1, source_target_pairs={{0,3},{1,2},{2,1},{3,0},{4,7},{5,6},{6,5},{7,4},{8,11},{9,10},{10,... | collective-permute-start | bytes 294920 | tf_op jit(solution)/shard_map/ppermute | solution.py:823
  103.0 3.0 %collective-permute-done.43.codes_3_ = s16[384,128]{1,0:T(8,128)(2,1)S(1)} collective-permute-done((s16[384,128]{1,0:T(8,128)(2,1)S(1)}, s16[384,128]{1,0:T(8,128)(2,1)S(1)}, u32[]{:S(2)}, u32[]{:S(2)}) %collective-permute-start.43) | collective-permute-done | bytes 98336 | tf_op jit(solution)/shard_map/ppermute | solution.py:823
  108.1 4.0 %update.1 = (f32[4,96,864]{2,1,0:T(8,128)}, f32[4,96,864]{2,1,0:T(8,128)}, f32[4,96,864]{2,1,0:T(8,128)}, f32[4,96,864]{2,1,0:T(8,128)}, bf16[4,96,864]{2,1,0:T(...) custom-call(f32[2,672,128]{2,1,0:T(8,128)S(1)} %get-tuple-element.20, ...), custom_call_target="tpu_custom_call" | custom-call | tf_op jit(solution)/shard_map/update/pallas_call | solution.py:1104
  (130 shorter events, 29.3 us)
Async XLA Ops:
  9.0 4.9 %collective-permute-start.3 = (f32[8,128]{1,0:T(8,128)S(1)}, f32[8,128]{1,0:T(8,128)S(1)}, u32[]{:S(2)}, u32[]{:S(2)}) collective-permute-start(f32[8,128]{1,0:T(8,128)S(1)} %get-tuple-element.130), channel_id=1, source_target_pairs={{0,19},{1,18},{2,17},{3,16},{4,23},{5,22},{6,21},{7,20},{8,27},{9,... | collective-permute-start | bytes 12296 | tf_op jit(solution)/shard_map/ppermute | solution.py:828
  16.3 5.6 %collective-permute-start.7 = (f32[8,128]{1,0:T(8,128)S(1)}, f32[8,128]{1,0:T(8,128)S(1)}, u32[]{:S(2)}, u32[]{:S(2)}) collective-permute-start(f32[8,128]{1,0:T(8,128)S(1)} %add_add_fusion.2), channel_id=1, source_target_pairs={{0,28},{1,29},{2,30},{3,31},{4,24},{5,25},{6,26},{7,27},{8,20},{9,... | collective-permute-start | bytes 12296 | tf_op jit(solution)/shard_map/ppermute | solution.py:828
  19.7 4.0 %collective-permute-start.6 = (f32[8,128]{1,0:T(8,128)S(1)}, f32[8,128]{1,0:T(8,128)S(1)}, u32[]{:S(2)}, u32[]{:S(2)}) collective-permute-start(f32[8,128]{1,0:T(8,128)S(1)} %add_add_fusion.2), channel_id=1, source_target_pairs={{0,24},{1,25},{2,26},{3,27},{4,28},{5,29},{6,30},{7,31},{8,16},{9,... | collective-permute-start | bytes 12296 | tf_op jit(solution)/shard_map/ppermute | solution.py:828
  19.7 4.0 %collective-permute-start.5 = (f32[8,128]{1,0:T(8,128)S(1)}, f32[8,128]{1,0:T(8,128)S(1)}, u32[]{:S(2)}, u32[]{:S(2)}) collective-permute-start(f32[8,128]{1,0:T(8,128)S(1)} %add_add_fusion.2), channel_id=1, source_target_pairs={{0,20},{1,21},{2,22},{3,23},{4,16},{5,17},{6,18},{7,19},{8,28},{9,... | collective-permute-start | bytes 12296 | tf_op jit(solution)/shard_map/ppermute | solution.py:828
  20.3 3.3 %collective-permute-start.4 = (f32[8,128]{1,0:T(8,128)S(1)}, f32[8,128]{1,0:T(8,128)S(1)}, u32[]{:S(2)}, u32[]{:S(2)}) collective-permute-start(f32[8,128]{1,0:T(8,128)S(1)} %add_add_fusion.2), channel_id=1, source_target_pairs={{0,16},{1,17},{2,18},{3,19},{4,20},{5,21},{6,22},{7,23},{8,24},{9,... | collective-permute-start | bytes 12296 | tf_op jit(solution)/shard_map/ppermute | solution.py:828
  32.0 4.0 %collective-permute-start.11 = (f32[8,128]{1,0:T(8,128)S(1)}, f32[8,128]{1,0:T(8,128)S(1)}, u32[]{:S(2)}, u32[]{:S(2)}) collective-permute-start(f32[8,128]{1,0:T(8,128)S(1)} %get-tuple-element.143), channel_id=1, source_target_pairs={{0,19},{1,18},{2,17},{3,16},{4,23},{5,22},{6,21},{7,20},{8,27},{9,... | collective-permute-start | bytes 12296 | tf_op jit(solution)/shard_map/ppermute | solution.py:828
  36.8 4.9 %collective-permute-start.15 = (f32[8,128]{1,0:T(8,128)S(1)}, f32[8,128]{1,0:T(8,128)S(1)}, u32[]{:S(2)}, u32[]{:S(2)}) collective-permute-start(f32[8,128]{1,0:T(8,128)S(1)} %add_add_fusion.1), channel_id=1, source_target_pairs={{0,28},{1,29},{2,30},{3,31},{4,24},{5,25},{6,26},{7,27},{8,20},{9,... | collective-permute-start | bytes 12296 | tf_op jit(solution)/shard_map/ppermute | solution.py:828
  38.6 3.9 %collective-permute-start.14 = (f32[8,128]{1,0:T(8,128)S(1)}, f32[8,128]{1,0:T(8,128)S(1)}, u32[]{:S(2)}, u32[]{:S(2)}) collective-permute-start(f32[8,128]{1,0:T(8,128)S(1)} %add_add_fusion.1), channel_id=1, source_target_pairs={{0,24},{1,25},{2,26},{3,27},{4,28},{5,29},{6,30},{7,31},{8,16},{9,... | collective-permute-start | bytes 12296 | tf_op jit(solution)/shard_map/ppermute | solution.py:828
  38.7 3.8 %collective-permute-start.13 = (f32[8,128]{1,0:T(8,128)S(1)}, f32[8,128]{1,0:T(8,128)S(1)}, u32[]{:S(2)}, u32[]{:S(2)}) collective-permute-start(f32[8,128]{1,0:T(8,128)S(1)} %add_add_fusion.1), channel_id=1, source_target_pairs={{0,20},{1,21},{2,22},{3,23},{4,16},{5,17},{6,18},{7,19},{8,28},{9,... | collective-permute-start | bytes 12296 | tf_op jit(solution)/shard_map/ppermute | solution.py:828
  45.7 4.9 %collective-permute-start.20 = (f32[1,8,384]{2,1,0:T(8,128)S(1)}, f32[1,8,384]{2,1,0:T(8,128)S(1)}, u32[]{:S(2)}, u32[]{:S(2)}) collective-permute-start(f32[1,8,384]{2,1,0:T(8,128)S(1)} %assemble.1), channel_id=1, source_target_pairs={{0,28},{1,29},{2,30},{3,31},{4,24},{5,25},{6,26},{7,27},{8,20},{9,... | collective-permute-start | bytes 36872 | tf_op jit(solution)/shard_map/ppermute | solution.py:828
  47.5 4.1 %collective-permute-start.19 = (f32[1,8,384]{2,1,0:T(8,128)S(1)}, f32[1,8,384]{2,1,0:T(8,128)S(1)}, u32[]{:S(2)}, u32[]{:S(2)}) collective-permute-start(f32[1,8,384]{2,1,0:T(8,128)S(1)} %assemble.1), channel_id=1, source_target_pairs={{0,24},{1,25},{2,26},{3,27},{4,28},{5,29},{6,30},{7,31},{8,16},{9,... | collective-permute-start | bytes 36872 | tf_op jit(solution)/shard_map/ppermute | solution.py:828
  48.4 3.3 %collective-permute-start.18 = (f32[1,8,384]{2,1,0:T(8,128)S(1)}, f32[1,8,384]{2,1,0:T(8,128)S(1)}, u32[]{:S(2)}, u32[]{:S(2)}) collective-permute-start(f32[1,8,384]{2,1,0:T(8,128)S(1)} %assemble.1), channel_id=1, source_target_pairs={{0,20},{1,21},{2,22},{3,23},{4,16},{5,17},{6,18},{7,19},{8,28},{9,... | collective-permute-start | bytes 36872 | tf_op jit(solution)/shard_map/ppermute | solution.py:828
  51.6 4.7 %collective-permute-start.24 = (f32[4,8,384]{2,1,0:T(8,128)S(1)}, f32[4,8,384]{2,1,0:T(8,128)S(1)}, u32[]{:S(2)}, u32[]{:S(2)}) collective-permute-start(f32[4,8,384]{2,1,0:T(8,128)S(1)} %stack.1), channel_id=1, source_target_pairs={{0,19},{1,18},{2,17},{3,16},{4,23},{5,22},{6,21},{7,20},{8,27},{9,... | collective-permute-start | bytes 147464 | tf_op jit(solution)/shard_map/ppermute | solution.py:828
  54.0 3.5 %collective-permute-start.23 = (f32[4,8,384]{2,1,0:T(8,128)S(1)}, f32[4,8,384]{2,1,0:T(8,128)S(1)}, u32[]{:S(2)}, u32[]{:S(2)}) collective-permute-start(f32[4,8,384]{2,1,0:T(8,128)S(1)} %stack.1), channel_id=1, source_target_pairs={{0,18},{1,19},{2,16},{3,17},{4,22},{5,23},{6,20},{7,21},{8,26},{9,... | collective-permute-start | bytes 147464 | tf_op jit(solution)/shard_map/ppermute | solution.py:828
  54.4 3.8 %collective-permute-start.22 = (f32[4,8,384]{2,1,0:T(8,128)S(1)}, f32[4,8,384]{2,1,0:T(8,128)S(1)}, u32[]{:S(2)}, u32[]{:S(2)}) collective-permute-start(f32[4,8,384]{2,1,0:T(8,128)S(1)} %stack.1), channel_id=1, source_target_pairs={{0,17},{1,16},{2,19},{3,18},{4,21},{5,20},{6,23},{7,22},{8,25},{9,... | collective-permute-start | bytes 147464 | tf_op jit(solution)/shard_map/ppermute | solution.py:828
  54.7 3.5 %collective-permute-start.21 = (f32[4,8,384]{2,1,0:T(8,128)S(1)}, f32[4,8,384]{2,1,0:T(8,128)S(1)}, u32[]{:S(2)}, u32[]{:S(2)}) collective-permute-start(f32[4,8,384]{2,1,0:T(8,128)S(1)} %stack.1), channel_id=1, source_target_pairs={{0,16},{1,17},{2,18},{3,19},{4,20},{5,21},{6,22},{7,23},{8,24},{9,... | collective-permute-start | bytes 147464 | tf_op jit(solution)/shard_map/ppermute | solution.py:828
  63.1 5.3 %collective-permute-start.28 = (f32[8,128]{1,0:T(8,128)S(1)}, f32[8,128]{1,0:T(8,128)S(1)}, u32[]{:S(2)}, u32[]{:S(2)}) collective-permute-start(f32[8,128]{1,0:T(8,128)S(1)} %get-tuple-element.161), channel_id=1, source_target_pairs={{0,19},{1,18},{2,17},{3,16},{4,23},{5,22},{6,21},{7,20},{8,27},{9,... | collective-permute-start | bytes 12296 | tf_op jit(solution)/shard_map/ppermute | solution.py:828
  64.5 4.0 %collective-permute-start.27 = (f32[8,128]{1,0:T(8,128)S(1)}, f32[8,128]{1,0:T(8,128)S(1)}, u32[]{:S(2)}, u32[]{:S(2)}) collective-permute-start(f32[8,128]{1,0:T(8,128)S(1)} %get-tuple-element.161), channel_id=1, source_target_pairs={{0,18},{1,19},{2,16},{3,17},{4,22},{5,23},{6,20},{7,21},{8,26},{9,... | collective-permute-start | bytes 12296 | tf_op jit(solution)/shard_map/ppermute | solution.py:828
  65.4 3.1 %collective-permute-start.26 = (f32[8,128]{1,0:T(8,128)S(1)}, f32[8,128]{1,0:T(8,128)S(1)}, u32[]{:S(2)}, u32[]{:S(2)}) collective-permute-start(f32[8,128]{1,0:T(8,128)S(1)} %get-tuple-element.161), channel_id=1, source_target_pairs={{0,17},{1,16},{2,19},{3,18},{4,21},{5,20},{6,23},{7,22},{8,25},{9,... | collective-permute-start | bytes 12296 | tf_op jit(solution)/shard_map/ppermute | solution.py:828
  68.5 6.3 %collective-permute-start.32 = (f32[8,128]{1,0:T(8,128)S(1)}, f32[8,128]{1,0:T(8,128)S(1)}, u32[]{:S(2)}, u32[]{:S(2)}) collective-permute-start(f32[8,128]{1,0:T(8,128)S(1)} %add_add_fusion), channel_id=1, source_target_pairs={{0,28},{1,29},{2,30},{3,31},{4,24},{5,25},{6,26},{7,27},{8,20},{9,... | collective-permute-start | bytes 12296 | tf_op jit(solution)/shard_map/ppermute | solution.py:828
  70.0 4.7 %collective-permute-start.31 = (f32[8,128]{1,0:T(8,128)S(1)}, f32[8,128]{1,0:T(8,128)S(1)}, u32[]{:S(2)}, u32[]{:S(2)}) collective-permute-start(f32[8,128]{1,0:T(8,128)S(1)} %add_add_fusion), channel_id=1, source_target_pairs={{0,24},{1,25},{2,26},{3,27},{4,28},{5,29},{6,30},{7,31},{8,16},{9,... | collective-permute-start | bytes 12296 | tf_op jit(solution)/shard_map/ppermute | solution.py:828
  70.9 3.9 %collective-permute-start.30 = (f32[8,128]{1,0:T(8,128)S(1)}, f32[8,128]{1,0:T(8,128)S(1)}, u32[]{:S(2)}, u32[]{:S(2)}) collective-permute-start(f32[8,128]{1,0:T(8,128)S(1)} %add_add_fusion), channel_id=1, source_target_pairs={{0,20},{1,21},{2,22},{3,23},{4,16},{5,17},{6,18},{7,19},{8,28},{9,... | collective-permute-start | bytes 12296 | tf_op jit(solution)/shard_map/ppermute | solution.py:828
  80.5 7.2 %collective-permute-start.35 = (s16[352,128]{1,0:T(8,128)(2,1)S(1)}, s16[352,128]{1,0:T(8,128)(2,1)S(1)}, u32[]{:S(2)}, u32[]{:S(2)}) collective-permute-start(s16[352,128]{1,0:T(8,128)(2,1)S(1)} %get-tuple-element.192), channel_id=1, source_target_pairs={{0,1},{1,0},{2,3},{3,2},{4,5},{5,4},{6,7},{7,6},{8,9},{9,8},{10,11... | collective-permute-start | bytes 270344 | tf_op jit(solution)/shard_map/ppermute | solution.py:823
  81.5 6.2 %collective-permute-start.36 = (s16[352,128]{1,0:T(8,128)(2,1)S(1)}, s16[352,128]{1,0:T(8,128)(2,1)S(1)}, u32[]{:S(2)}, u32[]{:S(2)}) collective-permute-start(s16[352,128]{1,0:T(8,128)(2,1)S(1)} %get-tuple-element.193), channel_id=1, source_target_pairs={{0,2},{1,3},{2,0},{3,1},{4,6},{5,7},{6,4},{7,5},{8,10},{9,11},{10,... | collective-permute-start | bytes 270344 | tf_op jit(solution)/shard_map/ppermute | solution.py:823
  83.2 5.4 %collective-permute-start.37 = (s16[352,128]{1,0:T(8,128)(2,1)S(1)}, s16[352,128]{1,0:T(8,128)(2,1)S(1)}, u32[]{:S(2)}, u32[]{:S(2)}) collective-permute-start(s16[352,128]{1,0:T(8,128)(2,1)S(1)} %get-tuple-element.194), channel_id=1, source_target_pairs={{0,3},{1,2},{2,1},{3,0},{4,7},{5,6},{6,5},{7,4},{8,11},{9,10},{10,... | collective-permute-start | bytes 270344 | tf_op jit(solution)/shard_map/ppermute | solution.py:823
  88.7 7.4 %collective-permute-start.40 = (s16[384,128]{1,0:T(8,128)(2,1)S(1)}, s16[384,128]{1,0:T(8,128)(2,1)S(1)}, u32[]{:S(2)}, u32[]{:S(2)}) collective-permute-start(s16[384,128]{1,0:T(8,128)(2,1)S(1)} %combine.1.recv_refs_0_), channel_id=1, source_target_pairs={{0,12},{1,13},{2,14},{3,15},{4,8},{5,9},{6,10},{7,11},{8,4},{9,5},... | collective-permute-start | bytes 294920 | tf_op jit(solution)/shard_map/ppermute | solution.py:823
  90.5 8.8 %collective-permute-start.39 = (s16[384,128]{1,0:T(8,128)(2,1)S(1)}, s16[384,128]{1,0:T(8,128)(2,1)S(1)}, u32[]{:S(2)}, u32[]{:S(2)}) collective-permute-start(s16[384,128]{1,0:T(8,128)(2,1)S(1)} %combine.1.recv_refs_0_), channel_id=1, source_target_pairs={{0,8},{1,9},{2,10},{3,11},{4,12},{5,13},{6,14},{7,15},{8,0},{9,1},... | collective-permute-start | bytes 294920 | tf_op jit(solution)/shard_map/ppermute | solution.py:823
  91.1 8.2 %collective-permute-start.38 = (s16[384,128]{1,0:T(8,128)(2,1)S(1)}, s16[384,128]{1,0:T(8,128)(2,1)S(1)}, u32[]{:S(2)}, u32[]{:S(2)}) collective-permute-start(s16[384,128]{1,0:T(8,128)(2,1)S(1)} %combine.1.recv_refs_0_), channel_id=1, source_target_pairs={{0,4},{1,5},{2,6},{3,7},{4,0},{5,1},{6,2},{7,3},{8,12},{9,13},{10,... | collective-permute-start | bytes 294920 | tf_op jit(solution)/shard_map/ppermute | solution.py:823
  99.4 6.5 %collective-permute-start.43 = (s16[384,128]{1,0:T(8,128)(2,1)S(1)}, s16[384,128]{1,0:T(8,128)(2,1)S(1)}, u32[]{:S(2)}, u32[]{:S(2)}) collective-permute-start(s16[384,128]{1,0:T(8,128)(2,1)S(1)} %recode.1.codes_0_), channel_id=1, source_target_pairs={{0,3},{1,2},{2,1},{3,0},{4,7},{5,6},{6,5},{7,4},{8,11},{9,10},{10,... | collective-permute-start | bytes 294920 | tf_op jit(solution)/shard_map/ppermute | solution.py:823
  101.5 5.1 %collective-permute-start.42 = (s16[384,128]{1,0:T(8,128)(2,1)S(1)}, s16[384,128]{1,0:T(8,128)(2,1)S(1)}, u32[]{:S(2)}, u32[]{:S(2)}) collective-permute-start(s16[384,128]{1,0:T(8,128)(2,1)S(1)} %recode.1.codes_0_), channel_id=1, source_target_pairs={{0,2},{1,3},{2,0},{3,1},{4,6},{5,7},{6,4},{7,5},{8,10},{9,11},{10,... | collective-permute-start | bytes 294920 | tf_op jit(solution)/shard_map/ppermute | solution.py:823
  102.0 4.6 %collective-permute-start.41 = (s16[384,128]{1,0:T(8,128)(2,1)S(1)}, s16[384,128]{1,0:T(8,128)(2,1)S(1)}, u32[]{:S(2)}, u32[]{:S(2)}) collective-permute-start(s16[384,128]{1,0:T(8,128)(2,1)S(1)} %recode.1.codes_0_), channel_id=1, source_target_pairs={{0,1},{1,0},{2,3},{3,2},{4,5},{5,4},{6,7},{7,6},{8,9},{9,8},{10,11... | collective-permute-start | bytes 294920 | tf_op jit(solution)/shard_map/ppermute | solution.py:823
  103.0 4.2 %collective-permute-start.44 = (s16[384,128]{1,0:T(8,128)(2,1)S(1)}, s16[384,128]{1,0:T(8,128)(2,1)S(1)}, u32[]{:S(2)}, u32[]{:S(2)}) collective-permute-start(s16[384,128]{1,0:T(8,128)(2,1)S(1)} %recode.1.codes_0_), channel_id=1, source_target_pairs={{0,16},{16,0},{1,17},{17,1},{2,18},{18,2},{3,19},{19,3},{4,20},{20... | collective-permute-start | bytes 294920 | tf_op jit(solution)/shard_map/ppermute | solution.py:880
  (36 other events, 329.0 us)

commit v4 on v3

--- a/solution.py
+++ b/solution.py
@@ -828,14 +828,18 @@
     return lax.ppermute(values, ("view", "dp"), [(i, i ^ (difference + size)) for i in range(2 * size)])
 
 
-def far_last(ways):
-    return (1, 3, 2) if ways == 4 else range(1, ways)
+def issue_order(ways, shift, crossing):
+    if ways < 4:
+        return range(1, ways)
+    if shift == 0:
+        return (1, 3, 2)
+    return (1, 2, 3) if crossing else (1, 3, 2)
 
 
 def from_partners(values, shift, ways, crossing=True):
     send = to_other_core if crossing else to_partner
     parts = [to_other_core(values, 0) if crossing else values] + [None] * (ways - 1)
-    for offset in far_last(ways):
+    for offset in issue_order(ways, shift, crossing):
         parts[offset] = send(values, offset << shift)
     return parts
 
@@ -1070,7 +1074,7 @@
         name="encode",
     )(keep2, recv_grad2, keep1, recv_grad1)
     scattered = [coded[0]] + [None] * (QUARTERS - 1)
-    for offset in far_last(QUARTERS):
+    for offset in issue_order(QUARTERS, 0, False):
         scattered[offset] = to_partner(coded[offset], offset)
     scattered = tuple(scattered)
 

time: 112 us -> 112 us (level)
  no operation moved by 1% of the time
where the time goes in v4:
time: 112 us
  starting transfers between devices  44.7 us (40%)
  Pallas kernels  43.2 us (39%)
  waiting for transfers between devices  22.8 us (20%)
  between operations  1.41 us (1%)
    ppermute x32, starting transfers between devices, to_other_core(): lax.ppermute(values, ('view', 'dp'), [(i, i ^ difference + size) for i in...  31.7 us
    ppermute x9, starting transfers between devices, to_partner(): lax.ppermute(values, 'dp', [(i, i ^ difference) for i in range(lax.axis_s...  11.6 us
    ppermute x32, waiting for transfers between devices, to_other_core(): lax.ppermute(values, ('view', 'dp'), [(i, i ^ difference + size) for i in...  11.3 us
    ppermute x9, waiting for transfers between devices, to_partner(): lax.ppermute(values, 'dp', [(i, i ^ difference) for i in range(lax.axis_s...  10.5 us
    pallas_call x1, Pallas kernels, shards(): pl.pallas_call(first_kernel, in_specs=[pl.BlockSpec(memory_space=pltpu.HB...  8.3 us
    pallas_call x1, Pallas kernels, shards(): pl.pallas_call(functools.partial(second_kernel, cell_count), in_specs=[he...  8.29 us
    pallas_call x1, Pallas kernels, shards(): pl.pallas_call(functools.partial(back_second_kernel, cell_count, float(al...  4.94 us
    pallas_call x4, Pallas kernels, back_stem(): pl.pallas_call(functools.partial(back_stem_kernel, step), in_specs=[held(...  4.66 us
  transfers between devices with their start and end apart: 48, of which 21 were waited for; matrix products, arithmetic and copies ran while one was open for 0% of the time, Pallas kernels for 11%

profile of v4, /device:TPU:0, one launch (start us, length us, event | category | flops | bytes accessed | tf_op | source)
XLA Modules:
  0.0 112.3 jit_solution(3069697956645762030)
XLA Ops:
  0.7 8.3 %first_conv.1 = (f32[4096,256]{1,0:T(8,128)S(1)}, f32[4096,256]{1,0:T(8,128)S(1)}, bf16[34,10,16,128]{3,2,1,0:T(8,128)(2,1)S(1)}, f32[3,288,128]{2,1,0:T(8,128)S...) custom-call(bf16[4,3,32,32]{3,2,1,0:T(8,128)(2,1)} %bitcast.44, f32[27,96]{1,0:T(8,128)} %sw.1, f32[27,96]{1,0:T(8,128)} %st.1, ...), custom_call_target="tpu_custom_call" | custom-call | tf_op jit(solution)/shard_map/first_conv/pallas_call | solution.py:941
  9.0 3.4 %collective-permute-start.3 = (f32[8,128]{1,0:T(8,128)S(1)}, f32[8,128]{1,0:T(8,128)S(1)}, u32[]{:S(2)}, u32[]{:S(2)}) collective-permute-start(f32[8,128]{1,0:T(8,128)S(1)} %get-tuple-element.130), channel_id=1, source_target_pairs={{0,19},{1,18},{2,17},{3,16},{4,23},{5,22},{6,21},{7,20},{8,27},{9,... | collective-permute-start | bytes 12296 | tf_op jit(solution)/shard_map/ppermute | solution.py:828
  13.9 1.6 %collective-permute-done.2 = f32[8,128]{1,0:T(8,128)S(1)} collective-permute-done((f32[8,128]{1,0:T(8,128)S(1)}, f32[8,128]{1,0:T(8,128)S(1)}, u32[]{:S(2)}, u32[]{:S(2)}) %collective-permute-start.2) | collective-permute-done | bytes 4128 | tf_op jit(solution)/shard_map/ppermute | solution.py:828
  16.3 3.4 %collective-permute-start.7 = (f32[8,128]{1,0:T(8,128)S(1)}, f32[8,128]{1,0:T(8,128)S(1)}, u32[]{:S(2)}, u32[]{:S(2)}) collective-permute-start(f32[8,128]{1,0:T(8,128)S(1)} %add_add_fusion.2), channel_id=1, source_target_pairs={{0,28},{1,29},{2,30},{3,31},{4,24},{5,25},{6,26},{7,27},{8,20},{9,... | collective-permute-start | bytes 12296 | tf_op jit(solution)/shard_map/ppermute | solution.py:828
  21.9 1.7 %collective-permute-done.6.recv_ref_2_.recv1_ref_2_ = f32[8,128]{1,0:T(8,128)S(1)} collective-permute-done((f32[8,128]{1,0:T(8,128)S(1)}, f32[8,128]{1,0:T(8,128)S(1)}, u32[]{:S(2)}, u32[]{:S(2)}) %collective-permute-start.6) | collective-permute-done | bytes 4128 | tf_op jit(solution)/shard_map/ppermute | solution.py:828
  23.7 8.3 %second_conv.1 = (f32[4096,256]{1,0:T(8,128)S(1)}, f32[4096,256]{1,0:T(8,128)S(1)}, bf16[2,34,10,16,128]{4,3,2,1,0:T(8,128)(2,1)S(1)}, f32[4096,256]{1,0:T(8,128...) custom-call(f32[4096,256]{1,0:T(8,128)S(1)} %get-tuple-element.128.first_s.first_ref, ...), custom_call_target="tpu_custom_call" | custom-call | tf_op jit(solution)/shard_map/second_conv/pallas_call | solution.py:970
  32.0 1.6 %collective-permute-start.11 = (f32[8,128]{1,0:T(8,128)S(1)}, f32[8,128]{1,0:T(8,128)S(1)}, u32[]{:S(2)}, u32[]{:S(2)}) collective-permute-start(f32[8,128]{1,0:T(8,128)S(1)} %get-tuple-element.143), channel_id=1, source_target_pairs={{0,19},{1,18},{2,17},{3,16},{4,23},{5,22},{6,21},{7,20},{8,27},{9,... | collective-permute-start | bytes 12296 | tf_op jit(solution)/shard_map/ppermute | solution.py:828
  33.8 1.4 %collective-permute-start.9 = (f32[8,128]{1,0:T(8,128)S(1)}, f32[8,128]{1,0:T(8,128)S(1)}, u32[]{:S(2)}, u32[]{:S(2)}) collective-permute-start(f32[8,128]{1,0:T(8,128)S(1)} %get-tuple-element.143), channel_id=1, source_target_pairs={{0,17},{1,16},{2,19},{3,18},{4,21},{5,20},{6,23},{7,22},{8,25},{9,... | collective-permute-start | bytes 12296 | tf_op jit(solution)/shard_map/ppermute | solution.py:828
  36.8 1.7 %collective-permute-start.15 = (f32[8,128]{1,0:T(8,128)S(1)}, f32[8,128]{1,0:T(8,128)S(1)}, u32[]{:S(2)}, u32[]{:S(2)}) collective-permute-start(f32[8,128]{1,0:T(8,128)S(1)} %add_add_fusion.1), channel_id=1, source_target_pairs={{0,28},{1,29},{2,30},{3,31},{4,24},{5,25},{6,26},{7,27},{8,20},{9,... | collective-permute-start | bytes 12296 | tf_op jit(solution)/shard_map/ppermute | solution.py:828
  38.7 2.2 %collective-permute-start.13 = (f32[8,128]{1,0:T(8,128)S(1)}, f32[8,128]{1,0:T(8,128)S(1)}, u32[]{:S(2)}, u32[]{:S(2)}) collective-permute-start(f32[8,128]{1,0:T(8,128)S(1)} %add_add_fusion.1), channel_id=1, source_target_pairs={{0,20},{1,21},{2,22},{3,23},{4,16},{5,17},{6,18},{7,19},{8,28},{9,... | collective-permute-start | bytes 12296 | tf_op jit(solution)/shard_map/ppermute | solution.py:828
  44.0 1.7 %student_logits.1 = (f32[8,384]{1,0:T(8,128)S(1)}, f32[4096,256]{1,0:T(8,128)S(1)}) custom-call(f32[2,8,128]{2,1,0:T(8,128)S(1)} %facts.1.facts_ref, f32[4096,256]{1,0:T(8,128)S(1)} %get-tuple-element.141.second_ref, f32[8,128]{1,0:T(8,128)S(1)} %collective-permute-done.12.recv_ref_0_.recv2_ref_0_, ...), custom_call_target="tpu_custom_call" | custom-call | flops 4000000000 | bytes 8000000 | tf_op jit(solution)/shard_map/student_logits/pallas_call | solution.py:993
  45.7 1.9 %collective-permute-start.20 = (f32[1,8,384]{2,1,0:T(8,128)S(1)}, f32[1,8,384]{2,1,0:T(8,128)S(1)}, u32[]{:S(2)}, u32[]{:S(2)}) collective-permute-start(f32[1,8,384]{2,1,0:T(8,128)S(1)} %assemble.1), channel_id=1, source_target_pairs={{0,28},{1,29},{2,30},{3,31},{4,24},{5,25},{6,26},{7,27},{8,20},{9,... | collective-permute-start | bytes 36872 | tf_op jit(solution)/shard_map/ppermute | solution.py:828
  48.4 1.2 %collective-permute-start.18 = (f32[1,8,384]{2,1,0:T(8,128)S(1)}, f32[1,8,384]{2,1,0:T(8,128)S(1)}, u32[]{:S(2)}, u32[]{:S(2)}) collective-permute-start(f32[1,8,384]{2,1,0:T(8,128)S(1)} %assemble.1), channel_id=1, source_target_pairs={{0,20},{1,21},{2,22},{3,23},{4,16},{5,17},{6,18},{7,19},{8,28},{9,... | collective-permute-start | bytes 36872 | tf_op jit(solution)/shard_map/ppermute | solution.py:828
  51.6 2.3 %collective-permute-start.24 = (f32[4,8,384]{2,1,0:T(8,128)S(1)}, f32[4,8,384]{2,1,0:T(8,128)S(1)}, u32[]{:S(2)}, u32[]{:S(2)}) collective-permute-start(f32[4,8,384]{2,1,0:T(8,128)S(1)} %stack.1), channel_id=1, source_target_pairs={{0,19},{1,18},{2,17},{3,16},{4,23},{5,22},{6,21},{7,20},{8,27},{9,... | collective-permute-start | bytes 147464 | tf_op jit(solution)/shard_map/ppermute | solution.py:828
  55.0 1.3 %collective-permute-done.24.recv3_ref_3_ = f32[4,8,384]{2,1,0:T(8,128)S(1)} collective-permute-done((f32[4,8,384]{2,1,0:T(8,128)S(1)}, f32[4,8,384]{2,1,0:T(8,128)S(1)}, u32[]{:S(2)}, u32[]{:S(2)}) %collective-permute-start.24) | collective-permute-done | bytes 49184 | tf_op jit(solution)/shard_map/ppermute | solution.py:828
  58.2 4.9 %back_second.1 = (f32[4096,256]{1,0:T(8,128)S(1)}, bf16[2,34,10,16,128]{4,3,2,1,0:T(8,128)(2,1)S(1)}, f32[8,128]{1,0:T(8,128)S(1)}, f32[24,128]{1,0:T(8,128)S(1)}, f32[8,128]{1,0:T(8,128)S(1)}) custom-call(f32[4096,256]{1,0:T(8,128)S(1)} %get-tuple-element.141.second_ref, f32[4096,256]{1,0:T(8,128)S(1)} %get-tuple-element.128.first_s.first_ref, ...), custom_call_target="tpu_custom_call" | custom-call | tf_op jit(solution)/shard_map/back_second/pallas_call | solution.py:1010
  63.1 1.4 %collective-permute-start.28 = (f32[8,128]{1,0:T(8,128)S(1)}, f32[8,128]{1,0:T(8,128)S(1)}, u32[]{:S(2)}, u32[]{:S(2)}) collective-permute-start(f32[8,128]{1,0:T(8,128)S(1)} %get-tuple-element.161), channel_id=1, source_target_pairs={{0,19},{1,18},{2,17},{3,16},{4,23},{5,22},{6,21},{7,20},{8,27},{9,... | collective-permute-start | bytes 12296 | tf_op jit(solution)/shard_map/ppermute | solution.py:828
  66.5 1.9 %second_weight.2 = f32[672,128]{1,0:T(8,128)S(1)} custom-call(bf16[2,34,10,16,128]{4,3,2,1,0:T(8,128)(2,1)S(1)} %get-tuple-element.162.frame_ref, bf16[2,34,10,16,128]{4,3,2,1,0:T(8,128)(2,1)S(1)} %get-tuple-element.163.dy_ref), custom_call_target="tpu_custom_call" | custom-call | flops 4000000000 | bytes 8000000 | tf_op jit(solution)/shard_map/second_weight/pallas_call | solution.py:1026
  68.5 1.6 %collective-permute-start.32 = (f32[8,128]{1,0:T(8,128)S(1)}, f32[8,128]{1,0:T(8,128)S(1)}, u32[]{:S(2)}, u32[]{:S(2)}) collective-permute-start(f32[8,128]{1,0:T(8,128)S(1)} %add_add_fusion), channel_id=1, source_target_pairs={{0,28},{1,29},{2,30},{3,31},{4,24},{5,25},{6,26},{7,27},{8,20},{9,... | collective-permute-start | bytes 12296 | tf_op jit(solution)/shard_map/ppermute | solution.py:828
  70.9 1.4 %collective-permute-start.30 = (f32[8,128]{1,0:T(8,128)S(1)}, f32[8,128]{1,0:T(8,128)S(1)}, u32[]{:S(2)}, u32[]{:S(2)}) collective-permute-start(f32[8,128]{1,0:T(8,128)S(1)} %add_add_fusion), channel_id=1, source_target_pairs={{0,20},{1,21},{2,22},{3,23},{4,16},{5,17},{6,18},{7,19},{8,28},{9,... | collective-permute-start | bytes 12296 | tf_op jit(solution)/shard_map/ppermute | solution.py:828
  72.9 1.9 %second_weight.3.keep2 = f32[672,128]{1,0:T(8,128)S(1)} custom-call(bf16[2,34,10,16,128]{4,3,2,1,0:T(8,128)(2,1)S(1)} %get-tuple-element.162.frame_ref, bf16[2,34,10,16,128]{4,3,2,1,0:T(8,128)(2,1)S(1)} %get-tuple-element.163.dy_ref), custom_call_target="tpu_custom_call" | custom-call | flops 4000000000 | bytes 8000000 | tf_op jit(solution)/shard_map/second_weight/pallas_call | solution.py:1026
  74.8 3.6 %back_weight.1 = (bf16[2,34,10,16,128]{4,3,2,1,0:T(8,128)(2,1)S(1)}, f32[704,128]{1,0:T(8,128)S(1)}, f32[704,128]{1,0:T(8,128)S(1)}) custom-call(f32[4096,256]{1,0:T(8,128)S(1)} %get-tuple-element.159.du_ref, f32[4096,256]{1,0:T(8,128)S(1)} %get-tuple-element.128.first_s.first_ref, bf16[34,10,16,128]{3,2,1,0:T(8,128)(2,1)S(1)} %get-tuple-element.160.low_ref, ...), custom_call_target="tpu_custom_call" | custom-call | flops 8000000000 | bytes 16000000 | tf_op jit(solution)/shard_map/back_weight/pallas_call | solution.py:1042
  81.5 1.6 %collective-permute-start.36 = (s16[352,128]{1,0:T(8,128)(2,1)S(1)}, s16[352,128]{1,0:T(8,128)(2,1)S(1)}, u32[]{:S(2)}, u32[]{:S(2)}) collective-permute-start(s16[352,128]{1,0:T(8,128)(2,1)S(1)} %get-tuple-element.193), channel_id=1, source_target_pairs={{0,2},{1,3},{2,0},{3,1},{4,6},{5,7},{6,4},{7,5},{8,10},{9,11},{10,... | collective-permute-start | bytes 270344 | tf_op jit(solution)/shard_map/ppermute | solution.py:823
  85.2 1.2 %back_stem.6 = (f32[128,128]{1,0:T(8,128)S(1)}, f32[80,128]{1,0:T(8,128)S(1)}) custom-call(bf16[2,34,10,16,128]{4,3,2,1,0:T(8,128)(2,1)S(1)} %get-tuple-element.174.frame_ref, f32[3,288,128]{2,1,0:T(8,128)S(1)} %get-tuple-element.175.moved_ref, f32[8,128]{1,0:T(8,128)S(1)} %get-tuple-element.176.dmix_ref, bf16[2,768,256]{2,1,0:T(8,128)(2,1)S(1)} %get-tuple-element.177.w_ref, ...), custom_call_target="tpu_custom_call" | custom-call | flops 2000000000 | bytes 4000000 | tf_op jit(solution)/shard_map/back_stem/pallas_call | solution.py:1057
  86.5 1.2 %back_stem.7.stem_ref = f32[27,128]{1,0:T(8,128)S(1)} custom-call(bf16[2,34,10,16,128]{4,3,2,1,0:T(8,128)(2,1)S(1)} %get-tuple-element.174.frame_ref, f32[3,288,128]{2,1,0:T(8,128)S(1)} %get-tuple-element.175.moved_ref, f32[8,128]{1,0:T(8,128)S(1)} %get-tuple-element.176.dmix_ref, bf16[2,768,256]{2,1,0:T(8,128)(2,1)S(1)} %get-tuple-element.177.w_ref, ...), custom_call_target="tpu_custom_call" | custom-call | flops 2000000000 | bytes 4000000 | tf_op jit(solution)/shard_map/back_stem/pallas_call | solution.py:1057
  88.7 1.7 %collective-permute-start.40 = (s16[384,128]{1,0:T(8,128)(2,1)S(1)}, s16[384,128]{1,0:T(8,128)(2,1)S(1)}, u32[]{:S(2)}, u32[]{:S(2)}) collective-permute-start(s16[384,128]{1,0:T(8,128)(2,1)S(1)} %combine.1.recv_refs_0_), channel_id=1, source_target_pairs={{0,12},{1,13},{2,14},{3,15},{4,8},{5,9},{6,10},{7,11},{8,4},{9,5},... | collective-permute-start | bytes 294920 | tf_op jit(solution)/shard_map/ppermute | solution.py:823
  91.1 2.1 %collective-permute-start.38 = (s16[384,128]{1,0:T(8,128)(2,1)S(1)}, s16[384,128]{1,0:T(8,128)(2,1)S(1)}, u32[]{:S(2)}, u32[]{:S(2)}) collective-permute-start(s16[384,128]{1,0:T(8,128)(2,1)S(1)} %combine.1.recv_refs_0_), channel_id=1, source_target_pairs={{0,4},{1,5},{2,6},{3,7},{4,0},{5,1},{6,2},{7,3},{8,12},{9,13},{10,... | collective-permute-start | bytes 294920 | tf_op jit(solution)/shard_map/ppermute | solution.py:823
  93.2 2.9 %collective-permute-done.40.recv_refs_3_ = s16[384,128]{1,0:T(8,128)(2,1)S(1)} collective-permute-done((s16[384,128]{1,0:T(8,128)(2,1)S(1)}, s16[384,128]{1,0:T(8,128)(2,1)S(1)}, u32[]{:S(2)}, u32[]{:S(2)}) %collective-permute-start.40) | collective-permute-done | bytes 98336 | tf_op jit(solution)/shard_map/ppermute | solution.py:823
  96.1 3.1 %collective-permute-done.39.recv_refs_2_ = s16[384,128]{1,0:T(8,128)(2,1)S(1)} collective-permute-done((s16[384,128]{1,0:T(8,128)(2,1)S(1)}, s16[384,128]{1,0:T(8,128)(2,1)S(1)}, u32[]{:S(2)}, u32[]{:S(2)}) %collective-permute-start.39) | collective-permute-done | bytes 98336 | tf_op jit(solution)/shard_map/ppermute | solution.py:823
  99.4 2.1 %collective-permute-start.43 = (s16[384,128]{1,0:T(8,128)(2,1)S(1)}, s16[384,128]{1,0:T(8,128)(2,1)S(1)}, u32[]{:S(2)}, u32[]{:S(2)}) collective-permute-start(s16[384,128]{1,0:T(8,128)(2,1)S(1)} %recode.1.codes_0_), channel_id=1, source_target_pairs={{0,3},{1,2},{2,1},{3,0},{4,7},{5,6},{6,5},{7,4},{8,11},{9,10},{10,... | collective-permute-start | bytes 294920 | tf_op jit(solution)/shard_map/ppermute | solution.py:823
  103.0 3.0 %collective-permute-done.43.codes_3_ = s16[384,128]{1,0:T(8,128)(2,1)S(1)} collective-permute-done((s16[384,128]{1,0:T(8,128)(2,1)S(1)}, s16[384,128]{1,0:T(8,128)(2,1)S(1)}, u32[]{:S(2)}, u32[]{:S(2)}) %collective-permute-start.43) | collective-permute-done | bytes 98336 | tf_op jit(solution)/shard_map/ppermute | solution.py:823
  108.1 4.0 %update.1 = (f32[4,96,864]{2,1,0:T(8,128)}, f32[4,96,864]{2,1,0:T(8,128)}, f32[4,96,864]{2,1,0:T(8,128)}, f32[4,96,864]{2,1,0:T(8,128)}, bf16[4,96,864]{2,1,0:T(...) custom-call(f32[2,672,128]{2,1,0:T(8,128)S(1)} %get-tuple-element.20, ...), custom_call_target="tpu_custom_call" | custom-call | tf_op jit(solution)/shard_map/update/pallas_call | solution.py:1108
  (130 shorter events, 29.3 us)
Async XLA Ops:
  9.0 4.9 %collective-permute-start.3 = (f32[8,128]{1,0:T(8,128)S(1)}, f32[8,128]{1,0:T(8,128)S(1)}, u32[]{:S(2)}, u32[]{:S(2)}) collective-permute-start(f32[8,128]{1,0:T(8,128)S(1)} %get-tuple-element.130), channel_id=1, source_target_pairs={{0,19},{1,18},{2,17},{3,16},{4,23},{5,22},{6,21},{7,20},{8,27},{9,... | collective-permute-start | bytes 12296 | tf_op jit(solution)/shard_map/ppermute | solution.py:828
  16.3 5.6 %collective-permute-start.7 = (f32[8,128]{1,0:T(8,128)S(1)}, f32[8,128]{1,0:T(8,128)S(1)}, u32[]{:S(2)}, u32[]{:S(2)}) collective-permute-start(f32[8,128]{1,0:T(8,128)S(1)} %add_add_fusion.2), channel_id=1, source_target_pairs={{0,28},{1,29},{2,30},{3,31},{4,24},{5,25},{6,26},{7,27},{8,20},{9,... | collective-permute-start | bytes 12296 | tf_op jit(solution)/shard_map/ppermute | solution.py:828
  19.7 4.0 %collective-permute-start.6 = (f32[8,128]{1,0:T(8,128)S(1)}, f32[8,128]{1,0:T(8,128)S(1)}, u32[]{:S(2)}, u32[]{:S(2)}) collective-permute-start(f32[8,128]{1,0:T(8,128)S(1)} %add_add_fusion.2), channel_id=1, source_target_pairs={{0,24},{1,25},{2,26},{3,27},{4,28},{5,29},{6,30},{7,31},{8,16},{9,... | collective-permute-start | bytes 12296 | tf_op jit(solution)/shard_map/ppermute | solution.py:828
  19.7 4.0 %collective-permute-start.5 = (f32[8,128]{1,0:T(8,128)S(1)}, f32[8,128]{1,0:T(8,128)S(1)}, u32[]{:S(2)}, u32[]{:S(2)}) collective-permute-start(f32[8,128]{1,0:T(8,128)S(1)} %add_add_fusion.2), channel_id=1, source_target_pairs={{0,20},{1,21},{2,22},{3,23},{4,16},{5,17},{6,18},{7,19},{8,28},{9,... | collective-permute-start | bytes 12296 | tf_op jit(solution)/shard_map/ppermute | solution.py:828
  20.3 3.3 %collective-permute-start.4 = (f32[8,128]{1,0:T(8,128)S(1)}, f32[8,128]{1,0:T(8,128)S(1)}, u32[]{:S(2)}, u32[]{:S(2)}) collective-permute-start(f32[8,128]{1,0:T(8,128)S(1)} %add_add_fusion.2), channel_id=1, source_target_pairs={{0,16},{1,17},{2,18},{3,19},{4,20},{5,21},{6,22},{7,23},{8,24},{9,... | collective-permute-start | bytes 12296 | tf_op jit(solution)/shard_map/ppermute | solution.py:828
  32.0 4.0 %collective-permute-start.11 = (f32[8,128]{1,0:T(8,128)S(1)}, f32[8,128]{1,0:T(8,128)S(1)}, u32[]{:S(2)}, u32[]{:S(2)}) collective-permute-start(f32[8,128]{1,0:T(8,128)S(1)} %get-tuple-element.143), channel_id=1, source_target_pairs={{0,19},{1,18},{2,17},{3,16},{4,23},{5,22},{6,21},{7,20},{8,27},{9,... | collective-permute-start | bytes 12296 | tf_op jit(solution)/shard_map/ppermute | solution.py:828
  36.8 4.9 %collective-permute-start.15 = (f32[8,128]{1,0:T(8,128)S(1)}, f32[8,128]{1,0:T(8,128)S(1)}, u32[]{:S(2)}, u32[]{:S(2)}) collective-permute-start(f32[8,128]{1,0:T(8,128)S(1)} %add_add_fusion.1), channel_id=1, source_target_pairs={{0,28},{1,29},{2,30},{3,31},{4,24},{5,25},{6,26},{7,27},{8,20},{9,... | collective-permute-start | bytes 12296 | tf_op jit(solution)/shard_map/ppermute | solution.py:828
  38.6 3.9 %collective-permute-start.14 = (f32[8,128]{1,0:T(8,128)S(1)}, f32[8,128]{1,0:T(8,128)S(1)}, u32[]{:S(2)}, u32[]{:S(2)}) collective-permute-start(f32[8,128]{1,0:T(8,128)S(1)} %add_add_fusion.1), channel_id=1, source_target_pairs={{0,24},{1,25},{2,26},{3,27},{4,28},{5,29},{6,30},{7,31},{8,16},{9,... | collective-permute-start | bytes 12296 | tf_op jit(solution)/shard_map/ppermute | solution.py:828
  38.7 3.8 %collective-permute-start.13 = (f32[8,128]{1,0:T(8,128)S(1)}, f32[8,128]{1,0:T(8,128)S(1)}, u32[]{:S(2)}, u32[]{:S(2)}) collective-permute-start(f32[8,128]{1,0:T(8,128)S(1)} %add_add_fusion.1), channel_id=1, source_target_pairs={{0,20},{1,21},{2,22},{3,23},{4,16},{5,17},{6,18},{7,19},{8,28},{9,... | collective-permute-start | bytes 12296 | tf_op jit(solution)/shard_map/ppermute | solution.py:828
  45.7 4.9 %collective-permute-start.20 = (f32[1,8,384]{2,1,0:T(8,128)S(1)}, f32[1,8,384]{2,1,0:T(8,128)S(1)}, u32[]{:S(2)}, u32[]{:S(2)}) collective-permute-start(f32[1,8,384]{2,1,0:T(8,128)S(1)} %assemble.1), channel_id=1, source_target_pairs={{0,28},{1,29},{2,30},{3,31},{4,24},{5,25},{6,26},{7,27},{8,20},{9,... | collective-permute-start | bytes 36872 | tf_op jit(solution)/shard_map/ppermute | solution.py:828
  47.5 4.1 %collective-permute-start.19 = (f32[1,8,384]{2,1,0:T(8,128)S(1)}, f32[1,8,384]{2,1,0:T(8,128)S(1)}, u32[]{:S(2)}, u32[]{:S(2)}) collective-permute-start(f32[1,8,384]{2,1,0:T(8,128)S(1)} %assemble.1), channel_id=1, source_target_pairs={{0,24},{1,25},{2,26},{3,27},{4,28},{5,29},{6,30},{7,31},{8,16},{9,... | collective-permute-start | bytes 36872 | tf_op jit(solution)/shard_map/ppermute | solution.py:828
  48.4 3.3 %collective-permute-start.18 = (f32[1,8,384]{2,1,0:T(8,128)S(1)}, f32[1,8,384]{2,1,0:T(8,128)S(1)}, u32[]{:S(2)}, u32[]{:S(2)}) collective-permute-start(f32[1,8,384]{2,1,0:T(8,128)S(1)} %assemble.1), channel_id=1, source_target_pairs={{0,20},{1,21},{2,22},{3,23},{4,16},{5,17},{6,18},{7,19},{8,28},{9,... | collective-permute-start | bytes 36872 | tf_op jit(solution)/shard_map/ppermute | solution.py:828
  51.6 4.7 %collective-permute-start.24 = (f32[4,8,384]{2,1,0:T(8,128)S(1)}, f32[4,8,384]{2,1,0:T(8,128)S(1)}, u32[]{:S(2)}, u32[]{:S(2)}) collective-permute-start(f32[4,8,384]{2,1,0:T(8,128)S(1)} %stack.1), channel_id=1, source_target_pairs={{0,19},{1,18},{2,17},{3,16},{4,23},{5,22},{6,21},{7,20},{8,27},{9,... | collective-permute-start | bytes 147464 | tf_op jit(solution)/shard_map/ppermute | solution.py:828
  54.0 3.5 %collective-permute-start.23 = (f32[4,8,384]{2,1,0:T(8,128)S(1)}, f32[4,8,384]{2,1,0:T(8,128)S(1)}, u32[]{:S(2)}, u32[]{:S(2)}) collective-permute-start(f32[4,8,384]{2,1,0:T(8,128)S(1)} %stack.1), channel_id=1, source_target_pairs={{0,18},{1,19},{2,16},{3,17},{4,22},{5,23},{6,20},{7,21},{8,26},{9,... | collective-permute-start | bytes 147464 | tf_op jit(solution)/shard_map/ppermute | solution.py:828
  54.4 3.8 %collective-permute-start.22 = (f32[4,8,384]{2,1,0:T(8,128)S(1)}, f32[4,8,384]{2,1,0:T(8,128)S(1)}, u32[]{:S(2)}, u32[]{:S(2)}) collective-permute-start(f32[4,8,384]{2,1,0:T(8,128)S(1)} %stack.1), channel_id=1, source_target_pairs={{0,17},{1,16},{2,19},{3,18},{4,21},{5,20},{6,23},{7,22},{8,25},{9,... | collective-permute-start | bytes 147464 | tf_op jit(solution)/shard_map/ppermute | solution.py:828
  54.7 3.5 %collective-permute-start.21 = (f32[4,8,384]{2,1,0:T(8,128)S(1)}, f32[4,8,384]{2,1,0:T(8,128)S(1)}, u32[]{:S(2)}, u32[]{:S(2)}) collective-permute-start(f32[4,8,384]{2,1,0:T(8,128)S(1)} %stack.1), channel_id=1, source_target_pairs={{0,16},{1,17},{2,18},{3,19},{4,20},{5,21},{6,22},{7,23},{8,24},{9,... | collective-permute-start | bytes 147464 | tf_op jit(solution)/shard_map/ppermute | solution.py:828
  63.1 5.3 %collective-permute-start.28 = (f32[8,128]{1,0:T(8,128)S(1)}, f32[8,128]{1,0:T(8,128)S(1)}, u32[]{:S(2)}, u32[]{:S(2)}) collective-permute-start(f32[8,128]{1,0:T(8,128)S(1)} %get-tuple-element.161), channel_id=1, source_target_pairs={{0,19},{1,18},{2,17},{3,16},{4,23},{5,22},{6,21},{7,20},{8,27},{9,... | collective-permute-start | bytes 12296 | tf_op jit(solution)/shard_map/ppermute | solution.py:828
  64.5 4.0 %collective-permute-start.27 = (f32[8,128]{1,0:T(8,128)S(1)}, f32[8,128]{1,0:T(8,128)S(1)}, u32[]{:S(2)}, u32[]{:S(2)}) collective-permute-start(f32[8,128]{1,0:T(8,128)S(1)} %get-tuple-element.161), channel_id=1, source_target_pairs={{0,18},{1,19},{2,16},{3,17},{4,22},{5,23},{6,20},{7,21},{8,26},{9,... | collective-permute-start | bytes 12296 | tf_op jit(solution)/shard_map/ppermute | solution.py:828
  65.4 3.1 %collective-permute-start.26 = (f32[8,128]{1,0:T(8,128)S(1)}, f32[8,128]{1,0:T(8,128)S(1)}, u32[]{:S(2)}, u32[]{:S(2)}) collective-permute-start(f32[8,128]{1,0:T(8,128)S(1)} %get-tuple-element.161), channel_id=1, source_target_pairs={{0,17},{1,16},{2,19},{3,18},{4,21},{5,20},{6,23},{7,22},{8,25},{9,... | collective-permute-start | bytes 12296 | tf_op jit(solution)/shard_map/ppermute | solution.py:828
  68.5 6.3 %collective-permute-start.32 = (f32[8,128]{1,0:T(8,128)S(1)}, f32[8,128]{1,0:T(8,128)S(1)}, u32[]{:S(2)}, u32[]{:S(2)}) collective-permute-start(f32[8,128]{1,0:T(8,128)S(1)} %add_add_fusion), channel_id=1, source_target_pairs={{0,28},{1,29},{2,30},{3,31},{4,24},{5,25},{6,26},{7,27},{8,20},{9,... | collective-permute-start | bytes 12296 | tf_op jit(solution)/shard_map/ppermute | solution.py:828
  70.0 4.7 %collective-permute-start.31 = (f32[8,128]{1,0:T(8,128)S(1)}, f32[8,128]{1,0:T(8,128)S(1)}, u32[]{:S(2)}, u32[]{:S(2)}) collective-permute-start(f32[8,128]{1,0:T(8,128)S(1)} %add_add_fusion), channel_id=1, source_target_pairs={{0,24},{1,25},{2,26},{3,27},{4,28},{5,29},{6,30},{7,31},{8,16},{9,... | collective-permute-start | bytes 12296 | tf_op jit(solution)/shard_map/ppermute | solution.py:828
  70.9 3.9 %collective-permute-start.30 = (f32[8,128]{1,0:T(8,128)S(1)}, f32[8,128]{1,0:T(8,128)S(1)}, u32[]{:S(2)}, u32[]{:S(2)}) collective-permute-start(f32[8,128]{1,0:T(8,128)S(1)} %add_add_fusion), channel_id=1, source_target_pairs={{0,20},{1,21},{2,22},{3,23},{4,16},{5,17},{6,18},{7,19},{8,28},{9,... | collective-permute-start | bytes 12296 | tf_op jit(solution)/shard_map/ppermute | solution.py:828
  80.5 7.2 %collective-permute-start.35 = (s16[352,128]{1,0:T(8,128)(2,1)S(1)}, s16[352,128]{1,0:T(8,128)(2,1)S(1)}, u32[]{:S(2)}, u32[]{:S(2)}) collective-permute-start(s16[352,128]{1,0:T(8,128)(2,1)S(1)} %get-tuple-element.192), channel_id=1, source_target_pairs={{0,1},{1,0},{2,3},{3,2},{4,5},{5,4},{6,7},{7,6},{8,9},{9,8},{10,11... | collective-permute-start | bytes 270344 | tf_op jit(solution)/shard_map/ppermute | solution.py:823
  81.5 6.2 %collective-permute-start.36 = (s16[352,128]{1,0:T(8,128)(2,1)S(1)}, s16[352,128]{1,0:T(8,128)(2,1)S(1)}, u32[]{:S(2)}, u32[]{:S(2)}) collective-permute-start(s16[352,128]{1,0:T(8,128)(2,1)S(1)} %get-tuple-element.193), channel_id=1, source_target_pairs={{0,2},{1,3},{2,0},{3,1},{4,6},{5,7},{6,4},{7,5},{8,10},{9,11},{10,... | collective-permute-start | bytes 270344 | tf_op jit(solution)/shard_map/ppermute | solution.py:823
  83.2 5.4 %collective-permute-start.37 = (s16[352,128]{1,0:T(8,128)(2,1)S(1)}, s16[352,128]{1,0:T(8,128)(2,1)S(1)}, u32[]{:S(2)}, u32[]{:S(2)}) collective-permute-start(s16[352,128]{1,0:T(8,128)(2,1)S(1)} %get-tuple-element.194), channel_id=1, source_target_pairs={{0,3},{1,2},{2,1},{3,0},{4,7},{5,6},{6,5},{7,4},{8,11},{9,10},{10,... | collective-permute-start | bytes 270344 | tf_op jit(solution)/shard_map/ppermute | solution.py:823
  88.7 7.4 %collective-permute-start.40 = (s16[384,128]{1,0:T(8,128)(2,1)S(1)}, s16[384,128]{1,0:T(8,128)(2,1)S(1)}, u32[]{:S(2)}, u32[]{:S(2)}) collective-permute-start(s16[384,128]{1,0:T(8,128)(2,1)S(1)} %combine.1.recv_refs_0_), channel_id=1, source_target_pairs={{0,12},{1,13},{2,14},{3,15},{4,8},{5,9},{6,10},{7,11},{8,4},{9,5},... | collective-permute-start | bytes 294920 | tf_op jit(solution)/shard_map/ppermute | solution.py:823
  90.5 8.8 %collective-permute-start.39 = (s16[384,128]{1,0:T(8,128)(2,1)S(1)}, s16[384,128]{1,0:T(8,128)(2,1)S(1)}, u32[]{:S(2)}, u32[]{:S(2)}) collective-permute-start(s16[384,128]{1,0:T(8,128)(2,1)S(1)} %combine.1.recv_refs_0_), channel_id=1, source_target_pairs={{0,8},{1,9},{2,10},{3,11},{4,12},{5,13},{6,14},{7,15},{8,0},{9,1},... | collective-permute-start | bytes 294920 | tf_op jit(solution)/shard_map/ppermute | solution.py:823
  91.1 8.2 %collective-permute-start.38 = (s16[384,128]{1,0:T(8,128)(2,1)S(1)}, s16[384,128]{1,0:T(8,128)(2,1)S(1)}, u32[]{:S(2)}, u32[]{:S(2)}) collective-permute-start(s16[384,128]{1,0:T(8,128)(2,1)S(1)} %combine.1.recv_refs_0_), channel_id=1, source_target_pairs={{0,4},{1,5},{2,6},{3,7},{4,0},{5,1},{6,2},{7,3},{8,12},{9,13},{10,... | collective-permute-start | bytes 294920 | tf_op jit(solution)/shard_map/ppermute | solution.py:823
  99.4 6.5 %collective-permute-start.43 = (s16[384,128]{1,0:T(8,128)(2,1)S(1)}, s16[384,128]{1,0:T(8,128)(2,1)S(1)}, u32[]{:S(2)}, u32[]{:S(2)}) collective-permute-start(s16[384,128]{1,0:T(8,128)(2,1)S(1)} %recode.1.codes_0_), channel_id=1, source_target_pairs={{0,3},{1,2},{2,1},{3,0},{4,7},{5,6},{6,5},{7,4},{8,11},{9,10},{10,... | collective-permute-start | bytes 294920 | tf_op jit(solution)/shard_map/ppermute | solution.py:823
  101.5 5.1 %collective-permute-start.42 = (s16[384,128]{1,0:T(8,128)(2,1)S(1)}, s16[384,128]{1,0:T(8,128)(2,1)S(1)}, u32[]{:S(2)}, u32[]{:S(2)}) collective-permute-start(s16[384,128]{1,0:T(8,128)(2,1)S(1)} %recode.1.codes_0_), channel_id=1, source_target_pairs={{0,2},{1,3},{2,0},{3,1},{4,6},{5,7},{6,4},{7,5},{8,10},{9,11},{10,... | collective-permute-start | bytes 294920 | tf_op jit(solution)/shard_map/ppermute | solution.py:823
  102.0 4.6 %collective-permute-start.41 = (s16[384,128]{1,0:T(8,128)(2,1)S(1)}, s16[384,128]{1,0:T(8,128)(2,1)S(1)}, u32[]{:S(2)}, u32[]{:S(2)}) collective-permute-start(s16[384,128]{1,0:T(8,128)(2,1)S(1)} %recode.1.codes_0_), channel_id=1, source_target_pairs={{0,1},{1,0},{2,3},{3,2},{4,5},{5,4},{6,7},{7,6},{8,9},{9,8},{10,11... | collective-permute-start | bytes 294920 | tf_op jit(solution)/shard_map/ppermute | solution.py:823
  103.0 4.2 %collective-permute-start.44 = (s16[384,128]{1,0:T(8,128)(2,1)S(1)}, s16[384,128]{1,0:T(8,128)(2,1)S(1)}, u32[]{:S(2)}, u32[]{:S(2)}) collective-permute-start(s16[384,128]{1,0:T(8,128)(2,1)S(1)} %recode.1.codes_0_), channel_id=1, source_target_pairs={{0,16},{16,0},{1,17},{17,1},{2,18},{18,2},{3,19},{19,3},{4,20},{20... | collective-permute-start | bytes 294920 | tf_op jit(solution)/shard_map/ppermute | solution.py:884
  (36 other events, 329.0 us)
